TPU v7x, 32 devices: a whole 2x2x4 slice. The times are simulated.
32 devices in a mesh: dp: 16 (over z, y, core), tensor: 2 (over x).
Axes of the slice: x: 2, y: 2, z: 4, core: 2. Of those that a mesh axis runs over, the one named last changes fastest.
Arguments:
- tokens: bfloat16 [8192, 1536], P(('dp', 'tensor')), may hold values from -6 to 6
- cotangent: bfloat16 [8192, 1536], P(('dp', 'tensor')), may hold values from -6 to 6
- segments: int32 [8192], P('dp'), may hold values from 0 to 4, as said below
- small_params: float32 [5120], replicated, as said below
- small_first: float32 [5120], replicated
- small_second: float32 [5120], replicated, as said below
- qkv_weight: float32 [1536, 2048], P('dp', 'tensor'), may hold values from -0.15625 to 0.15625
- qkv_first: float32 [1536, 2048], P('dp', 'tensor')
- qkv_second: float32 [1536, 2048], P('dp', 'tensor'), as said below
- out_weight: float32 [1536, 1536], P('tensor', 'dp')
- out_first: float32 [1536, 1536], P('tensor', 'dp')
- out_second: float32 [1536, 1536], P('tensor', 'dp'), as said below
- gateup_weight: float32 [2, 1536, 8960], P(None, 'dp', 'tensor'), may hold values from -0.15625 to 0.15625
- gateup_first: float32 [2, 1536, 8960], P(None, 'dp', 'tensor')
- gateup_second: float32 [2, 1536, 8960], P(None, 'dp', 'tensor'), as said below
- down_weight: float32 [8960, 1536], P('tensor', 'dp')
- down_first: float32 [8960, 1536], P('tensor', 'dp')
- down_second: float32 [8960, 1536], P('tensor', 'dp'), as said below
Outputs:
- block_out: bfloat16 [8192, 1536], P(('dp', 'tensor'))
- input_grad: float32 [8192, 1536], P(('dp', 'tensor'))
- grad_norm: float32 [], replicated
- new_small: float32 [5120], replicated
- new_small_first: float32 [5120], replicated
- new_small_second: float32 [5120], replicated
- new_qkv: float32 [1536, 2048], P('dp', 'tensor')
- new_qkv_first: float32 [1536, 2048], P('dp', 'tensor')
- new_qkv_second: float32 [1536, 2048], P('dp', 'tensor')
- new_out: float32 [1536, 1536], P('tensor', 'dp')
- new_out_first: float32 [1536, 1536], P('tensor', 'dp')
- new_out_second: float32 [1536, 1536], P('tensor', 'dp')
- new_gateup: float32 [2, 1536, 8960], P(None, 'dp', 'tensor')
- new_gateup_first: float32 [2, 1536, 8960], P(None, 'dp', 'tensor')
- new_gateup_second: float32 [2, 1536, 8960], P(None, 'dp', 'tensor')
- new_down: float32 [8960, 1536], P('tensor', 'dp')
- new_down_first: float32 [8960, 1536], P('tensor', 'dp')
- new_down_second: float32 [8960, 1536], P('tensor', 'dp')
Inputs may be any that keep to these rules, and one draw needn't show every extreme that they name: `segments`: within each sequence of 1024 tokens the numbers start at 0, never fall and rise by one at each document's start; every sequence holds five documents, and the one that holds the sequence's middle token starts in its first quarter and ends in its last. `small_params`: the first 3072 entries are positive. `small_second`: positive. `qkv_second`: positive. `out_second`: positive. `gateup_second`: positive. `down_second`: positive.
All inputs are finite; a program needn't handle non-finite values.
Results may differ from a plain program's by a relative error of at most 0.015.
Values may be sent and summed in bfloat16 or wider, within the bound.
No kernel may reach another device: no remote copies, remote signals or barrier semaphores. Data moves between devices by JAX's collectives and lax.ppermute only.
A program may use at most 384 MiB of HBM per device.

v0:
```python
import math

import jax
import jax.numpy as jnp
from jax import lax
from jax.sharding import PartitionSpec as P

D = 1536
FF = 8960
QUERY_HEADS = 12
KEY_VALUE_HEADS = 2
HEAD_WIDTH = 128
STEP = 10


EPSILON = 1e-06
ROPE_BASE = 1000000.0
BETA_ONE = 0.9
BETA_TWO = 0.999
ADAM_EPS = 1e-08
WEIGHT_DECAY = 0.1
MAX_NORM = 1.0
NEGATIVE = -1e30


def passed_along(value, axis, steps):
    count = lax.axis_size(axis)
    leading, last = (max(0, -steps), min(count, count - steps))
    return lax.ppermute(value, axis, [(source, source + steps) for source in range(leading, last)])


def contract_rows(left_side, right_side):
    return lax.dot_general(
        left_side, right_side, (((0,), (0,)), ((), ())), preferred_element_type=jnp.float32
    )


def contract_cols(left_side, right_side):
    return lax.dot_general(
        left_side, right_side, (((1,), (1,)), ((), ())), preferred_element_type=jnp.float32
    )


def rms_scale(inputs):
    return lax.rsqrt(jnp.mean(inputs * inputs, axis=-1, keepdims=True) + EPSILON)


def norm_backward(inputs, inv_rms, gain_vec, upstream):
    normed = inputs * inv_rms
    normed_grad = upstream * gain_vec
    input_part = inv_rms * (
        normed_grad - normed * jnp.mean(normed_grad * normed, axis=-1, keepdims=True)
    )
    return (input_part, jnp.sum(upstream * normed, axis=0))


def rotate(features, cos_part, sin_part):
    half = features.shape[-1] // 2
    front_half = features[..., :half]
    back_half = features[..., half:]
    return jnp.concatenate(
        [
            front_half * cos_part - back_half * sin_part,
            back_half * cos_part + front_half * sin_part,
        ],
        axis=-1,
    )


def unrotate(grad_parts, cos_part, sin_part):
    half = grad_parts.shape[-1] // 2
    front_half = grad_parts[..., :half]
    back_half = grad_parts[..., half:]
    return jnp.concatenate(
        [
            front_half * cos_part + back_half * sin_part,
            back_half * cos_part - front_half * sin_part,
        ],
        axis=-1,
    )


def adam_update(weight, moment_one, moment_two, gradient, step_rate, decay_rate):
    first_new = BETA_ONE * moment_one + (1.0 - BETA_ONE) * gradient
    second_new = BETA_TWO * moment_two + (1.0 - BETA_TWO) * gradient * gradient
    corrected = first_new / (1.0 - BETA_ONE**STEP)
    spread = jnp.sqrt(second_new / (1.0 - BETA_TWO**STEP)) + ADAM_EPS
    return (
        weight * (1.0 - step_rate * decay_rate) - step_rate * corrected / spread,
        first_new,
        second_new,
    )


def gather_rows(row_block):
    return lax.all_gather(row_block, "tensor", axis=0, tiled=True)


def sum_rows(term, row_count):
    return lax.psum_scatter(
        term(jnp.int32(0), row_count * lax.axis_size("tensor")),
        "tensor",
        scatter_dimension=0,
        tiled=True,
    )


def masked_scores(query_rows, keys_all, allowed, score_scale):
    scores = (
        jnp.einsum("qgih,kgh->giqk", query_rows, keys_all, preferred_element_type=jnp.float32)
        * score_scale
    )
    return jnp.where(allowed[None, None], scores, NEGATIVE)


def body(
    tokens,
    cotangent,
    segments,
    small_params,
    small_first,
    small_second,
    qkv_weight,
    qkv_first,
    qkv_second,
    out_weight,
    out_first,
    out_second,
    gateup_weight,
    gateup_first,
    gateup_second,
    down_weight,
    down_first,
    down_second,
):
    tensor_list = lax.axis_size("tensor")
    tensor_place = lax.axis_index("tensor")
    odd_device = lax.axis_index("dp") % 2 == 1
    own_rows = tokens.shape[0]
    local_rows = own_rows * tensor_list
    head_group_count = KEY_VALUE_HEADS // tensor_list
    queries_each_group = QUERY_HEADS // KEY_VALUE_HEADS
    local_qkv = qkv_weight.shape[1]
    score_scale = 1.0 / math.sqrt(HEAD_WIDTH)
    gain_one = small_params[:D]
    gain_two = small_params[D : 2 * D]
    bias_local = lax.dynamic_slice_in_dim(
        small_params[2 * D :], tensor_place * local_qkv, local_qkv
    )
    partner_ids = passed_along(segments, "dp", 1)
    joined = jnp.concatenate([partner_ids, segments])
    places = jnp.arange(2 * local_rows, dtype=jnp.int32)
    earlier = jnp.concatenate([joined[:1], joined[:-1]])
    begins = (
        (places == 0) | (joined != earlier) | (places == local_rows) & jnp.logical_not(odd_device)
    )
    starts = lax.cummax(jnp.where(begins, places, 0), axis=0)
    own_places = places[local_rows:]
    positions = (own_places - starts[local_rows:]).astype(jnp.float32)
    frequency = 1.0 / ROPE_BASE ** (jnp.arange(0, HEAD_WIDTH, 2, dtype=jnp.float32) / HEAD_WIDTH)
    angles = positions[:, None] * frequency[None, :]
    cos_part = jnp.cos(angles)[:, None, :]
    sin_part = jnp.sin(angles)[:, None, :]
    allowed = (
        (joined[None, :] == segments[:, None])
        & (places[None, :] <= own_places[:, None])
        & ((places[None, :] >= local_rows) | odd_device)
    )
    qkv_full, out_full = (
        lax.all_gather(qkv_weight.astype(jnp.bfloat16), "dp", axis=0, tiled=True),
        lax.all_gather(out_weight.astype(jnp.bfloat16), "dp", axis=1, tiled=True),
    )
    rows_in = tokens.astype(jnp.float32)
    scale_one = rms_scale(rows_in)
    gathered_one = gather_rows((rows_in * scale_one * gain_one).astype(jnp.bfloat16))
    projected_output = (
        jnp.dot(gathered_one, qkv_full, preferred_element_type=jnp.float32) + bias_local
    )
    reshaped_input = projected_output.reshape(
        local_rows, head_group_count, queries_each_group + 2, HEAD_WIDTH
    )
    query_rows = rotate(
        reshaped_input[:, :, :queries_each_group], cos_part[:, :, None, :], sin_part[:, :, None, :]
    ).astype(jnp.bfloat16)
    own_keys = rotate(reshaped_input[:, :, queries_each_group], cos_part, sin_part).astype(
        jnp.bfloat16
    )
    own_values = reshaped_input[:, :, queries_each_group + 1].astype(jnp.bfloat16)
    partner_pair = passed_along(jnp.stack([own_keys, own_values], axis=2), "dp", 1)
    keys_all = jnp.concatenate([partner_pair[:, :, 0], own_keys], axis=0)
    values_all = jnp.concatenate([partner_pair[:, :, 1], own_values], axis=0)
    scores = masked_scores(query_rows, keys_all, allowed, score_scale)
    row_max = jnp.max(scores, axis=-1, keepdims=True)
    weights_exp = jnp.exp(scores - row_max)
    row_sum = jnp.sum(weights_exp, axis=-1, keepdims=True)
    log_total = row_max + jnp.log(row_sum)
    prob_low = (weights_exp / row_sum).astype(jnp.bfloat16)
    attention_blended = jnp.einsum(
        "giqk,kgh->qgih", prob_low, values_all, preferred_element_type=jnp.float32
    )
    attn_rows = attention_blended.reshape(
        local_rows, queries_each_group * head_group_count * HEAD_WIDTH
    ).astype(jnp.bfloat16)

    def attn_term(offset, length):
        return jnp.dot(attn_rows, out_full, preferred_element_type=jnp.float32)

    residual = rows_in + sum_rows(attn_term, own_rows)
    gateup_full, down_full = (
        lax.all_gather(gateup_weight.astype(jnp.bfloat16), "dp", axis=1, tiled=True),
        lax.all_gather(down_weight.astype(jnp.bfloat16), "dp", axis=1, tiled=True),
    )
    scale_two = rms_scale(residual)
    gathered_two = gather_rows((residual * scale_two * gain_two).astype(jnp.bfloat16))
    gate_pre = jnp.dot(gathered_two, gateup_full[0], preferred_element_type=jnp.float32)
    up_proj = jnp.dot(gathered_two, gateup_full[1], preferred_element_type=jnp.float32)
    gate_sigmoid = jax.nn.sigmoid(gate_pre)
    gate_silu = gate_pre * gate_sigmoid
    hidden = (gate_silu * up_proj).astype(jnp.bfloat16)

    def mlp_term(offset, length):
        return jnp.dot(hidden, down_full, preferred_element_type=jnp.float32)

    block_out = (residual + sum_rows(mlp_term, own_rows)).astype(jnp.bfloat16)
    gateup_full, down_full = (
        lax.all_gather(gateup_weight.astype(jnp.bfloat16), "dp", axis=1, tiled=True),
        lax.all_gather(down_weight.astype(jnp.bfloat16), "dp", axis=1, tiled=True),
    )
    cot_full = gather_rows(cotangent)
    hidden_grad = contract_cols(cot_full, down_full)
    gate_grad = (
        hidden_grad * up_proj * gate_sigmoid * (1.0 + gate_pre * (1.0 - gate_sigmoid))
    ).astype(jnp.bfloat16)
    up_grad = (hidden_grad * gate_silu).astype(jnp.bfloat16)
    down_grad = contract_rows(hidden, cot_full)
    gateup_grad = jnp.stack(
        [contract_rows(gathered_two, gate_grad), contract_rows(gathered_two, up_grad)]
    )
    mlp_owned = (
        lax.psum_scatter(gateup_grad, "dp", scatter_dimension=1, tiled=True),
        lax.psum_scatter(down_grad, "dp", scatter_dimension=1, tiled=True),
    )

    def normed_two_term(offset, length):
        return contract_cols(gate_grad, gateup_full[0]) + contract_cols(up_grad, gateup_full[1])

    norm_two_in, gain_two_grad = norm_backward(
        residual, scale_two, gain_two, sum_rows(normed_two_term, own_rows)
    )
    residual_grad = cotangent.astype(jnp.float32) + norm_two_in
    qkv_full, out_full = (
        lax.all_gather(qkv_weight.astype(jnp.bfloat16), "dp", axis=0, tiled=True),
        lax.all_gather(out_weight.astype(jnp.bfloat16), "dp", axis=1, tiled=True),
    )
    branch_full = gather_rows(residual_grad.astype(jnp.bfloat16))
    mixed_grad = contract_cols(branch_full, out_full).astype(jnp.bfloat16)
    mixed_grad = mixed_grad.reshape(local_rows, head_group_count, queries_each_group, HEAD_WIDTH)
    scores = masked_scores(query_rows, keys_all, allowed, score_scale)
    prob_full = jnp.exp(scores - log_total)
    prob_low = prob_full.astype(jnp.bfloat16)
    values_grad = jnp.einsum(
        "giqk,qgih->kgh", prob_low, mixed_grad, preferred_element_type=jnp.float32
    )
    prob_grad = jnp.einsum(
        "qgih,kgh->giqk", mixed_grad, values_all, preferred_element_type=jnp.float32
    )
    row_inner = jnp.sum(prob_full * prob_grad, axis=-1, keepdims=True)
    score_grad = (prob_full * (prob_grad - row_inner)).astype(jnp.bfloat16)
    query_grad = (
        jnp.einsum("giqk,kgh->qgih", score_grad, keys_all, preferred_element_type=jnp.float32)
        * score_scale
    )
    key_grad = (
        jnp.einsum("giqk,qgih->kgh", score_grad, query_rows, preferred_element_type=jnp.float32)
        * score_scale
    )
    back_pair = passed_along(
        jnp.stack([key_grad[:local_rows], values_grad[:local_rows]], axis=2), "dp", -1
    )
    back_pair = jnp.where(odd_device, 0.0, back_pair)
    key_own = key_grad[local_rows:] + back_pair[:, :, 0]
    value_own = values_grad[local_rows:] + back_pair[:, :, 1]
    projected_grad = (
        jnp.concatenate(
            [
                unrotate(query_grad, cos_part[:, :, None, :], sin_part[:, :, None, :]),
                unrotate(key_own, cos_part, sin_part)[:, :, None],
                value_own[:, :, None],
            ],
            axis=2,
        )
        .reshape(local_rows, local_qkv)
        .astype(jnp.bfloat16)
    )
    bias_grad = jnp.sum(projected_grad, axis=0, dtype=jnp.float32)

    def normed_one_term(offset, length):
        return contract_cols(projected_grad, qkv_full)

    norm_one_in, gain_one_grad = norm_backward(
        rows_in, scale_one, gain_one, sum_rows(normed_one_term, own_rows)
    )
    input_grad = residual_grad + norm_one_in
    qkv_grad = contract_rows(gathered_one, projected_grad)
    out_grad = contract_rows(attn_rows, branch_full)
    qkv_owned, out_owned = (
        lax.psum_scatter(qkv_grad, "dp", scatter_dimension=0, tiled=True),
        lax.psum_scatter(out_grad, "dp", scatter_dimension=1, tiled=True),
    )
    gateup_owned, down_owned = mlp_owned
    bias_slots = lax.dynamic_update_slice_in_dim(
        jnp.zeros((small_params.shape[0] - 2 * D,), jnp.float32),
        bias_grad,
        tensor_place * local_qkv,
        0,
    )
    small_grad = lax.psum(
        jnp.concatenate([gain_one_grad, gain_two_grad, bias_slots]), ("dp", "tensor")
    )
    owned_squares = (
        jnp.sum(qkv_owned * qkv_owned)
        + jnp.sum(out_owned * out_owned)
        + jnp.sum(gateup_owned * gateup_owned)
        + jnp.sum(down_owned * down_owned)
    )
    squares = lax.psum(owned_squares, ("dp", "tensor")) + jnp.sum(small_grad * small_grad)
    grad_norm = jnp.sqrt(squares)
    clip_factor = jnp.minimum(1.0, MAX_NORM / (grad_norm + 1e-06))
    new_small, new_small_first, new_small_second = adam_update(
        small_params, small_first, small_second, clip_factor * small_grad, 0.5, 0.0
    )
    new_qkv, new_qkv_first, new_qkv_second = adam_update(
        qkv_weight, qkv_first, qkv_second, clip_factor * qkv_owned, 2.0 / math.sqrt(D), WEIGHT_DECAY
    )
    new_out, new_out_first, new_out_second = adam_update(
        out_weight,
        out_first,
        out_second,
        clip_factor * out_owned,
        8.0 / math.sqrt(QUERY_HEADS * HEAD_WIDTH),
        WEIGHT_DECAY,
    )
    new_gateup, new_gateup_first, new_gateup_second = adam_update(
        gateup_weight,
        gateup_first,
        gateup_second,
        clip_factor * gateup_owned,
        2.0 / math.sqrt(D),
        WEIGHT_DECAY,
    )
    new_down, new_down_first, new_down_second = adam_update(
        down_weight,
        down_first,
        down_second,
        clip_factor * down_owned,
        3.0 / math.sqrt(FF),
        WEIGHT_DECAY,
    )
    return (
        block_out,
        input_grad,
        grad_norm,
        new_small,
        new_small_first,
        new_small_second,
        new_qkv,
        new_qkv_first,
        new_qkv_second,
        new_out,
        new_out_first,
        new_out_second,
        new_gateup,
        new_gateup_first,
        new_gateup_second,
        new_down,
        new_down_first,
        new_down_second,
    )


def solution(mesh):
    return jax.shard_map(
        body,
        mesh=mesh,
        in_specs=(
            P(("dp", "tensor"), None),
            P(("dp", "tensor"), None),
            P("dp"),
            P(),
            P(),
            P(),
            P("dp", "tensor"),
            P("dp", "tensor"),
            P("dp", "tensor"),
            P("tensor", "dp"),
            P("tensor", "dp"),
            P("tensor", "dp"),
            P(None, "dp", "tensor"),
            P(None, "dp", "tensor"),
            P(None, "dp", "tensor"),
            P("tensor", "dp"),
            P("tensor", "dp"),
            P("tensor", "dp"),
        ),
        out_specs=(
            P(("dp", "tensor"), None),
            P(("dp", "tensor"), None),
            P(),
            P(),
            P(),
            P(),
            P("dp", "tensor"),
            P("dp", "tensor"),
            P("dp", "tensor"),
            P("tensor", "dp"),
            P("tensor", "dp"),
            P("tensor", "dp"),
            P(None, "dp", "tensor"),
            P(None, "dp", "tensor"),
            P(None, "dp", "tensor"),
            P("tensor", "dp"),
            P("tensor", "dp"),
            P("tensor", "dp"),
        ),
        check_vma=False,
    )
```

profile of v0, /device:TPU:0, one launch (start us, length us, event | category | flops | bytes accessed | tf_op | source)
XLA Modules:
  0.0 1762.5 jit_solution(12510758961325017284)
XLA Ops:
  19.6 22.2 %all-gather.9.cloned.1.call-done = bf16[512,1536]{1,0:T(8,128)(2,1)} async-done(((bf16[256,1536]{1,0:T(8,128)(2,1)}), bf16[512,1536]{1,0:T(8,128)(2,1)}) %all-gather.9.cloned.1.call-update) | async-done | bytes 1572880 | tf_op jit(solution)/shard_map/all_gather | solution.py:96
  41.9 48.1 %all-gather.11.cloned.1.call-done = bf16[1536,1024]{1,0:T(8,128)(2,1)} async-done(((bf16[96,1024]{1,0:T(8,128)(2,1)}), bf16[1536,1024]{1,0:T(8,128)(2,1)}) %all-gather.11.cloned.1.call-update) | async-done | bytes 3145744 | tf_op jit(solution)/shard_map/all_gather | solution.py:170
  110.5 23.8 %all-gather.13.cloned.1.call-done = bf16[768,1536]{0,1:T(8,128)(2,1)} async-done(((bf16[768,96]{0,1:T(8,128)(2,1)}), bf16[768,1536]{0,1:T(8,128)(2,1)}) %all-gather.13.cloned.1.call-update) | async-done | bytes 2359312 | tf_op jit(solution)/shard_map/all_gather | solution.py:171
  139.1 42.2 %reduce-scatter.9.cloned.1.call-done = f32[256,1536]{1,0:T(8,128)} async-done(((f32[512,1536]{1,0:T(8,128)}), f32[256,1536]{1,0:T(8,128)}) %reduce-scatter.9.cloned.1.call-update) | async-done | bytes 1572880 | tf_op jit(solution)/shard_map/reduce_scatter | solution.py:100
  190.9 20.9 %all-gather.15.cloned.1.call-done = bf16[512,1536]{1,0:T(8,128)(2,1)} async-done(((bf16[256,1536]{1,0:T(8,128)(2,1)}), bf16[512,1536]{1,0:T(8,128)(2,1)}) %all-gather.15.cloned.1.call-update) | async-done | bytes 1572880 | tf_op jit(solution)/shard_map/all_gather | solution.py:96
  211.8 141.8 %all-gather.17.cloned.1.call-done = bf16[2,1536,4480]{2,1,0:T(8,128)(2,1)} async-done(((bf16[2,96,4480]{2,1,0:T(8,128)(2,1)}), bf16[2,1536,4480]{2,1,0:T(8,128)(2,1)}) %all-gather.17.cloned.1.call-update) | async-done | bytes 27525136 | tf_op jit(solution)/shard_map/all_gather | solution.py:210
  353.6 13.2 fusion.6
  366.8 12.7 fusion.4
  382.5 111.3 %all-gather.19.cloned.1.call-done = bf16[4480,1536]{0,1:T(8,128)(2,1)} async-done(((bf16[4480,96]{0,1:T(8,128)(2,1)}), bf16[4480,1536]{0,1:T(8,128)(2,1)}) %all-gather.19.cloned.1.call-update) | async-done | bytes 13762576 | tf_op jit(solution)/shard_map/all_gather | solution.py:211
  493.8 21.7 %multiply_convert_fusion = (bf16[512,4480]{1,0:T(8,128)(2,1)}, bf16[512,4480]{1,0:T(8,128)(2,1)}, bf16[512,4480]{1,0:T(8,128)(2,1)}) fusion(f32[512,4480]{1,0:T(8,128)} %fusion.4, f32[512,4480]{1,0:T(8,128)} %fusion.6, bf16[512,1536]{1,0:T(8,128)(2,1)} %all-gather.21.cloned.1.call-done, bf16[4480,1536]{0,1:T(8,128)(2,1)} %all-gather.19.cloned.1.call-done), kind=kOutput, calls=%fused_computation.20 | convolution fusion | flops 7080837120 | bytes 47448064 | tf_op jit(solution)/shard_map/dot_general | solution.py:39
  527.3 12.0 fusion.18
  539.4 41.6 %reduce-scatter.13.cloned.1.call-done = f32[256,1536]{1,0:T(8,128)} async-done(((f32[512,1536]{1,0:T(8,128)}), f32[256,1536]{1,0:T(8,128)}) %reduce-scatter.13.cloned.1.call-update) | async-done | bytes 1572880 | tf_op jit(solution)/shard_map/reduce_scatter | solution.py:100
  585.2 27.3 %all-gather.23.cloned.1.call-done = bf16[512,1536]{1,0:T(8,128)(2,1)} async-done(((bf16[256,1536]{1,0:T(8,128)(2,1)}), bf16[512,1536]{1,0:T(8,128)(2,1)}) %all-gather.23.cloned.1.call-update) | async-done | bytes 1572880 | tf_op jit(solution)/shard_map/all_gather | solution.py:96
  667.1 14.7 fusion.92
  683.3 14.8 convolution_bitcast_fusion
  698.1 14.6 convolution_bitcast_fusion.1
  712.7 38.7 %pad_maximum_fusion = f32[2,1536,4480]{2,1,0:T(8,128)} fusion(f32[1,1536,4480]{2,1,0:T(8,128)} %convolution_bitcast_fusion, f32[1,1536,4480]{2,1,0:T(8,128)} %convolution_bitcast_fusion.1), kind=kLoop, calls=%fused_computation | loop fusion | flops 13762560 | bytes 110100480 | tf_op jit(solution)/shard_map/stack | solution.py:236
  751.4 13.3 fusion.88
  767.8 13.1 reduce-scatter.19.cloned.1.call-done
  782.6 86.6 %reduce-scatter.17.cloned.1.call-done = f32[96,1024]{1,0:T(8,128)} async-done(((f32[1536,1024]{1,0:T(8,128)}), f32[96,1024]{1,0:T(8,128)}) %reduce-scatter.17.cloned.1.call-update) | async-done | bytes 393232 | tf_op jit(solution)/shard_map/reduce_scatter | solution.py:307
  872.2 263.7 %reduce-scatter.23.cloned.1.call-done = f32[4480,96]{0,1:T(8,128)} async-done(((f32[4480,1536]{0,1:T(8,128)}), f32[4480,96]{0,1:T(8,128)}) %reduce-scatter.23.cloned.1.call-update) | async-done | bytes 1720336 | tf_op jit(solution)/shard_map/reduce_scatter | solution.py:241
  1138.4 507.2 %reduce-scatter.21.cloned.1.call-done = f32[2,96,4480]{2,1,0:T(8,128)} async-done(((f32[2,1536,4480]{2,1,0:T(8,128)}), f32[2,96,4480]{2,1,0:T(8,128)}) %reduce-scatter.21.cloned.1.call-update) | async-done | bytes 3440656 | tf_op jit(solution)/shard_map/reduce_scatter | solution.py:240
  1650.4 40.4 %reduce-scatter.11.cloned.1.call-done = f32[256,1536]{1,0:T(8,128)} async-done(((f32[512,1536]{1,0:T(8,128)}), f32[256,1536]{1,0:T(8,128)}) %reduce-scatter.11.cloned.1.call-update) | async-done | bytes 1572880 | tf_op jit(solution)/shard_map/reduce_scatter | solution.py:100
  1695.4 40.0 %all-reduce = (f32[]{:T(128)}, f32[5120]{0:T(1024)S(1)}) all-reduce(f32[]{:T(128)S(6)} %add.199, f32[5120]{0:T(1024)S(1)} %pad_maximum_fusion.6), channel_id=1, replica_groups=mesh['dp'=16,'tensor'=2] {'dp','tensor'}, use_global_device_ids=true, to_apply=%region_21.22 | all-reduce | flops 5121 | bytes 40968 | tf_op jit(solution)/shard_map/psum | solution.py:326
  (267 shorter events, 156.1 us)
Async XLA Ops:
  7.2 34.6 %all-gather.9.cloned.1.call-start = ((), (), s32[]{:S(2)}) async-start(), calls=%async_computation.8 | async-start | bytes 2359296 | tf_op jit(solution)/shard_map/all_gather | solution.py:96
  11.8 78.2 %all-gather.11.cloned.1.call-start = ((), (), s32[]{:S(2)}) async-start(), calls=%async_computation.9 | async-start | bytes 3342336 | tf_op jit(solution)/shard_map/all_gather | solution.py:170
  12.6 121.7 %all-gather.13.cloned.1.call-start = ((), (), s32[]{:S(2)}) async-start(), calls=%async_computation.10 | async-start | bytes 2506752 | tf_op jit(solution)/shard_map/all_gather | solution.py:171
  12.6 3.2 collective-permute-start
  15.7 165.6 %reduce-scatter.9.cloned.1.call-start = ((), (), s32[]{:S(2)}) async-start(), calls=%async_computation.11 | async-start | bytes 4718592 | tf_op jit(solution)/shard_map/reduce_scatter | solution.py:100
  96.4 3.8 collective-permute-start.1
  139.1 72.7 %all-gather.15.cloned.1.call-start = ((), (), s32[]{:S(2)}) async-start(), calls=%async_computation.12 | async-start | bytes 2359296 | tf_op jit(solution)/shard_map/all_gather | solution.py:96
  184.4 169.1 %all-gather.17.cloned.1.call-start = ((), (), s32[]{:S(2)}) async-start(), calls=%async_computation.13 | async-start | bytes 29245440 | tf_op jit(solution)/shard_map/all_gather | solution.py:210
  187.9 194.6 %all-gather.21.cloned.1.call-start = ((), (), s32[]{:S(2)}) async-start(), calls=%async_computation.16 | async-start | bytes 2359296 | tf_op jit(solution)/shard_map/all_gather | solution.py:96
  188.6 305.1 %all-gather.19.cloned.1.call-start = ((), (), s32[]{:S(2)}) async-start(), calls=%async_computation.14 | async-start | bytes 14622720 | tf_op jit(solution)/shard_map/all_gather | solution.py:211
  190.3 390.7 %reduce-scatter.13.cloned.1.call-start = ((), (), s32[]{:S(2)}) async-start(), calls=%async_computation.17 | async-start | bytes 4718592 | tf_op jit(solution)/shard_map/reduce_scatter | solution.py:100
  539.4 73.1 %all-gather.23.cloned.1.call-start = ((), (), s32[]{:S(2)}) async-start(), calls=%async_computation.18 | async-start | bytes 2359296 | tf_op jit(solution)/shard_map/all_gather | solution.py:96
  585.1 179.7 %reduce-scatter.15.cloned.1.call-start = ((), (), s32[]{:S(2)}) async-start(), calls=%async_computation.19 | async-start | bytes 4718592 | tf_op jit(solution)/shard_map/reduce_scatter | solution.py:100
  639.5 5.1 collective-permute-start.2
  653.2 127.8 %reduce-scatter.19.cloned.1.call-start = ((), (), s32[]{:S(2)}) async-start(), calls=%async_computation.21 | async-start | bytes 5013504 | tf_op jit(solution)/shard_map/reduce_scatter | solution.py:308
  659.3 209.9 %reduce-scatter.17.cloned.1.call-start = ((), (), s32[]{:S(2)}) async-start(), calls=%async_computation.20 | async-start | bytes 6684672 | tf_op jit(solution)/shard_map/reduce_scatter | solution.py:307
  665.8 470.1 %reduce-scatter.23.cloned.1.call-start = ((), (), s32[]{:S(2)}) async-start(), calls=%async_computation.23 | async-start | bytes 29245440 | tf_op jit(solution)/shard_map/reduce_scatter | solution.py:241
  681.9 963.7 %reduce-scatter.21.cloned.1.call-start = ((), (), s32[]{:S(2)}) async-start(), calls=%async_computation.22 | async-start | bytes 58490880 | tf_op jit(solution)/shard_map/reduce_scatter | solution.py:240
  751.4 939.5 %reduce-scatter.11.cloned.1.call-start = ((), (), s32[]{:S(2)}) async-start(), calls=%async_computation.15 | async-start | bytes 4718592 | tf_op jit(solution)/shard_map/reduce_scatter | solution.py:100
  1138.4 552.4 %copy-start.2 = (f32[256,1536]{1,0:T(8,128)S(1)}, f32[256,1536]{1,0:T(8,128)}, u32[]{:S(2)}) copy-start(f32[256,1536]{1,0:T(8,128)} %copy-done.1) | copy-start | bytes 4718596
  1138.4 552.4 %copy-start.10 = (bf16[256,1536]{1,0:T(8,128)(2,1)S(1)}, bf16[256,1536]{1,0:T(8,128)(2,1)}, u32[]{:S(2)}) copy-start(bf16[256,1536]{1,0:T(8,128)(2,1)} %param.19) | copy-start | bytes 2359300
  1138.4 552.4 %copy-start.38 = (f32[1536]{0:T(1024)S(1)}, f32[1536]{0:T(1024)}, u32[]{:S(2)}) copy-start(f32[1536]{0:T(1024)} %copy-done.36) | copy-start | bytes 18436
  1138.4 552.4 %copy-start.51 = (f32[256]{0:T(256)S(1)}, f32[256]{0:T(256)}, u32[]{:S(2)}) copy-start(f32[256]{0:T(256)} %copy-done.49) | copy-start | bytes 3076
  1138.4 552.4 %copy-start.58 = (f32[256]{0:T(256)S(1)}, f32[256]{0:T(256)}, u32[]{:S(2)}) copy-start(f32[256]{0:T(256)} %copy-done.57) | copy-start | bytes 3076
  (66 other events, 1982.2 us)
Sparse Core Ops, SparseCore 0:
  11.9 29.9 all-gather.8
  44.7 45.1 all-gather.10
  92.8 41.4 all-gather.12
  139.2 42.1 reduce-scatter.8
  184.6 27.2 all-gather.14
  213.9 139.6 all-gather.16
  355.2 27.1 all-gather.20
  385.6 108.1 all-gather.18
  539.5 41.5 reduce-scatter.12
  585.2 27.2 all-gather.22
  653.3 47.8 reduce-scatter.14
  705.4 75.5 reduce-scatter.18
  784.9 84.2 reduce-scatter.16
  873.7 262.1 reduce-scatter.22
  1140.0 505.5 reduce-scatter.20
  1648.3 42.4 reduce-scatter.10
where the time goes:
time: 1770 us; the launch traced here: 1760 us
  waiting for transfers between devices  1390 us (79%)
  matrix products  184 us (10%)
  other arithmetic  102 us (6%)
  blocking collectives  40 us (2%)
  between operations  20.4 us (1%)
    reduce_scatter x1, waiting for transfers between devices, body(): lax.psum_scatter(gateup_grad, 'dp', scatter_dimension=1, tiled=True)  507 us
    reduce_scatter x1, waiting for transfers between devices, body(): lax.psum_scatter(down_grad, 'dp', scatter_dimension=1, tiled=True)  264 us
    all_gather x1, waiting for transfers between devices, body(): lax.all_gather(gateup_weight.astype(jnp.bfloat16), 'dp', axis=1, tiled=True)  142 us
    reduce_scatter x4, waiting for transfers between devices, sum_rows(): lax.psum_scatter(term(jnp.int32(0), row_count * lax.axis_size('tensor')),...  124 us
    all_gather x1, waiting for transfers between devices, body(): lax.all_gather(down_weight.astype(jnp.bfloat16), 'dp', axis=1, tiled=True)  111 us
    reduce_scatter x1, waiting for transfers between devices, body(): lax.psum_scatter(qkv_grad, 'dp', scatter_dimension=0, tiled=True)  86.6 us
    all_gather x4, waiting for transfers between devices, gather_rows(): return lax.all_gather(row_block, 'tensor', axis=0, tiled=True)  73.4 us
    dot_general x5, matrix products, contract_rows(): lax.dot_general(left_side, right_side, (((0,), (0,)), ((), ())), preferre...  55.5 us
  transfers between devices with their start and end apart: 19, of which 15 were waited for; matrix products, arithmetic and copies ran while one was open for 10% of the time, Pallas kernels for 0%

commit v1 on v0

v1 whole, which is shorter than its diff:
```python
import functools
import math

import jax
import jax.numpy as jnp
from jax import lax
from jax.experimental import pallas as pl
from jax.experimental.pallas import tpu as pltpu
from jax.sharding import Mesh
from jax.sharding import PartitionSpec as P

D = 1536
FF = 8960
QUERY_HEADS = 12
KEY_VALUE_HEADS = 2
HEAD_WIDTH = 128
STEP = 10

EPSILON = 1e-06
ROPE_BASE = 1000000.0
BETA_ONE = 0.9
BETA_TWO = 0.999
ADAM_EPS = 1e-08
WEIGHT_DECAY = 0.1
MAX_NORM = 1.0
NEGATIVE = -1e30

BF = jnp.bfloat16
F32 = jnp.float32
HEADS = 3
Q_COLS = HEADS * HEAD_WIDTH
QKV_COLS = Q_COLS + 2 * HEAD_WIDTH
ATT_COLS = QKV_COLS + Q_COLS
FF_LOCAL = FF // 2
FF_PAD = 4608
FF_CORE = FF_PAD // 2
FF_OWN = FF_PAD // 4
TILE = 256
VMEM_LIMIT = 60 * 2**20
CHIP = ("hi", "lo", "yy")


def dot_ab(a, b):
    return lax.dot_general(a, b, (((1,), (0,)), ((), ())), preferred_element_type=F32)


def dot_abt(a, b):
    return lax.dot_general(a, b, (((1,), (1,)), ((), ())), preferred_element_type=F32)


def dot_atb(a, b):
    return lax.dot_general(a, b, (((0,), (0,)), ((), ())), preferred_element_type=F32)


def rms_scale(inputs):
    return lax.rsqrt(jnp.mean(inputs * inputs, axis=-1, keepdims=True) + EPSILON)


def norm_backward(inputs, inv_rms, gain_vec, upstream):
    normed = inputs * inv_rms
    normed_grad = upstream * gain_vec
    input_part = inv_rms * (
        normed_grad - normed * jnp.mean(normed_grad * normed, axis=-1, keepdims=True)
    )
    return (input_part, jnp.sum(upstream * normed, axis=0))


def adam_update(weight, moment_one, moment_two, gradient, step_rate, decay_rate):
    first_new = BETA_ONE * moment_one + (1.0 - BETA_ONE) * gradient
    second_new = BETA_TWO * moment_two + (1.0 - BETA_TWO) * gradient * gradient
    corrected = first_new / (1.0 - BETA_ONE**STEP)
    spread = jnp.sqrt(second_new / (1.0 - BETA_TWO**STEP)) + ADAM_EPS
    return (
        weight * (1.0 - step_rate * decay_rate) - step_rate * corrected / spread,
        first_new,
        second_new,
    )


def swap(value, axis):
    return lax.ppermute(value, axis, [(0, 1), (1, 0)])


class Order:
    def __init__(self):
        self.mark = None

    def after(self, value):
        if self.mark is None:
            return value
        return lax.optimization_barrier((value, self.mark))[0]

    def done(self, value):
        value = self.after(value)
        self.mark = value
        return value


def chip_at(step, other_lo, other_yy):
    count = lax.axis_size("hi")
    hi = (lax.axis_index("hi") + step) % count
    return (hi * 2 + (lax.axis_index("lo") ^ other_lo)) * 2 + (lax.axis_index("yy") ^ other_yy)


def turn(value, axis, steps):
    count = lax.axis_size(axis)
    return lax.ppermute(value, axis, [(i, (i + steps) % count) for i in range(count)])


def tree_order(sign):
    steps = [(0, 0), (0, 1)] + [(k, l) for k in range(1, lax.axis_size("hi")) for l in (0, 1)]
    return jnp.stack([chip_at(sign * k, l, y) for y in (0, 1) for k, l in steps]).astype(jnp.int32)


def sum_order():
    steps = range(1, lax.axis_size("hi"))
    chips = [chip_at(k, l, y) for l in (1, 0) for ks in (steps, (0,)) for k in ks for y in (1, 0)]
    return jnp.stack(chips).astype(jnp.int32)


class ChipSum:
    def __init__(self, lo_far, lo_near, far, near):
        self.far, self.near = far, near
        self.lo_far, self.lo_near = swap(lo_far, "lo"), swap(lo_near, "lo")

    def far_yy(self, order):
        self.far = self.far.astype(F32) + order.done(self.lo_far).astype(F32)
        theirs = self.far[0::2].astype(BF)
        self.yy_far = swap(theirs, "yy")
        order.mark = theirs

    def far_hi(self, order):
        far = (self.far[1::2] + order.done(self.yy_far).astype(F32)).astype(BF)
        self.hi = [turn(far[k - 1], "hi", k) for k in range(1, lax.axis_size("hi"))]
        order.mark = far

    def near_yy(self, order):
        self.near = self.near.astype(F32) + order.done(self.lo_near).astype(F32)
        theirs = self.near[0].astype(BF)
        self.yy_near = swap(theirs, "yy")
        order.mark = theirs

    def total(self, order):
        hi = order.done(self.hi)
        total = self.near[1] + order.done(self.yy_near).astype(F32)
        for part in hi:
            total = total + part.astype(F32)
        return total


def cost(flops, bytes_accessed, transcendentals):
    part = 4096
    return pl.CostEstimate(
        flops=flops // part,
        bytes_accessed=bytes_accessed // part,
        transcendentals=transcendentals // part,
    )


ANYWHERE = pl.BlockSpec(memory_space=pl.ANY)
WHOLE = pl.BlockSpec(memory_space=pltpu.VMEM)


def turn_halves(features, cos_both, sin_both):
    return features * cos_both + pltpu.roll(features, HEAD_WIDTH // 2, 1) * sin_both


def scores_t(keys, queries, key_place, place, start):
    scores = dot_abt(keys, queries) * (1.0 / math.sqrt(HEAD_WIDTH))
    return jnp.where((key_place <= place) & (key_place >= start), scores, NEGATIVE)


def attention_kernel(
    parts,
    rows,
    chips_ref,
    near_ref,
    far_ref,
    bias_ref,
    cos_ref,
    sin_ref,
    key_place_ref,
    place_ref,
    start_ref,
    *refs,
):
    shards, refs = refs[:parts], refs[parts:]
    qkv_ref, o_ref, lse_ref, *out_refs, weight_ref, weights, sems, out_sem = refs
    half = near_ref.shape[0]
    copies = [
        pltpu.make_async_copy(
            shards[i],
            weights.at[pl.ds(pl.multiple_of(chips_ref[i] * rows, rows), rows), :],
            sems.at[i],
        )
        for i in range(parts)
    ]
    for copy in copies:
        copy.start()
    for copy in copies:
        copy.wait()
    save = pltpu.make_async_copy(weights, weight_ref, out_sem)
    save.start()
    for side, ref in enumerate((near_ref, far_ref)):
        at = slice(side * half, (side + 1) * half)
        projected = dot_ab(ref[...], weights[:, :QKV_COLS]) + bias_ref[...]
        cos_both, sin_both = cos_ref[at, :], sin_ref[at, :]
        for j in range(HEADS + 1):
            cols = slice(j * HEAD_WIDTH, (j + 1) * HEAD_WIDTH)
            qkv_ref[at, cols] = turn_halves(projected[:, cols], cos_both, sin_both).astype(BF)
        cols = slice(Q_COLS + HEAD_WIDTH, QKV_COLS)
        qkv_ref[at, cols] = projected[:, cols].astype(BF)
    keys = qkv_ref[:, Q_COLS : Q_COLS + HEAD_WIDTH]
    values_t = qkv_ref[:, Q_COLS + HEAD_WIDTH : QKV_COLS].T
    lse_ref[...] = jnp.zeros_like(lse_ref)
    key_place = key_place_ref[...]
    for at in range(0, 2 * half, TILE):
        block = slice(at, at + TILE)
        place, start = place_ref[:, block], start_ref[:, block]
        for h in range(HEADS):
            cols = slice(h * HEAD_WIDTH, (h + 1) * HEAD_WIDTH)
            scores = scores_t(keys, qkv_ref[block, cols], key_place, place, start)
            top = jnp.max(scores, axis=0, keepdims=True)
            weights_exp = jnp.exp(scores - top)
            total = jnp.sum(weights_exp, axis=0, keepdims=True)
            lse_ref[h : h + 1, block] = top + jnp.log(total)
            prob = (weights_exp * (1.0 / total)).astype(BF)
            o_ref[block, cols] = dot_ab(values_t, prob).astype(BF).T
    for side in range(2):
        part = dot_abt(o_ref[side * half : (side + 1) * half, :], weights[:, QKV_COLS:])
        out_refs[2 * side][...] = part[: half // 2].astype(BF)
        out_refs[2 * side + 1][...] = part[half // 2 :].astype(BF)
    save.wait()


def attention(chips, rows_pair, bias, tables, shards):
    near, far = rows_pair
    half = near.shape[0]
    length = 2 * half
    parts = len(shards)
    rows = shards[0].shape[0]
    return pl.pallas_call(
        functools.partial(attention_kernel, parts, rows),
        grid_spec=pltpu.PrefetchScalarGridSpec(
            num_scalar_prefetch=1,
            grid=(),
            in_specs=[WHOLE] * 8 + [ANYWHERE] * parts,
            out_specs=[WHOLE] * 7 + [ANYWHERE],
            scratch_shapes=[
                pltpu.VMEM((D, ATT_COLS), BF),
                pltpu.SemaphoreType.DMA((parts,)),
                pltpu.SemaphoreType.DMA,
            ],
        ),
        out_shape=[
            jax.ShapeDtypeStruct((length, QKV_COLS), BF),
            jax.ShapeDtypeStruct((length, Q_COLS), BF),
            jax.ShapeDtypeStruct((8, length), F32),
            *[jax.ShapeDtypeStruct((half // 2, D), BF)] * 4,
            jax.ShapeDtypeStruct((D, ATT_COLS), BF),
        ],
        compiler_params=pltpu.CompilerParams(vmem_limit_bytes=VMEM_LIMIT),
        cost_estimate=cost(
            flops=2 * length * D * ATT_COLS + 4 * HEADS * length * length * HEAD_WIDTH,
            bytes_accessed=16 * 2**20,
            transcendentals=HEADS * length * length,
        ),
        name="attention",
    )(chips, near, far, bias, *tables, *shards)


def attention_back_kernel(
    count,
    rows,
    chips_ref,
    near_ref,
    far_ref,
    n1_near_ref,
    n1_far_ref,
    qkv_ref,
    o_ref,
    lse_ref,
    weight_ref,
    cos_ref,
    sin_ref,
    key_place_ref,
    place_ref,
    start_ref,
    dqkv_ref,
    bias_ref,
    *refs,
):
    *out_refs, mixed, grads = refs
    half = near_ref.shape[0]
    length = 2 * half
    scale = 1.0 / math.sqrt(HEAD_WIDTH)
    for side, ref in enumerate((near_ref, far_ref)):
        mixed[side * half : (side + 1) * half, :] = dot_ab(
            ref[...], weight_ref[:, QKV_COLS:]
        ).astype(BF)
    key_cols = slice(Q_COLS, Q_COLS + HEAD_WIDTH)
    value_cols = slice(Q_COLS + HEAD_WIDTH, QKV_COLS)
    keys, values = qkv_ref[:, key_cols], qkv_ref[:, value_cols]
    keys_t = keys.T
    key_place = key_place_ref[...]
    keys_grad = jnp.zeros((length, HEAD_WIDTH), F32)
    values_grad = jnp.zeros((length, HEAD_WIDTH), F32)
    for at in range(0, length, TILE):
        block = slice(at, at + TILE)
        place, start = place_ref[:, block], start_ref[:, block]
        for h in range(HEADS):
            cols = slice(h * HEAD_WIDTH, (h + 1) * HEAD_WIDTH)
            queries, up = qkv_ref[block, cols], mixed[block, cols]
            scores = scores_t(keys, queries, key_place, place, start)
            prob = jnp.exp(scores - lse_ref[h : h + 1, block])
            prob_grad = dot_abt(values, up)
            inner = jnp.sum(prob * prob_grad, axis=0, keepdims=True)
            score_grad = (prob * (prob_grad - inner)).astype(BF)
            values_grad += dot_ab(prob.astype(BF), up)
            keys_grad += dot_ab(score_grad, queries)
            query_grad = dot_ab(keys_t, score_grad).T * scale
            dqkv_ref[block, cols] = turn_halves(
                query_grad, cos_ref[block, :], -sin_ref[block, :]
            ).astype(BF)
    dqkv_ref[:, key_cols] = turn_halves(keys_grad * scale, cos_ref[...], -sin_ref[...]).astype(BF)
    dqkv_ref[:, value_cols] = values_grad.astype(BF)
    bias_ref[...] = jnp.sum(dqkv_ref[...].astype(F32), axis=0, keepdims=True)
    for cols, pair, right_ref in (
        (slice(0, QKV_COLS), (n1_near_ref, n1_far_ref), dqkv_ref),
        (slice(QKV_COLS, ATT_COLS), (near_ref, far_ref), o_ref),
    ):
        grads[:, :, cols] = (
            dot_ab(pair[0][...].T, right_ref[:half, :]) + dot_ab(pair[1][...].T, right_ref[half:, :])
        ).astype(BF).reshape(4 * count, rows, -1)
    at = 0
    for ref in out_refs:
        for k in range(ref.shape[0]):
            ref[k] = grads[chips_ref[at]]
            at += 1


def attention_back(chips, da_pair, n1_pair, qkv, o, lse, weight, tables):
    length = qkv.shape[0]
    count = chips.shape[0] // 4
    rows = D // (4 * count)
    blocks = [
        jax.ShapeDtypeStruct((2 * k, rows, ATT_COLS), BF) for k in (count - 1, 1, count - 1, 1)
    ]
    return pl.pallas_call(
        functools.partial(attention_back_kernel, count, rows),
        grid_spec=pltpu.PrefetchScalarGridSpec(
            num_scalar_prefetch=1,
            grid=(),
            in_specs=[WHOLE] * 13,
            out_specs=[WHOLE] * 6,
            scratch_shapes=[
                pltpu.VMEM((length, Q_COLS), BF),
                pltpu.VMEM((4 * count, rows, ATT_COLS), BF),
            ],
        ),
        out_shape=[
            jax.ShapeDtypeStruct((length, QKV_COLS), BF),
            jax.ShapeDtypeStruct((1, QKV_COLS), F32),
            *blocks,
        ],
        compiler_params=pltpu.CompilerParams(vmem_limit_bytes=VMEM_LIMIT),
        cost_estimate=cost(
            flops=2 * length * D * 2 * ATT_COLS + 10 * HEADS * length * length * HEAD_WIDTH,
            bytes_accessed=24 * 2**20,
            transcendentals=HEADS * length * length,
        ),
        name="attention_back",
    )(chips, *da_pair, *n1_pair, qkv, o, lse, weight, *tables)


def feed_forward_kernel(whole, split, rows, chips_ref, *refs):
    n2_refs, dy_refs, refs = refs[:2], refs[2:4], refs[4:]
    pieces, refs = refs[: whole + 2 * split], refs[whole + 2 * split :]
    keep_ref, send_ref, u_ref, dgate_ref, dup_ref, *refs = refs
    n2_t_ref, dy_t_ref, down_ref, gu_w, d_w, n2_s, dy_s, sems, out_sem = refs
    step = pl.program_id(0)
    steps = pl.num_programs(0)

    def copies():
        for i in range(whole + split):
            at = pl.ds(pl.multiple_of(chips_ref[i] * rows, rows), rows)
            for j in range(3):
                if i < whole:
                    here = pieces[i].at[j]
                elif j < 2:
                    here = pieces[i].at[j]
                else:
                    here = pieces[i + split]
                if j < 2:
                    there = gu_w.at[at, pl.ds(j * FF_OWN, FF_OWN)]
                else:
                    there = d_w.at[at, :]
                yield pltpu.make_async_copy(here, there, sems.at[i, j])

    save = pltpu.make_async_copy(d_w, down_ref, out_sem)

    @pl.when(step == 0)
    def _():
        for copy in copies():
            copy.start()
        for copy in copies():
            copy.wait()
        save.start()

    for j in range(2):

        @pl.when(step // 4 == j)
        def _(j=j):
            n2_s[...] = n2_refs[j][...]
            dy_s[...] = dy_refs[j][...]

    n2, dy = n2_s[...], dy_s[...]
    n2_t_ref[...] = n2.T
    dy_t_ref[...] = dy.T
    gate_up = dot_ab(n2, gu_w[...])
    du = dot_ab(dy, d_w[...])
    gate, up = gate_up[:, :FF_OWN], gate_up[:, FF_OWN:]
    sig = jax.nn.sigmoid(gate)
    silu = gate * sig
    u_ref[...] = (silu * up).astype(BF)
    dup = (du * silu).astype(BF)
    dgate = (du * up * sig * (1.0 + gate * (1.0 - sig))).astype(BF)
    dup_ref[...] = dup
    dgate_ref[...] = dgate
    dn2 = dot_abt(jnp.concatenate([dgate, dup], axis=1), gu_w[...]).astype(BF)

    @pl.when(step < steps // 2)
    def _():
        keep_ref[...] = dn2

    @pl.when(step >= steps // 2)
    def _():
        send_ref[...] = dn2

    @pl.when(step == steps - 1)
    def _():
        save.wait()


def feed_forward(chips, n2, dy, whole, split):
    rows = whole[0].shape[1]
    one = n2[0].shape[0] // 4
    length = 8 * one
    tile = lambda width: pl.BlockSpec((one, width), lambda i, c: (i, 0))
    turned = pl.BlockSpec((D, one), lambda i, c: (0, i))
    taken = [
        pl.BlockSpec((one, D), lambda i, c: (jnp.minimum(i, 3), 0)),
        pl.BlockSpec((one, D), lambda i, c: (jnp.maximum(i - 4, 0), 0)),
    ]
    parts = len(whole) + len(split)
    return pl.pallas_call(
        functools.partial(feed_forward_kernel, len(whole), len(split), rows),
        grid_spec=pltpu.PrefetchScalarGridSpec(
            num_scalar_prefetch=1,
            grid=(8,),
            in_specs=taken * 2 + [ANYWHERE] * (len(whole) + 2 * len(split)),
            out_specs=taken + [tile(FF_OWN)] * 3 + [turned, turned, ANYWHERE],
            scratch_shapes=[
                pltpu.VMEM((D, 2 * FF_OWN), BF),
                pltpu.VMEM((D, FF_OWN), BF),
                pltpu.VMEM((one, D), BF),
                pltpu.VMEM((one, D), BF),
                pltpu.SemaphoreType.DMA((parts, 3)),
                pltpu.SemaphoreType.DMA,
            ],
        ),
        out_shape=[jax.ShapeDtypeStruct((length // 2, D), BF)] * 2
        + [jax.ShapeDtypeStruct((length, FF_OWN), BF)] * 3
        + [jax.ShapeDtypeStruct((D, length), BF)] * 2
        + [jax.ShapeDtypeStruct((D, FF_OWN), BF)],
        compiler_params=pltpu.CompilerParams(vmem_limit_bytes=VMEM_LIMIT),
        cost_estimate=cost(
            flops=2 * 5 * length * D * FF_OWN,
            bytes_accessed=60 * 2**20,
            transcendentals=length * FF_OWN,
        ),
        name="feed_forward",
    )(chips, *n2, *dy, *whole, *[gu for gu, _ in split], *[d for _, d in split])


def weight_grad_kernel(rows, place_ref, left_ref, right_ref, *refs):
    out_refs, total = refs[:4], refs[4]
    width = right_ref.shape[1]
    for at in range(0, width, 256):
        to = min(at + 256, width)
        total[:, :, at:to] = dot_ab(left_ref[...], right_ref[:, at:to]).reshape(
            4, rows, to - at
        )
    lo, yy = place_ref[1], place_ref[2]
    for k in range(2):
        row = jnp.where(lo == 0, k, 1 - k) * 2
        out_refs[k][0] = total[row + yy].astype(BF)
        out_refs[2 + k][0] = total[row + 1 - yy].astype(BF)


def weight_grad(place, left, right):
    count = lax.axis_size("hi")
    length, width = right.shape
    rows = left.shape[0] // (4 * count)
    block = pl.BlockSpec((1, rows, width), lambda i, p: (i, 0, 0))
    out = jax.ShapeDtypeStruct((count, rows, width), BF)
    return pl.pallas_call(
        functools.partial(weight_grad_kernel, rows),
        grid_spec=pltpu.PrefetchScalarGridSpec(
            num_scalar_prefetch=1,
            grid=(count,),
            in_specs=[
                pl.BlockSpec((4 * rows, length), lambda i, p: (lax.rem(i + p[0], count), 0)),
                pl.BlockSpec((length, width), lambda i, p: (0, 0)),
            ],
            out_specs=[block] * 4,
            scratch_shapes=[pltpu.VMEM((4, rows, width), F32)],
        ),
        out_shape=[out] * 4,
        compiler_params=pltpu.CompilerParams(vmem_limit_bytes=VMEM_LIMIT),
        cost_estimate=cost(
            flops=2 * length * D * width, bytes_accessed=16 * 2**20, transcendentals=0
        ),
        name="weight_grad",
    )(place, left, right)


def down_kernel(left_ref, right_ref, keep_ref, send_ref):
    step = pl.program_id(0)
    product = dot_abt(left_ref[...], right_ref[...]).astype(BF)

    @pl.when(step < pl.num_programs(0) // 2)
    def _():
        keep_ref[...] = product

    @pl.when(step >= pl.num_programs(0) // 2)
    def _():
        send_ref[...] = product


def down(left, right):
    length, width = left.shape
    one = length // 8
    return pl.pallas_call(
        down_kernel,
        grid=(8,),
        in_specs=[
            pl.BlockSpec((one, width), lambda i: (i, 0)),
            pl.BlockSpec((D, width), lambda i: (0, 0)),
        ],
        out_specs=[
            pl.BlockSpec((one, D), lambda i: (jnp.minimum(i, 3), 0)),
            pl.BlockSpec((one, D), lambda i: (jnp.maximum(i - 4, 0), 0)),
        ],
        out_shape=[jax.ShapeDtypeStruct((length // 2, D), BF)] * 2,
        compiler_params=pltpu.CompilerParams(vmem_limit_bytes=VMEM_LIMIT),
        cost_estimate=cost(
            flops=2 * length * D * width, bytes_accessed=14 * 2**20, transcendentals=0
        ),
        name="down",
    )(left, right)


class EightSum:
    def __init__(self, keep, send):
        self.keep = keep
        self.one = keep.shape[0] // 4
        self.half = self.one // 2
        self.core = swap(send, "core")

    def part(self, begin, rows):
        at = slice(begin, begin + rows)
        return self.keep[at].astype(F32) + self.core[at].astype(F32)

    def second(self, order):
        self.core = order.done(self.core)
        one, half = self.one, self.half
        both_lo = self.part(3 * one, half).astype(BF)
        both_x = self.part(3 * one + half, half).astype(BF)
        self.to_lo, self.to_x = swap(both_lo, "tensor"), swap(both_x, "lo")

    def third(self, order):
        one, half = self.one, self.half
        to_lo, to_x = order.done((self.to_lo, self.to_x))
        by_x = [self.part(one, half), self.part(one + half, half) + to_x.astype(F32)]
        by_lo = [self.part(2 * one, half) + to_lo.astype(F32), self.part(2 * one + half, half)]
        self.by_x = swap(jnp.concatenate(by_x, axis=0).astype(BF), "tensor")
        self.by_lo = swap(jnp.concatenate(by_lo, axis=0).astype(BF), "lo")

    def total(self, order):
        by_x, by_lo = order.done((self.by_x, self.by_lo))
        return self.part(0, self.one) + by_x.astype(F32) + by_lo.astype(F32)


class FourSum:
    def __init__(self, own, by_x, core_own, core_by_x):
        self.own, self.by_x = own, by_x
        self.core_by_x, self.core_own = swap(core_by_x, "core"), swap(core_own, "core")

    def second(self, order):
        core_by_x = order.done(self.core_by_x)
        by_x = (self.by_x.astype(F32) + core_by_x.astype(F32)).astype(BF)
        self.x = swap(by_x, "tensor")
        order.mark = by_x
        self.core_own = order.done(self.core_own)

    def total(self, order):
        x = order.done(self.x)
        return self.own.astype(F32) + self.core_own.astype(F32) + x.astype(F32)


class GradSum:
    def __init__(self, keep, send):
        self.keep = keep
        self.other = swap(send, "yy")

    def across(self, order):
        self.other = order.done(self.other)
        self.far = [
            turn((self.keep[k].astype(F32) + self.other[k].astype(F32)).astype(BF), "hi", k)
            for k in range(1, lax.axis_size("hi"))
        ]

    def total(self, order):
        self.far = order.done(self.far)
        total = self.keep[0].astype(F32) + self.other[0].astype(F32)
        for far in self.far:
            total = total + far.astype(F32)
        return total


def body(
    tokens,
    cotangent,
    segments,
    small_params,
    small_first,
    small_second,
    qkv_weight,
    qkv_first,
    qkv_second,
    out_weight,
    out_first,
    out_second,
    gateup_weight,
    gateup_first,
    gateup_second,
    down_weight,
    down_first,
    down_second,
):
    hi_count = lax.axis_size("hi")
    hi, lo, yy = lax.axis_index("hi"), lax.axis_index("lo"), lax.axis_index("yy")
    core = lax.axis_index("core")
    place_x = lax.axis_index("tensor")
    own_rows = tokens.shape[0]
    shard_rows = qkv_weight.shape[0]
    gain_one = small_params[:D]
    gain_two = small_params[D : 2 * D]
    bias_all = small_params[2 * D :]
    q_at = place_x * (bias_all.shape[0] // 2) + core * Q_COLS
    kv_at = place_x * (bias_all.shape[0] // 2) + 2 * Q_COLS
    bias_local = jnp.concatenate(
        [
            lax.dynamic_slice_in_dim(bias_all, q_at, Q_COLS),
            lax.dynamic_slice_in_dim(bias_all, kv_at, 2 * HEAD_WIDTH),
        ]
    )

    order = Order()
    steps = range(1, hi_count)

    def both_cores(mine, other, axis):
        return jnp.where(
            core == 0,
            jnp.concatenate([mine, other], axis=axis),
            jnp.concatenate([other, mine], axis=axis),
        )

    other_ids = swap(segments, "core")
    qkv_low = qkv_weight.astype(BF)
    out_low = out_weight.astype(BF).T

    def attention_pack(which):
        return jnp.concatenate(
            [
                lax.dynamic_slice_in_dim(qkv_low, which * Q_COLS, Q_COLS, 1),
                qkv_low[:, 2 * Q_COLS :],
                lax.dynamic_slice_in_dim(out_low, which * Q_COLS, Q_COLS, 1),
            ],
            axis=1,
        )

    att_theirs = attention_pack(1 - core)
    att_core = swap(att_theirs, "core")
    order.mark = att_theirs
    rows_in = order.after(tokens).astype(F32)
    scale_one = rms_scale(rows_in)
    n1 = (rows_in * scale_one * gain_one).astype(BF)
    n1_x = swap(n1, "tensor")
    order.mark = n1
    att_shard = both_cores(attention_pack(core), order.done(att_core), 0)
    order.mark = att_shard
    other_ids = order.done(other_ids)
    att_hi = [turn(att_shard, "hi", k) for k in steps]
    att_yy = swap(att_shard, "yy")
    att_lo = swap(att_shard, "lo")

    gateup_in, down_in = order.after((gateup_weight, down_weight))
    ff_low = jnp.pad(
        jnp.concatenate([gateup_in.astype(BF), down_in.astype(BF).T[None]], axis=0),
        ((0, 0), (0, 0), (0, FF_PAD - FF_LOCAL)),
    )
    ff_mine = lax.dynamic_slice_in_dim(ff_low, core * FF_CORE, FF_CORE, 2)
    ff_theirs = lax.dynamic_slice_in_dim(ff_low, (1 - core) * FF_CORE, FF_CORE, 2)
    ff_core = swap(ff_theirs, "core")
    order.mark = ff_theirs
    ff_shard = both_cores(ff_mine, order.done(ff_core), 1)
    ff_own = lax.dynamic_slice_in_dim(ff_shard, lo * FF_OWN, FF_OWN, 2)
    ff_theirs = lax.dynamic_slice_in_dim(ff_shard, (1 - lo) * FF_OWN, FF_OWN, 2)
    order.mark = ff_theirs
    ff_hi = [turn(ff_own, "hi", k) for k in steps]
    ff_lo = swap(ff_theirs, "lo")
    att_lo = order.done(att_lo)
    att_lo_yy = swap(att_lo, "yy")

    ids = both_cores(segments, other_ids, 0)
    length = ids.shape[0]
    places = jnp.arange(length, dtype=jnp.int32)
    earlier = jnp.concatenate([ids[:1], ids[:-1]])
    starts = lax.cummax(jnp.where((places == 0) | (ids != earlier), places, 0), axis=0)

    def own_first(values):
        parts = values.reshape(4, own_rows)
        me = core * 2 + place_x
        return jnp.concatenate(
            [lax.dynamic_index_in_dim(parts, me ^ k, 0, keepdims=False) for k in range(4)]
        )

    starts = own_first(starts)
    places = own_first(places)
    positions = (places - starts).astype(F32)
    frequency = 1.0 / ROPE_BASE ** (jnp.arange(0, HEAD_WIDTH, 2, dtype=F32) / HEAD_WIDTH)
    angles = positions[:, None] * frequency[None, :]
    cos_part, sin_part = jnp.cos(angles), jnp.sin(angles)
    tables = (
        jnp.concatenate([cos_part, cos_part], axis=1),
        jnp.concatenate([-sin_part, sin_part], axis=1),
        places[:, None],
        places[None, :],
        starts[None, :],
    )
    tables = order.done(tables)

    att_yy = order.done(att_yy)
    att_hi = order.done(att_hi)
    att_hi_lo = [swap(part, "lo") for part in att_hi]
    att_hi_yy = [swap(part, "yy") for part in att_hi]
    n1_x = order.done(n1_x)
    n1_near = jnp.concatenate([n1, n1_x], axis=0)
    n1_far = swap(n1_near, "core")
    order.mark = n1_near
    cot_x = swap(order.after(cotangent), "tensor")
    att_lo_yy = order.done(att_lo_yy)
    ff_yy = swap(order.after(ff_own), "yy")
    att_hi_lo = order.done(att_hi_lo)
    att_hi_lo_yy = [swap(part, "yy") for part in att_hi_lo]
    n1_far = order.done(n1_far)
    att_hi_yy = order.done(att_hi_yy)
    cot_lo = swap(order.after(cotangent), "lo")
    att_hi_lo_yy = order.done(att_hi_lo_yy)

    near_parts = [att_shard, att_lo]
    yy_parts = [att_yy, att_lo_yy]
    for k in range(hi_count - 1):
        near_parts += [att_hi[k], att_hi_lo[k]]
        yy_parts += [att_hi_yy[k], att_hi_lo_yy[k]]
    att_parts = near_parts + yy_parts
    n1_pair = order.after((n1_near, n1_far))
    qkv, attn_rows, lse, *out_parts, att_weight = attention(
        tree_order(-1), n1_pair, bias_local[None], tables, att_parts
    )
    order.mark = lse

    out = FourSum(*out_parts)
    half = own_rows // 2
    ff_yy = order.done(ff_yy)
    ff_lo = order.done(ff_lo)
    ff_lo_yy = swap(ff_lo, "yy")
    ff_hi = order.done(ff_hi)
    ff_lo_hi_gu = [turn(order.after(ff_lo[:2]), "hi", k) for k in steps]
    out.second(order)
    cot_x, cot_lo = order.done((cot_x, cot_lo))
    cot_both = swap(cot_lo[:half], "tensor"), swap(cot_x[half:], "lo")
    ff_lo_yy = order.done(ff_lo_yy)
    ff_hi_yy = [swap(order.after(part), "yy") for part in ff_hi]
    residual = rows_in + out.total(order)
    scale_two = rms_scale(residual)
    n2 = (residual * scale_two * gain_two).astype(BF)
    n2_x, n2_lo = swap(n2, "tensor"), swap(n2, "lo")
    order.mark = n2
    cot_both = order.done(cot_both)
    cot_near = jnp.concatenate([cotangent, cot_x, cot_lo, *cot_both], axis=0)
    order.mark = cot_near
    ff_lo_hi_gu = order.done(ff_lo_hi_gu)
    ff_lo_hi_d = [turn(order.after(ff_lo[2]), "hi", k) for k in steps]
    n2_x, n2_lo = order.done((n2_x, n2_lo))
    n2_both = swap(n2_lo[:half], "tensor"), swap(n2_x[half:], "lo")
    ff_hi_yy = order.done(ff_hi_yy)
    ff_lo_hi_yy_gu = [swap(order.after(part), "yy") for part in ff_lo_hi_gu]
    cot_far = swap(order.after(cot_near), "core")
    n2_both = order.done(n2_both)
    n2_near = jnp.concatenate([n2, n2_x, n2_lo, *n2_both], axis=0)
    n2_far = swap(n2_near, "core")
    order.mark = n2_near
    ff_lo_hi_d = order.done(ff_lo_hi_d)
    ff_lo_hi_yy_d = [swap(part, "yy") for part in ff_lo_hi_d]
    cot_far = order.done(cot_far)
    n2_far = order.done(n2_far)
    ff_lo_hi_yy_gu = order.done(ff_lo_hi_yy_gu)
    ff_lo_hi_yy_d = order.done(ff_lo_hi_yy_d)

    whole = [ff_own, ff_lo, ff_yy, ff_lo_yy, *ff_hi, *ff_hi_yy]
    split = [*zip(ff_lo_hi_gu, ff_lo_hi_d), *zip(ff_lo_hi_yy_gu, ff_lo_hi_yy_d)]
    ff_chips = [chip_at(0, l, y) for y in (0, 1) for l in (0, 1)]
    ff_chips += [chip_at(-k, l, y) for l in (0, 1) for y in (0, 1) for k in steps]
    keep, send, hidden, gate_grad, up_grad, n2_t, cot_t, w_down = feed_forward(
        jnp.stack(ff_chips).astype(jnp.int32),
        order.after((n2_near, n2_far)),
        (cot_near, cot_far),
        whole,
        split,
    )
    order.mark = w_down

    place = jnp.stack([hi, lo, yy]).astype(jnp.int32)

    def grad_parts(left, right, send_now=True):
        keep_own, keep_lo, send_own, send_lo = weight_grad(place, order.after(left), right)
        order.mark = keep_own
        first = GradSum(keep_lo, send_lo) if send_now else (keep_lo, send_lo)
        return first, (keep_own, send_own)

    ff_squares = 0.0
    rows_of = lambda value, which, axis: lax.dynamic_slice_in_dim(
        value, which * shard_rows, shard_rows, axis
    )

    def this_side(lo_sum):
        nonlocal ff_squares
        total = lo_sum.total(order)
        ff_squares = ff_squares + jnp.sum(total * total)
        low = total.astype(BF)
        order.mark = low
        return low, swap(low, "lo")

    def own_rows_of(low, other):
        other = order.done(other)
        cols = jnp.where(
            lo == 0,
            jnp.concatenate([low, other], axis=1),
            jnp.concatenate([other, low], axis=1),
        )
        theirs = rows_of(cols, 1 - core, 0)
        order.mark = theirs
        return rows_of(cols, core, 0), swap(theirs, "core")

    def own_sum(own):
        nonlocal ff_squares
        total = own.total(order)
        ff_squares = ff_squares + jnp.sum(total * total)
        order.mark = total.astype(BF)
        return order.mark

    dn2 = EightSum(keep, send)
    d_lo, d_own = grad_parts(cot_t, hidden)
    d_own = GradSum(*d_own)
    dn2.second(order)
    g_lo, g_own = grad_parts(n2_t, gate_grad)
    dn2.third(order)
    u_lo, u_own = grad_parts(n2_t, up_grad, False)
    d_lo.across(order)
    norm_two_in, gain_two_grad = norm_backward(residual, scale_two, gain_two, dn2.total(order))
    residual_grad = cotangent.astype(F32) + norm_two_in
    da = residual_grad.astype(BF)
    da_x = swap(da, "tensor")
    order.mark = da
    keep, send = down(*order.after((hidden, w_down)))
    order.mark = keep
    da_x = order.done(da_x)
    da_near = jnp.concatenate([da, da_x], axis=0)
    da_far = swap(da_near, "core")
    order.mark = da_near
    d_own.across(order)
    g_own = GradSum(g_own[0], order.after(g_own[1]))
    g_lo.across(order)
    u_lo = GradSum(u_lo[0], order.after(u_lo[1]))
    d_way = this_side(d_lo)[1]
    da_far = order.done(da_far)

    projected_grad, bias_grad, *att_grads = attention_back(
        sum_order(), order.after((da_near, da_far)), n1_pair, qkv, attn_rows, lse, att_weight, tables
    )
    order.mark = bias_grad
    bias_grad = bias_grad[0]
    att = ChipSum(*att_grads)
    d_low = own_sum(d_own)
    g_own.across(order)
    g_way = this_side(g_lo)[1]
    u_lo.across(order)
    dn1_parts = [None] * 4
    for k in (3, 2, 1, 0):
        part = order.after(projected_grad)[k * own_rows : (k + 1) * own_rows]
        dn1_parts[k] = dot_abt(part, att_weight[:, :QKV_COLS]).astype(BF)
        order.mark = dn1_parts[k]
    dn1 = FourSum(*dn1_parts)
    dn1.second(order)
    att.far_yy(order)
    u_own = GradSum(u_own[0], order.after(u_own[1]))
    d_rows = own_rows_of(d_low, d_way)
    g_low = own_sum(g_own)
    att.far_hi(order)
    branch = EightSum(keep, order.after(send))
    norm_one_in, gain_one_grad = norm_backward(rows_in, scale_one, gain_one, dn1.total(order))
    input_grad = residual_grad + norm_one_in
    order.mark = gain_one_grad
    att.near_yy(order)
    u_way = this_side(u_lo)[1]
    branch.second(order)
    u_own.across(order)
    g_rows = own_rows_of(g_low, g_way)
    att_sum = att.total(order)
    att_low = att_sum.astype(BF)
    other_att = swap(rows_of(att_low, 1 - core, 0), "core")
    order.mark = att_low
    branch.third(order)
    u_low = own_sum(u_own)
    other_att = order.done(other_att)

    own_att = rows_of(att_low, core, 0)
    first_att = jnp.where(core == 0, own_att, other_att).astype(F32)
    second_att = jnp.where(core == 0, other_att, own_att).astype(F32)
    kv_sum = first_att[:, Q_COLS:QKV_COLS] + second_att[:, Q_COLS:QKV_COLS]
    qkv_owned = jnp.concatenate([first_att[:, :Q_COLS], second_att[:, :Q_COLS], kv_sum], axis=1)
    out_owned = jnp.concatenate([first_att[:, QKV_COLS:], second_att[:, QKV_COLS:]], axis=1).T
    owned_squares = (
        jnp.sum(qkv_owned * qkv_owned) + jnp.sum(out_owned * out_owned) + ff_squares
    )
    bias_slots = lax.dynamic_update_slice_in_dim(
        jnp.zeros_like(bias_all), bias_grad[:Q_COLS], q_at, 0
    )
    bias_slots = lax.dynamic_update_slice_in_dim(bias_slots, bias_grad[Q_COLS:], kv_at, 0)
    summed = jnp.concatenate(
        [gain_one_grad, gain_two_grad, bias_slots, jnp.full((128,), owned_squares)]
    )
    first = summed + order.done(swap(summed, "core"))
    order.mark = first
    u_rows = own_rows_of(u_low, u_way)
    summed = first + order.done(swap(first, "tensor"))
    summed = summed + order.done(swap(summed, "yy"))
    block_out = (residual + branch.total(order)).astype(BF)
    summed = summed + order.done(swap(summed, "lo"))
    step = 1
    while step < hi_count:
        moved = lax.ppermute(summed, "hi", [(i, i ^ step) for i in range(hi_count)])
        summed = summed + order.done(moved)
        step *= 2

    def owned(rows):
        mine, other = rows
        return both_cores(mine, other, 1)[:, :FF_LOCAL].astype(F32)

    gateup_owned = jnp.stack([owned(g_rows), owned(u_rows)])
    down_owned = owned(d_rows).T
    small_grad = summed[:-128]
    squares = summed[-1] + jnp.sum(small_grad * small_grad)
    grad_norm = jnp.sqrt(squares)
    clip_factor = jnp.minimum(1.0, MAX_NORM / (grad_norm + 1e-06))
    new_small, new_small_first, new_small_second = adam_update(
        small_params, small_first, small_second, clip_factor * small_grad, 0.5, 0.0
    )
    new_qkv, new_qkv_first, new_qkv_second = adam_update(
        qkv_weight, qkv_first, qkv_second, clip_factor * qkv_owned, 2.0 / math.sqrt(D), WEIGHT_DECAY
    )
    new_out, new_out_first, new_out_second = adam_update(
        out_weight,
        out_first,
        out_second,
        clip_factor * out_owned,
        8.0 / math.sqrt(QUERY_HEADS * HEAD_WIDTH),
        WEIGHT_DECAY,
    )
    new_gateup, new_gateup_first, new_gateup_second = adam_update(
        gateup_weight,
        gateup_first,
        gateup_second,
        clip_factor * gateup_owned,
        2.0 / math.sqrt(D),
        WEIGHT_DECAY,
    )
    new_down, new_down_first, new_down_second = adam_update(
        down_weight,
        down_first,
        down_second,
        clip_factor * down_owned,
        3.0 / math.sqrt(FF),
        WEIGHT_DECAY,
    )
    return (
        block_out,
        input_grad,
        grad_norm,
        new_small,
        new_small_first,
        new_small_second,
        new_qkv,
        new_qkv_first,
        new_qkv_second,
        new_out,
        new_out_first,
        new_out_second,
        new_gateup,
        new_gateup_first,
        new_gateup_second,
        new_down,
        new_down_first,
        new_down_second,
    )


def solution(mesh):
    count = mesh.shape["dp"]
    fine = Mesh(
        mesh.devices.reshape(count // 8, 2, 2, 2, mesh.shape["tensor"]),
        CHIP + ("core", "tensor"),
    )
    dp = CHIP + ("core",)
    rows = P(dp + ("tensor",), None)
    by_rows = P(dp, "tensor")
    by_cols = P("tensor", dp)
    stacked = P(None, dp, "tensor")
    weights = (by_rows,) * 3 + (by_cols,) * 3 + (stacked,) * 3 + (by_cols,) * 3
    return jax.shard_map(
        body,
        mesh=fine,
        in_specs=(rows, rows, P(dp), P(), P(), P()) + weights,
        out_specs=(rows, rows, P(), P(), P(), P()) + weights,
        check_vma=False,
    )
```

time: 1770 us -> 652 us (0.37)
  waiting for transfers between devices: 1390 us -> 271 us
  matrix products: 184 us -> 5.22 us
  Pallas kernels: 0 us -> 155 us
  starting transfers between devices: 8.04 us -> 75.2 us
  blocking collectives: 40 us -> 0 us
    reduce_scatter x8 -> x0, waiting for transfers between devices: 995 us -> none  [the longest x1 507 us: body(): lax.psum_scatter(gateup_grad, 'dp', scatter_dimension=1, tiled=True)]
    all_gather x8 -> x0, waiting for transfers between devices: 398 us -> none  [the longest x1 142 us: body(): lax.all_gather(gateup_weight.astype(jnp.bfloat16), 'dp', axis=1, tiled=True)]
    ppermute x3 -> x78, waiting for transfers between devices: 0.01 us -> 271 us  [the longest x66 230 us: swap(): return lax.ppermute(value, axis, [(0, 1), (1, 0)])]
    dot_general x21 -> x4, matrix products: 184 us -> 5.22 us  [dot_abt(): lax.dot_general(a, b, (((1,), (1,)), ((), ())), preferred_element_type=F32)]
    pallas_call x0 -> x7, Pallas kernels: none -> 155 us  [the longest x1 52.3 us: feed_forward(): pl.pallas_call(functools.partial(feed_forward_kernel, len(whole), len(spl...]
    ppermute x3 -> x78, starting transfers between devices: 6.46 us -> 75.2 us  [the longest x66 44.6 us: swap(): return lax.ppermute(value, axis, [(0, 1), (1, 0)])]
    psum x1 -> x0, blocking collectives: 40 us -> none  [body(): lax.psum(owned_squares, ('dp', 'tensor')) + jnp.sum(small_grad * small_grad)]
    another operation x8, other arithmetic: 45.6 us -> 9.61 us  [the longest x1 38.7 us: body(): jnp.stack([contract_rows(gathered_two, gate_grad), contract_rows(gathered...]
  transfers between devices with their start and end apart: 19 -> 78, of which waited for: 15 -> 34; matrix products, arithmetic and copies ran while one was open for 10% -> 18% of each run, Pallas kernels for 0% -> 16%
where the time goes in v1:
time: 652 us; the launch traced here: 647 us
  waiting for transfers between devices  271 us (42%)
  Pallas kernels  155 us (24%)
  other arithmetic  102 us (16%)
  starting transfers between devices  75.2 us (12%)
  local copies, waits for them, and re-layouts  28.1 us (4%)
  between operations  9.94 us (2%)
    ppermute x66, waiting for transfers between devices, swap(): return lax.ppermute(value, axis, [(0, 1), (1, 0)])  230 us
    pallas_call x1, Pallas kernels, feed_forward(): pl.pallas_call(functools.partial(feed_forward_kernel, len(whole), len(spl...  52.3 us
    ppermute x66, starting transfers between devices, swap(): return lax.ppermute(value, axis, [(0, 1), (1, 0)])  44.6 us
    pallas_call x3, Pallas kernels, weight_grad(): pl.pallas_call(functools.partial(weight_grad_kernel, rows), grid_spec=plt...  42.1 us
    ppermute x11, waiting for transfers between devices, turn(): lax.ppermute(value, axis, [(i, (i + steps) % count) for i in range(count)])  40.9 us
    ppermute x11, starting transfers between devices, turn(): lax.ppermute(value, axis, [(i, (i + steps) % count) for i in range(count)])  28.8 us
    pallas_call x1, Pallas kernels, attention_back(): pl.pallas_call(functools.partial(attention_back_kernel, count, rows), gri...  23.9 us
    pallas_call x1, Pallas kernels, attention(): pl.pallas_call(functools.partial(attention_kernel, parts, rows), grid_spe...  22.4 us
  transfers between devices with their start and end apart: 78, of which 34 were waited for; matrix products, arithmetic and copies ran while one was open for 18% of the time, Pallas kernels for 16%

profile of v1, /device:TPU:0, one launch (start us, length us, event | category | flops | bytes accessed | tf_op | source)
XLA Modules:
  0.0 646.6 jit_solution(15065862266389727960)
XLA Ops:
  28.8 9.7 %collective-permute-done.5.refs_1_ = bf16[192,1024]{1,0:T(8,128)(2,1)S(1)} collective-permute-done((bf16[192,1024]{1,0:T(8,128)(2,1)S(1)}, bf16[192,1024]{1,0:T(8,128)(2,1)S(1)}, u32[]{:S(2)}, u32[]{:S(2)}) %collective-permute-start.5) | collective-permute-done | bytes 393248 | tf_op jit(solution)/shard_map/ppermute | solution.py:81
  42.5 9.9 %collective-permute-done.9.refs_5_ = bf16[192,1024]{1,0:T(8,128)(2,1)S(1)} collective-permute-done((bf16[192,1024]{1,0:T(8,128)(2,1)S(1)}, bf16[192,1024]{1,0:T(8,128)(2,1)S(1)}, u32[]{:S(2)}, u32[]{:S(2)}) %collective-permute-start.9) | collective-permute-done | bytes 393248 | tf_op jit(solution)/shard_map/ppermute | solution.py:81
  64.4 28.9 %collective-permute-done.11.refs_6_ = bf16[192,1024]{1,0:T(8,128)(2,1)} collective-permute-done((bf16[192,1024]{1,0:T(8,128)(2,1)S(1)}, bf16[192,1024]{1,0:T(8,128)(2,1)}, u32[]{:S(2)}, u32[]{:S(2)}) %collective-permute-start.11) | collective-permute-done | bytes 393248 | tf_op jit(solution)/shard_map/ppermute | solution.py:81
  93.3 7.2 %collective-permute-done.10.refs_7_ = bf16[192,1024]{1,0:T(8,128)(2,1)} collective-permute-done((bf16[192,1024]{1,0:T(8,128)(2,1)}, bf16[192,1024]{1,0:T(8,128)(2,1)}, u32[]{:S(2)}, u32[]{:S(2)}) %collective-permute-start.10) | collective-permute-done | bytes 393248 | tf_op jit(solution)/shard_map/ppermute | solution.py:81
  100.5 22.4 %attention.1 = (bf16[1024,640]{1,0:T(8,128)(2,1)}, bf16[1024,384]{1,0:T(8,128)(2,1)}, f32[8,1024]{1,0:T(8,128)}, bf16[256,1536]{1,0:T(8,128)(2,1)}, bf16[256,153...) custom-call(s32[8]{0:T(128)} %stack.91.chips_ref, ...), custom_call_target="tpu_custom_call" | custom-call | flops 1179648 | bytes 4096 | tf_op jit(solution)/shard_map/attention/pallas_call | solution.py:242
  134.4 10.6 %collective-permute-done.19 = bf16[256,1536]{1,0:T(8,128)(2,1)S(1)} collective-permute-done((bf16[256,1536]{1,0:T(8,128)(2,1)S(1)}, bf16[256,1536]{1,0:T(8,128)(2,1)S(1)}, u32[]{:S(2)}, u32[]{:S(2)}) %collective-permute-start.19) | collective-permute-done | bytes 786464 | tf_op jit(solution)/shard_map/ppermute | solution.py:81
  144.9 10.2 %collective-permute-done.20 = bf16[256,1536]{1,0:T(8,128)(2,1)S(1)} collective-permute-done((bf16[256,1536]{1,0:T(8,128)(2,1)S(1)}, bf16[256,1536]{1,0:T(8,128)(2,1)S(1)}, u32[]{:S(2)}, u32[]{:S(2)}) %collective-permute-start.20) | collective-permute-done | bytes 786464 | tf_op jit(solution)/shard_map/ppermute | solution.py:81
  194.8 6.9 %collective-permute-done.26 = bf16[128,1536]{1,0:T(8,128)(2,1)S(1)} collective-permute-done((bf16[128,1536]{1,0:T(8,128)(2,1)S(1)}, bf16[128,1536]{1,0:T(8,128)(2,1)S(1)}, u32[]{:S(2)}, u32[]{:S(2)}) %collective-permute-start.26) | collective-permute-done | bytes 393248 | tf_op jit(solution)/shard_map/ppermute | solution.py:81
  207.5 20.4 %collective-permute-done.31.refs_12_ = bf16[192,1152]{1,0:T(8,128)(2,1)} collective-permute-done((bf16[192,1152]{1,0:T(8,128)(2,1)S(1)}, bf16[192,1152]{1,0:T(8,128)(2,1)}, u32[]{:S(2)}, u32[]{:S(2)}) %collective-permute-start.31) | collective-permute-done | bytes 442400 | tf_op jit(solution)/shard_map/ppermute | solution.py:107
  230.1 9.7 %collective-permute-done.32.refs_13_ = bf16[192,1152]{1,0:T(8,128)(2,1)} collective-permute-done((bf16[192,1152]{1,0:T(8,128)(2,1)}, bf16[192,1152]{1,0:T(8,128)(2,1)}, u32[]{:S(2)}, u32[]{:S(2)}) %collective-permute-start.32) | collective-permute-done | bytes 442400 | tf_op jit(solution)/shard_map/ppermute | solution.py:81
  239.8 52.3 %feed_forward.1 = (bf16[1024,1536]{1,0:T(8,128)(2,1)}, bf16[1024,1536]{1,0:T(8,128)(2,1)}, bf16[2048,1152]{1,0:T(8,128)(2,1)}, bf16[2048,1152]{1,0:T(8,128)(2,1)...) custom-call(s32[8]{0:T(128)} %stack.92.chips_ref, ...), custom_call_target="tpu_custom_call" | custom-call | flops 8847360 | bytes 15360 | tf_op jit(solution)/shard_map/feed_forward/pallas_call | solution.py:456
  292.8 14.3 %weight_grad.3 = (bf16[2,192,1152]{2,1,0:T(8,128)(2,1)}, bf16[2,192,1152]{2,1,0:T(8,128)(2,1)}, bf16[2,192,1152]{2,1,0:T(8,128)(2,1)}, bf16[2,192,1152]{2,1,0:T(8,128)(2,1)}) custom-call(s32[3]{0:T(128)} %pad_add_fusion.2.place_ref, bf16[1536,2048]{1,0:T(8,128)(2,1)} %get-tuple-element.228.left_ref, bf16[2048,1152]{1,0:T(8,128)(2,1)} %get-tuple-element.244.right_ref.left_ref), custom_call_target="tpu_custom_call" | custom-call | flops 1769472 | bytes 4096 | tf_op jit(solution)/shard_map/weight_grad/pallas_call | solution.py:507
  313.4 13.9 %weight_grad.4 = (bf16[2,192,1152]{2,1,0:T(8,128)(2,1)}, bf16[2,192,1152]{2,1,0:T(8,128)(2,1)}, bf16[2,192,1152]{2,1,0:T(8,128)(2,1)}, bf16[2,192,1152]{2,1,0:T(8,128)(2,1)}) custom-call(s32[3]{0:T(128)} %pad_add_fusion.2.place_ref, bf16[1536,2048]{1,0:T(8,128)(2,1)} %get-tuple-element.238.left_ref, bf16[2048,1152]{1,0:T(8,128)(2,1)} %get-tuple-element.233.right_ref), custom_call_target="tpu_custom_call" | custom-call | flops 1769472 | bytes 4096 | tf_op jit(solution)/shard_map/weight_grad/pallas_call | solution.py:507
  333.2 13.9 %weight_grad.5 = (bf16[2,192,1152]{2,1,0:T(8,128)(2,1)}, bf16[2,192,1152]{2,1,0:T(8,128)(2,1)}, bf16[2,192,1152]{2,1,0:T(8,128)(2,1)}, bf16[2,192,1152]{2,1,0:T(8,128)(2,1)}) custom-call(s32[3]{0:T(128)} %pad_add_fusion.2.place_ref, bf16[1536,2048]{1,0:T(8,128)(2,1)} %get-tuple-element.238.left_ref, bf16[2048,1152]{1,0:T(8,128)(2,1)} %get-tuple-element.239.right_ref), custom_call_target="tpu_custom_call" | custom-call | flops 1769472 | bytes 4096 | tf_op jit(solution)/shard_map/weight_grad/pallas_call | solution.py:507
  360.3 14.1 %down.1 = (bf16[1024,1536]{1,0:T(8,128)(2,1)}, bf16[1024,1536]{1,0:T(8,128)(2,1)}) custom-call(bf16[2048,1152]{1,0:T(8,128)(2,1)} %get-tuple-element.244.right_ref.left_ref, bf16[1536,1152]{1,0:T(8,128)(2,1)} %get-tuple-element.245.right_ref), custom_call_target="tpu_custom_call" | custom-call | flops 1769472 | bytes 3584 | tf_op jit(solution)/shard_map/down/pallas_call | solution.py:544
  380.5 16.1 %collective-permute-done.43 = bf16[2,192,1152]{2,1,0:T(8,128)(2,1)} collective-permute-done((bf16[2,192,1152]{2,1,0:T(8,128)(2,1)}, bf16[2,192,1152]{2,1,0:T(8,128)(2,1)}, u32[]{:S(2)}, u32[]{:S(2)}) %collective-permute-start.43) | collective-permute-done | bytes 884768 | tf_op jit(solution)/shard_map/ppermute | solution.py:81
  409.2 23.9 %attention_back.1 = (bf16[1024,640]{1,0:T(8,128)(2,1)}, f32[1,640]{1,0:T(1,128)}, bf16[2,192,1024]{2,1,0:T(8,128)(2,1)}, bf16[2,192,1024]{2,1,0:T(8,128)(2,1)}, ...) custom-call(s32[8]{0:T(128)} %stack.101.chips_ref, bf16[512,1536]{1,0:T(8,128)(2,1)} %copy-done.7, ...), custom_call_target="tpu_custom_call" | custom-call | flops 2555904 | bytes 6144 | tf_op jit(solution)/shard_map/attention_back/pallas_call | solution.py:349
  454.4 21.6 %collective-permute-done.45 = bf16[2,192,1024]{2,1,0:T(8,128)(2,1)S(1)} collective-permute-done((bf16[2,192,1024]{2,1,0:T(8,128)(2,1)S(1)}, bf16[2,192,1024]{2,1,0:T(8,128)(2,1)S(1)}, u32[]{:S(2)}, u32[]{:S(2)}) %collective-permute-start.45) | collective-permute-done | bytes 786464 | tf_op jit(solution)/shard_map/ppermute | solution.py:81
  496.9 11.0 %collective-permute-done.58 = bf16[256,1536]{1,0:T(8,128)(2,1)} collective-permute-done((bf16[256,1536]{1,0:T(8,128)(2,1)}, bf16[256,1536]{1,0:T(8,128)(2,1)}, u32[]{:S(2)}, u32[]{:S(2)}) %collective-permute-start.58) | collective-permute-done | bytes 786464 | tf_op jit(solution)/shard_map/ppermute | solution.py:81
  510.8 16.1 %collective-permute-done.57 = bf16[2,192,1024]{2,1,0:T(8,128)(2,1)} collective-permute-done((bf16[2,192,1024]{2,1,0:T(8,128)(2,1)}, bf16[2,192,1024]{2,1,0:T(8,128)(2,1)}, u32[]{:S(2)}, u32[]{:S(2)}) %collective-permute-start.57) | collective-permute-done | bytes 786464 | tf_op jit(solution)/shard_map/ppermute | solution.py:81
  537.5 12.3 %collective-permute-done.64 = bf16[2,192,1152]{2,1,0:T(8,128)(2,1)} collective-permute-done((bf16[2,192,1152]{2,1,0:T(8,128)(2,1)}, bf16[2,192,1152]{2,1,0:T(8,128)(2,1)}, u32[]{:S(2)}, u32[]{:S(2)}) %collective-permute-start.64) | collective-permute-done | bytes 884768 | tf_op jit(solution)/shard_map/ppermute | solution.py:81
  560.1 7.5 %collective-permute-done.60 = bf16[128,1536]{1,0:T(8,128)(2,1)S(1)} collective-permute-done((bf16[128,1536]{1,0:T(8,128)(2,1)S(1)}, bf16[128,1536]{1,0:T(8,128)(2,1)S(1)}, u32[]{:S(2)}, u32[]{:S(2)}) %collective-permute-start.60) | collective-permute-done | bytes 393248 | tf_op jit(solution)/shard_map/ppermute | solution.py:81
  574.0 15.9 %collective-permute-done.68 = bf16[192,1152]{1,0:T(8,128)(2,1)S(1)} collective-permute-done((bf16[192,1152]{1,0:T(8,128)(2,1)S(1)}, bf16[192,1152]{1,0:T(8,128)(2,1)S(1)}, u32[]{:S(2)}, u32[]{:S(2)}) %collective-permute-start.68) | collective-permute-done | bytes 442400 | tf_op jit(solution)/shard_map/ppermute | solution.py:107
  630.9 7.9 %divide_subtract_fusion = (f32[2,96,4480]{2,1,0:T(8,128)}, f32[2,96,4480]{2,1,0:T(8,128)}, f32[2,96,4480]{2,1,0:T(8,128)}) fusion(f32[2,96,4480]{2,1,0:T(8,128)} %param.30, bf16[1,96,4480]{2,1,0:T(8,128)(2,1)S(1)} %copy-done.12, bf16[1,96,4480]{2,1,0:T(8,128)(2,1)S(1)} %copy-done.11, f32[]{:T(128)S(6)} %min.3, f32[2,96,4480]{2,1,0:T(8,128)} %param.31, ...), kind=kLoop, calls=%fused_computation.5 | loop fusion | flops 13762560 | bytes 22364164 | tf_op jit(solution)/shard_map/sub | solution.py:74
  (427 shorter events, 260.1 us)
Async XLA Ops:
  4.8 34.5 %collective-permute-start = (bf16[256,1536]{1,0:T(8,128)(2,1)}, bf16[256,1536]{1,0:T(8,128)(2,1)}, u32[]{:S(2)}, u32[]{:S(2)}) collective-permute-start(bf16[256,1536]{1,0:T(8,128)(2,1)} %fusion.10), channel_id=1, source_target_pairs={{0,1},{1,0},{2,3},{3,2},{4,5},{5,4},{6,7},{7,6},{8,9},{9,8},{10,11... | collective-permute-start | bytes 2359304 | tf_op jit(solution)/shard_map/ppermute | solution.py:81
  52.5 70.4 %collective-permute-start.16 = (bf16[3,192,1152]{2,1,0:T(8,128)(2,1)}, bf16[3,192,1152]{2,1,0:T(8,128)(2,1)}, u32[]{:S(2)}, u32[]{:S(2)}) collective-permute-start(bf16[3,192,1152]{2,1,0:T(8,128)(2,1)} %get-tuple-element.190.refs_4_), channel_id=1, source_target_pairs={{0,4},{4,0},{1,5},{5,1},{2,6},{6,2},{3,7},{7,3},{8,12},{12,8},{9,1... | collective-permute-start | bytes 3981320 | tf_op jit(solution)/shard_map/ppermute | solution.py:81
  54.0 68.9 %collective-permute-start.15 = (bf16[3,192,1152]{2,1,0:T(8,128)(2,1)}, bf16[3,192,1152]{2,1,0:T(8,128)(2,1)}, u32[]{:S(2)}, u32[]{:S(2)}) collective-permute-start(bf16[3,192,1152]{2,1,0:T(8,128)(2,1)} %get-tuple-element.347), channel_id=1, source_target_pairs={{0,8},{8,0},{1,9},{9,1},{2,10},{10,2},{3,11},{11,3},{4,12},{12,4},... | collective-permute-start | bytes 3981320 | tf_op jit(solution)/shard_map/ppermute | solution.py:81
  54.0 71.1 %collective-permute-start.14 = (bf16[3,192,1152]{2,1,0:T(8,128)(2,1)}, bf16[3,192,1152]{2,1,0:T(8,128)(2,1)}, u32[]{:S(2)}, u32[]{:S(2)}) collective-permute-start(bf16[3,192,1152]{2,1,0:T(8,128)(2,1)} %get-tuple-element.190.refs_4_), channel_id=1, source_target_pairs={{0,16},{16,0},{1,17},{17,1},{2,18},{18,2},{3,19},{19,3},{4,20},{20... | collective-permute-start | bytes 3981320 | tf_op jit(solution)/shard_map/ppermute | solution.py:107
  58.1 35.2 %collective-permute-start.11 = (bf16[192,1024]{1,0:T(8,128)(2,1)S(1)}, bf16[192,1024]{1,0:T(8,128)(2,1)}, u32[]{:S(2)}, u32[]{:S(2)}) collective-permute-start(bf16[192,1024]{1,0:T(8,128)(2,1)S(1)} %copy-done.51), channel_id=1, source_target_pairs={{0,4},{4,0},{1,5},{5,1},{2,6},{6,2},{3,7},{7,3},{8,12},{12,8},{9,1... | collective-permute-start | bytes 1179656 | tf_op jit(solution)/shard_map/ppermute | solution.py:81
  59.7 40.7 %collective-permute-start.10 = (bf16[192,1024]{1,0:T(8,128)(2,1)}, bf16[192,1024]{1,0:T(8,128)(2,1)}, u32[]{:S(2)}, u32[]{:S(2)}) collective-permute-start(bf16[192,1024]{1,0:T(8,128)(2,1)} %collective-permute-done.8.refs_3_), channel_id=1, source_target_pairs={{0,4},{4,0},{1,5},{5,1},{2,6},{6,2},{3,7},{7,3},{8,12},{12,8},{9,1... | collective-permute-start | bytes 1179656 | tf_op jit(solution)/shard_map/ppermute | solution.py:81
  122.9 34.8 %collective-permute-start.18 = (bf16[3,192,1152]{2,1,0:T(8,128)(2,1)}, bf16[3,192,1152]{2,1,0:T(8,128)(2,1)S(1)}, u32[]{:S(2)}, u32[]{:S(2)}) collective-permute-start(bf16[3,192,1152]{2,1,0:T(8,128)(2,1)} %collective-permute-done.15.refs_5_), channel_id=1, source_target_pairs={{0,4},{4,0},{1,5},{5,1},{2,6},{6,2},{3,7},{7,3},{8,12},{12,8},{9,1... | collective-permute-start | bytes 3981320 | tf_op jit(solution)/shard_map/ppermute | solution.py:81
  126.8 35.0 %collective-permute-start.17 = (bf16[256,1536]{1,0:T(8,128)(2,1)S(1)}, bf16[256,1536]{1,0:T(8,128)(2,1)S(1)}, u32[]{:S(2)}, u32[]{:S(2)}) collective-permute-start(bf16[256,1536]{1,0:T(8,128)(2,1)S(1)} %add_convert_fusion.2), channel_id=1, source_target_pairs={{0,1},{1,0},{2,3},{3,2},{4,5},{5,4},{6,7},{7,6},{8,9},{9,8},{10,11... | collective-permute-start | bytes 2359304 | tf_op jit(solution)/shard_map/ppermute | solution.py:81
  130.3 49.3 %collective-permute-start.23 = (bf16[2,192,1152]{2,1,0:T(8,128)(2,1)S(1)}, bf16[2,192,1152]{2,1,0:T(8,128)(2,1)}, u32[]{:S(2)}, u32[]{:S(2)}) collective-permute-start(bf16[2,192,1152]{2,1,0:T(8,128)(2,1)S(1)} %slice.287), channel_id=1, source_target_pairs={{0,16},{16,0},{1,17},{17,1},{2,18},{18,2},{3,19},{19,3},{4,20},{20... | collective-permute-start | bytes 2654216 | tf_op jit(solution)/shard_map/ppermute | solution.py:107
  157.8 37.0 %collective-permute-start.28 = (bf16[3,192,1152]{2,1,0:T(8,128)(2,1)}, bf16[3,192,1152]{2,1,0:T(8,128)(2,1)}, u32[]{:S(2)}, u32[]{:S(2)}) collective-permute-start(bf16[3,192,1152]{2,1,0:T(8,128)(2,1)} %collective-permute-done.14.refs_8_), channel_id=1, source_target_pairs={{0,4},{4,0},{1,5},{5,1},{2,6},{6,2},{3,7},{7,3},{8,12},{12,8},{9,1... | collective-permute-start | bytes 3981320 | tf_op jit(solution)/shard_map/ppermute | solution.py:81
  311.7 35.5 %collective-permute-start.39 = (bf16[2,192,1152]{2,1,0:T(8,128)(2,1)}, bf16[2,192,1152]{2,1,0:T(8,128)(2,1)S(1)}, u32[]{:S(2)}, u32[]{:S(2)}) collective-permute-start(bf16[2,192,1152]{2,1,0:T(8,128)(2,1)} %get-tuple-element.237), channel_id=1, source_target_pairs={{0,4},{4,0},{1,5},{5,1},{2,6},{6,2},{3,7},{7,3},{8,12},{12,8},{9,1... | collective-permute-start | bytes 2654216 | tf_op jit(solution)/shard_map/ppermute | solution.py:81
  357.9 38.7 %collective-permute-start.43 = (bf16[2,192,1152]{2,1,0:T(8,128)(2,1)}, bf16[2,192,1152]{2,1,0:T(8,128)(2,1)}, u32[]{:S(2)}, u32[]{:S(2)}) collective-permute-start(bf16[2,192,1152]{2,1,0:T(8,128)(2,1)} %get-tuple-element.250), channel_id=1, source_target_pairs={{0,4},{4,0},{1,5},{5,1},{2,6},{6,2},{3,7},{7,3},{8,12},{12,8},{9,1... | collective-permute-start | bytes 2654216 | tf_op jit(solution)/shard_map/ppermute | solution.py:81
  396.6 46.0 %collective-permute-start.46 = (bf16[2,192,1152]{2,1,0:T(8,128)(2,1)}, bf16[2,192,1152]{2,1,0:T(8,128)(2,1)}, u32[]{:S(2)}, u32[]{:S(2)}) collective-permute-start(bf16[2,192,1152]{2,1,0:T(8,128)(2,1)} %get-tuple-element.265), channel_id=1, source_target_pairs={{0,4},{4,0},{1,5},{5,1},{2,6},{6,2},{3,7},{7,3},{8,12},{12,8},{9,1... | collective-permute-start | bytes 2654216 | tf_op jit(solution)/shard_map/ppermute | solution.py:81
  396.9 38.3 %collective-permute-start.48 = (bf16[2,192,1152]{2,1,0:T(8,128)(2,1)}, bf16[2,192,1152]{2,1,0:T(8,128)(2,1)}, u32[]{:S(2)}, u32[]{:S(2)}) collective-permute-start(bf16[2,192,1152]{2,1,0:T(8,128)(2,1)} %get-tuple-element.268), channel_id=1, source_target_pairs={{0,4},{4,0},{1,5},{5,1},{2,6},{6,2},{3,7},{7,3},{8,12},{12,8},{9,1... | collective-permute-start | bytes 2654216 | tf_op jit(solution)/shard_map/ppermute | solution.py:81
  405.8 33.9 %collective-permute-start.47 = (bf16[192,1152]{1,0:T(8,128)(2,1)}, bf16[192,1152]{1,0:T(8,128)(2,1)}, u32[]{:S(2)}, u32[]{:S(2)}) collective-permute-start(bf16[192,1152]{1,0:T(8,128)(2,1)} %fusion.37), channel_id=1, source_target_pairs={{0,16},{16,0},{1,17},{17,1},{2,18},{18,2},{3,19},{19,3},{4,20},{20... | collective-permute-start | bytes 1327112 | tf_op jit(solution)/shard_map/ppermute | solution.py:107
  408.6 68.1 %collective-permute-start.54 = (bf16[192,1152]{1,0:T(8,128)(2,1)}, bf16[192,1152]{1,0:T(8,128)(2,1)}, u32[]{:S(2)}, u32[]{:S(2)}) collective-permute-start(bf16[192,1152]{1,0:T(8,128)(2,1)} %get-tuple-element.361), channel_id=1, source_target_pairs={{0,8},{8,0},{1,9},{9,1},{2,10},{10,2},{3,11},{11,3},{4,12},{12,4},... | collective-permute-start | bytes 1327112 | tf_op jit(solution)/shard_map/ppermute | solution.py:81
  487.6 48.3 %collective-permute-start.55 = (bf16[1024,1536]{1,0:T(8,128)(2,1)}, bf16[1024,1536]{1,0:T(8,128)(2,1)}, u32[]{:S(2)}, u32[]{:S(2)}) collective-permute-start(bf16[1024,1536]{1,0:T(8,128)(2,1)} %get-tuple-element.284), channel_id=1, source_target_pairs={{0,2},{2,0},{1,3},{3,1},{4,6},{6,4},{5,7},{7,5},{8,10},{10,8},{9,1... | collective-permute-start | bytes 9437192 | tf_op jit(solution)/shard_map/ppermute | solution.py:81
  487.9 63.4 %collective-permute-start.63 = (bf16[192,1152]{1,0:T(8,128)(2,1)}, bf16[192,1152]{1,0:T(8,128)(2,1)}, u32[]{:S(2)}, u32[]{:S(2)}) collective-permute-start(bf16[192,1152]{1,0:T(8,128)(2,1)} %get-tuple-element.357), channel_id=1, source_target_pairs={{0,8},{8,0},{1,9},{9,1},{2,10},{10,2},{3,11},{11,3},{4,12},{12,4},... | collective-permute-start | bytes 1327112 | tf_op jit(solution)/shard_map/ppermute | solution.py:81
  487.9 38.9 %collective-permute-start.57 = (bf16[2,192,1024]{2,1,0:T(8,128)(2,1)}, bf16[2,192,1024]{2,1,0:T(8,128)(2,1)}, u32[]{:S(2)}, u32[]{:S(2)}) collective-permute-start(bf16[2,192,1024]{2,1,0:T(8,128)(2,1)} %get-tuple-element.287), channel_id=1, source_target_pairs={{0,8},{8,0},{1,9},{9,1},{2,10},{10,2},{3,11},{11,3},{4,12},{12,4},... | collective-permute-start | bytes 2359304 | tf_op jit(solution)/shard_map/ppermute | solution.py:81
  491.8 38.1 %collective-permute-start.56 = (bf16[192,1152]{1,0:T(8,128)(2,1)}, bf16[192,1152]{1,0:T(8,128)(2,1)}, u32[]{:S(2)}, u32[]{:S(2)}) collective-permute-start(bf16[192,1152]{1,0:T(8,128)(2,1)} %fusion.40), channel_id=1, source_target_pairs={{0,16},{16,0},{1,17},{17,1},{2,18},{18,2},{3,19},{19,3},{4,20},{20... | collective-permute-start | bytes 1327112 | tf_op jit(solution)/shard_map/ppermute | solution.py:107
  507.8 132.9 %collective-permute-start.77 = (bf16[96,2304]{1,0:T(8,128)(2,1)}, bf16[96,2304]{1,0:T(8,128)(2,1)}, u32[]{:S(2)}, u32[]{:S(2)}) collective-permute-start(bf16[96,2304]{1,0:T(8,128)(2,1)} %get-tuple-element.365), channel_id=1, source_target_pairs={{0,2},{2,0},{1,3},{3,1},{4,6},{6,4},{5,7},{7,5},{8,10},{10,8},{9,1... | collective-permute-start | bytes 1327112 | tf_op jit(solution)/shard_map/ppermute | solution.py:81
  549.8 50.2 %collective-permute-start.71 = (bf16[192,1152]{1,0:T(8,128)(2,1)}, bf16[192,1152]{1,0:T(8,128)(2,1)}, u32[]{:S(2)}, u32[]{:S(2)}) collective-permute-start(bf16[192,1152]{1,0:T(8,128)(2,1)} %get-tuple-element.353), channel_id=1, source_target_pairs={{0,8},{8,0},{1,9},{9,1},{2,10},{10,2},{3,11},{11,3},{4,12},{12,4},... | collective-permute-start | bytes 1327112 | tf_op jit(solution)/shard_map/ppermute | solution.py:81
  555.4 54.2 %collective-permute-start.75 = (bf16[96,2304]{1,0:T(8,128)(2,1)}, bf16[96,2304]{1,0:T(8,128)(2,1)}, u32[]{:S(2)}, u32[]{:S(2)}) collective-permute-start(bf16[96,2304]{1,0:T(8,128)(2,1)} %get-tuple-element.367), channel_id=1, source_target_pairs={{0,2},{2,0},{1,3},{3,1},{4,6},{6,4},{5,7},{7,5},{8,10},{10,8},{9,1... | collective-permute-start | bytes 1327112 | tf_op jit(solution)/shard_map/ppermute | solution.py:81
  559.9 33.1 %collective-permute-start.67 = (bf16[96,1024]{1,0:T(8,128)(2,1)S(1)}, bf16[96,1024]{1,0:T(8,128)(2,1)S(1)}, u32[]{:S(2)}, u32[]{:S(2)}) collective-permute-start(bf16[96,1024]{1,0:T(8,128)(2,1)S(1)} %constant_dynamic-slice_fusion.4), channel_id=1, source_target_pairs={{0,2},{2,0},{1,3},{3,1},{4,6},{6,4},{5,7},{7,5},{8,10},{10,8},{9,1... | collective-permute-start | bytes 589832 | tf_op jit(solution)/shard_map/ppermute | solution.py:81
  (129 other events, 1918.9 us)

commit v2 on v1

--- a/solution.py
+++ b/solution.py
@@ -3,6 +3,7 @@
 
 import jax
 import jax.numpy as jnp
+import numpy as np
 from jax import lax
 from jax.experimental import pallas as pl
 from jax.experimental.pallas import tpu as pltpu
@@ -107,6 +108,15 @@
     return lax.ppermute(value, axis, [(i, (i + steps) % count) for i in range(count)])
 
 
+def others_of(every):
+    count = lax.axis_size("hi")
+    hi = lax.axis_index("hi")
+    return [
+        lax.dynamic_index_in_dim(every, (hi - k) % count, 0, keepdims=False)
+        for k in range(1, count)
+    ]
+
+
 def tree_order(sign):
     steps = [(0, 0), (0, 1)] + [(k, l) for k in range(1, lax.axis_size("hi")) for l in (0, 1)]
     return jnp.stack([chip_at(sign * k, l, y) for y in (0, 1) for k, l in steps]).astype(jnp.int32)
@@ -120,14 +130,15 @@
 
 class ChipSum:
     def __init__(self, lo_far, lo_near, far, near):
-        self.far, self.near = far, near
-        self.lo_far, self.lo_near = swap(lo_far, "lo"), swap(lo_near, "lo")
+        self.far, self.near, self.lo_near = far, near, lo_near
+        self.lo_far = swap(lo_far, "lo")
 
     def far_yy(self, order):
         self.far = self.far.astype(F32) + order.done(self.lo_far).astype(F32)
         theirs = self.far[0::2].astype(BF)
         self.yy_far = swap(theirs, "yy")
         order.mark = theirs
+        self.lo_near = swap(order.after(self.lo_near), "lo")
 
     def far_hi(self, order):
         far = (self.far[1::2] + order.done(self.yy_far).astype(F32)).astype(BF)
@@ -170,23 +181,19 @@
     return jnp.where((key_place <= place) & (key_place >= start), scores, NEGATIVE)
 
 
-def attention_kernel(
-    parts,
-    rows,
-    chips_ref,
-    near_ref,
-    far_ref,
-    bias_ref,
-    cos_ref,
-    sin_ref,
-    key_place_ref,
-    place_ref,
-    start_ref,
-    *refs,
-):
+def rows_from(refs):
+    begin = 0
+    for ref in refs:
+        yield slice(begin, begin + ref.shape[0]), ref
+        begin += ref.shape[0]
+
+
+def attention_kernel(blocks, parts, rows, chips_ref, *refs):
+    n1_refs, refs = refs[:blocks], refs[blocks:]
+    bias_ref, cos_ref, sin_ref, key_place_ref, place_ref, start_ref, *refs = refs
     shards, refs = refs[:parts], refs[parts:]
     qkv_ref, o_ref, lse_ref, *out_refs, weight_ref, weights, sems, out_sem = refs
-    half = near_ref.shape[0]
+    length = qkv_ref.shape[0]
     copies = [
         pltpu.make_async_copy(
             shards[i],
@@ -201,8 +208,7 @@
         copy.wait()
     save = pltpu.make_async_copy(weights, weight_ref, out_sem)
     save.start()
-    for side, ref in enumerate((near_ref, far_ref)):
-        at = slice(side * half, (side + 1) * half)
+    for at, ref in rows_from(n1_refs):
         projected = dot_ab(ref[...], weights[:, :QKV_COLS]) + bias_ref[...]
         cos_both, sin_both = cos_ref[at, :], sin_ref[at, :]
         for j in range(HEADS + 1):
@@ -214,7 +220,7 @@
     values_t = qkv_ref[:, Q_COLS + HEAD_WIDTH : QKV_COLS].T
     lse_ref[...] = jnp.zeros_like(lse_ref)
     key_place = key_place_ref[...]
-    for at in range(0, 2 * half, TILE):
+    for at in range(0, length, TILE):
         block = slice(at, at + TILE)
         place, start = place_ref[:, block], start_ref[:, block]
         for h in range(HEADS):
@@ -226,26 +232,86 @@
             lse_ref[h : h + 1, block] = top + jnp.log(total)
             prob = (weights_exp * (1.0 / total)).astype(BF)
             o_ref[block, cols] = dot_ab(values_t, prob).astype(BF).T
-    for side in range(2):
-        part = dot_abt(o_ref[side * half : (side + 1) * half, :], weights[:, QKV_COLS:])
-        out_refs[2 * side][...] = part[: half // 2].astype(BF)
-        out_refs[2 * side + 1][...] = part[half // 2 :].astype(BF)
+    for at, ref in rows_from(out_refs):
+        ref[...] = dot_abt(o_ref[at, :], weights[:, QKV_COLS:]).astype(BF)
     save.wait()
 
 
-def attention(chips, rows_pair, bias, tables, shards):
-    near, far = rows_pair
-    half = near.shape[0]
-    length = 2 * half
+def documents_kernel(where_ref, ids_ref, other_ref, frequency_ref, angle_ref, key_place_ref, place_ref, start_ref):
+    core, place_x = where_ref[0], where_ref[1]
+    one = ids_ref.shape[1]
+
+    def in_order(ref):
+        rows = [ref[k : k + 1, :] for k in range(2)]
+        return [
+            jnp.where(place_x == 0, rows[0], rows[1]),
+            jnp.where(place_x == 0, rows[1], rows[0]),
+        ]
+
+    ids = jnp.concatenate(in_order(ids_ref) + in_order(other_ref), axis=1)
+    index = lax.broadcasted_iota(jnp.int32, (1, 4 * one), 1)
+    block = index // one
+    mine = core * 2 + place_x
+    place = jnp.bitwise_xor(mine, block) * one + index - block * one
+
+    def column(row):
+        return jnp.broadcast_to(row.astype(F32), (8, 4 * one)).T[:, :1]
+
+    ids_col, place_col = column(ids), column(place)
+    ids_row, place_row = ids.astype(F32), place.astype(F32)
+    start_row = jnp.min(
+        jnp.where(ids_col == ids_row, place_col, 4.0 * one), axis=0, keepdims=True
+    )
+    place_ref[...] = place
+    start_ref[...] = start_row.astype(jnp.int32)
+    key_place_ref[...] = place_col.astype(jnp.int32)
+    angle_ref[...] = column(place_row - start_row) * frequency_ref[...]
+
+
+def documents(core, place_x, ids, other_ids):
+    one = ids.shape[0] // 2
+    exponent = np.arange(0, HEAD_WIDTH, 2, dtype=np.float32) / np.float32(HEAD_WIDTH)
+    frequency = np.float32(1.0) / np.float32(ROPE_BASE) ** exponent
+    return pl.pallas_call(
+        documents_kernel,
+        grid_spec=pltpu.PrefetchScalarGridSpec(
+            num_scalar_prefetch=1,
+            grid=(),
+            in_specs=[WHOLE] * 3,
+            out_specs=[WHOLE] * 4,
+        ),
+        out_shape=[
+            jax.ShapeDtypeStruct((4 * one, HEAD_WIDTH), F32),
+            jax.ShapeDtypeStruct((4 * one, 1), jnp.int32),
+            jax.ShapeDtypeStruct((1, 4 * one), jnp.int32),
+            jax.ShapeDtypeStruct((1, 4 * one), jnp.int32),
+        ],
+        compiler_params=pltpu.CompilerParams(vmem_limit_bytes=VMEM_LIMIT),
+        cost_estimate=cost(flops=2**20, bytes_accessed=2**20, transcendentals=0),
+        name="documents",
+    )(
+        jnp.stack([core, place_x]).astype(jnp.int32),
+        ids.reshape(2, one),
+        other_ids.reshape(2, one),
+        jnp.asarray(np.concatenate([frequency, frequency])[None]),
+    )
+
+
+def four_shapes(rows):
+    return [jax.ShapeDtypeStruct((r, D), BF) for r in (rows, rows // 2, rows // 2) * 2]
+
+
+def attention(chips, n1, bias, tables, shards):
+    length = tables[0].shape[0]
     parts = len(shards)
     rows = shards[0].shape[0]
     return pl.pallas_call(
-        functools.partial(attention_kernel, parts, rows),
+        functools.partial(attention_kernel, len(n1), parts, rows),
         grid_spec=pltpu.PrefetchScalarGridSpec(
             num_scalar_prefetch=1,
             grid=(),
-            in_specs=[WHOLE] * 8 + [ANYWHERE] * parts,
-            out_specs=[WHOLE] * 7 + [ANYWHERE],
+            in_specs=[WHOLE] * (len(n1) + 6) + [ANYWHERE] * parts,
+            out_specs=[WHOLE] * 9 + [ANYWHERE],
             scratch_shapes=[
                 pltpu.VMEM((D, ATT_COLS), BF),
                 pltpu.SemaphoreType.DMA((parts,)),
@@ -256,7 +322,7 @@
             jax.ShapeDtypeStruct((length, QKV_COLS), BF),
             jax.ShapeDtypeStruct((length, Q_COLS), BF),
             jax.ShapeDtypeStruct((8, length), F32),
-            *[jax.ShapeDtypeStruct((half // 2, D), BF)] * 4,
+            *four_shapes(length // 4),
             jax.ShapeDtypeStruct((D, ATT_COLS), BF),
         ],
         compiler_params=pltpu.CompilerParams(vmem_limit_bytes=VMEM_LIMIT),
@@ -266,38 +332,19 @@
             transcendentals=HEADS * length * length,
         ),
         name="attention",
-    )(chips, near, far, bias, *tables, *shards)
-
-
-def attention_back_kernel(
-    count,
-    rows,
-    chips_ref,
-    near_ref,
-    far_ref,
-    n1_near_ref,
-    n1_far_ref,
-    qkv_ref,
-    o_ref,
-    lse_ref,
-    weight_ref,
-    cos_ref,
-    sin_ref,
-    key_place_ref,
-    place_ref,
-    start_ref,
-    dqkv_ref,
-    bias_ref,
-    *refs,
-):
-    *out_refs, mixed, grads = refs
-    half = near_ref.shape[0]
-    length = 2 * half
+    )(chips, *n1, bias, *tables, *shards)
+
+
+def attention_back_kernel(das, n1s, count, rows, chips_ref, *refs):
+    da_refs, n1_refs, refs = refs[:das], refs[das : das + n1s], refs[das + n1s :]
+    qkv_ref, o_ref, lse_ref, weight_ref, *refs = refs
+    cos_ref, sin_ref, key_place_ref, place_ref, start_ref, *refs = refs
+    dqkv_ref, bias_ref, *refs = refs
+    dn1_refs, block_refs, (mixed, left_t, grads) = refs[:6], refs[6:10], refs[10:]
+    length = qkv_ref.shape[0]
     scale = 1.0 / math.sqrt(HEAD_WIDTH)
-    for side, ref in enumerate((near_ref, far_ref)):
-        mixed[side * half : (side + 1) * half, :] = dot_ab(
-            ref[...], weight_ref[:, QKV_COLS:]
-        ).astype(BF)
+    for at, ref in rows_from(da_refs):
+        mixed[at, :] = dot_ab(ref[...], weight_ref[:, QKV_COLS:]).astype(BF)
     key_cols = slice(Q_COLS, Q_COLS + HEAD_WIDTH)
     value_cols = slice(Q_COLS + HEAD_WIDTH, QKV_COLS)
     keys, values = qkv_ref[:, key_cols], qkv_ref[:, value_cols]
@@ -325,21 +372,25 @@
     dqkv_ref[:, key_cols] = turn_halves(keys_grad * scale, cos_ref[...], -sin_ref[...]).astype(BF)
     dqkv_ref[:, value_cols] = values_grad.astype(BF)
     bias_ref[...] = jnp.sum(dqkv_ref[...].astype(F32), axis=0, keepdims=True)
-    for cols, pair, right_ref in (
-        (slice(0, QKV_COLS), (n1_near_ref, n1_far_ref), dqkv_ref),
-        (slice(QKV_COLS, ATT_COLS), (near_ref, far_ref), o_ref),
+    for cols, left_refs, right_ref in (
+        (slice(0, QKV_COLS), n1_refs, dqkv_ref),
+        (slice(QKV_COLS, ATT_COLS), da_refs, o_ref),
     ):
+        for at, ref in rows_from(left_refs):
+            left_t[:, at] = ref[...].T
         grads[:, :, cols] = (
-            dot_ab(pair[0][...].T, right_ref[:half, :]) + dot_ab(pair[1][...].T, right_ref[half:, :])
-        ).astype(BF).reshape(4 * count, rows, -1)
+            dot_ab(left_t[...], right_ref[...]).astype(BF).reshape(4 * count, rows, -1)
+        )
     at = 0
-    for ref in out_refs:
+    for ref in block_refs:
         for k in range(ref.shape[0]):
             ref[k] = grads[chips_ref[at]]
             at += 1
-
-
-def attention_back(chips, da_pair, n1_pair, qkv, o, lse, weight, tables):
+    for at, ref in rows_from(dn1_refs):
+        ref[...] = dot_abt(dqkv_ref[at, :], weight_ref[:, :QKV_COLS]).astype(BF)
+
+
+def attention_back(chips, da, n1, qkv, o, lse, weight, tables):
     length = qkv.shape[0]
     count = chips.shape[0] // 4
     rows = D // (4 * count)
@@ -347,20 +398,22 @@
         jax.ShapeDtypeStruct((2 * k, rows, ATT_COLS), BF) for k in (count - 1, 1, count - 1, 1)
     ]
     return pl.pallas_call(
-        functools.partial(attention_back_kernel, count, rows),
+        functools.partial(attention_back_kernel, len(da), len(n1), count, rows),
         grid_spec=pltpu.PrefetchScalarGridSpec(
             num_scalar_prefetch=1,
             grid=(),
-            in_specs=[WHOLE] * 13,
-            out_specs=[WHOLE] * 6,
+            in_specs=[WHOLE] * (len(da) + len(n1) + 9),
+            out_specs=[WHOLE] * 12,
             scratch_shapes=[
                 pltpu.VMEM((length, Q_COLS), BF),
+                pltpu.VMEM((D, length), BF),
                 pltpu.VMEM((4 * count, rows, ATT_COLS), BF),
             ],
         ),
         out_shape=[
             jax.ShapeDtypeStruct((length, QKV_COLS), BF),
             jax.ShapeDtypeStruct((1, QKV_COLS), F32),
+            *four_shapes(length // 4),
             *blocks,
         ],
         compiler_params=pltpu.CompilerParams(vmem_limit_bytes=VMEM_LIMIT),
@@ -370,24 +423,24 @@
             transcendentals=HEADS * length * length,
         ),
         name="attention_back",
-    )(chips, *da_pair, *n1_pair, qkv, o, lse, weight, *tables)
+    )(chips, *da, *n1, qkv, o, lse, weight, *tables)
 
 
 def feed_forward_kernel(whole, split, rows, chips_ref, *refs):
-    n2_refs, dy_refs, refs = refs[:2], refs[2:4], refs[4:]
+    n2_refs, dy_refs, refs = refs[:6], refs[6:12], refs[12:]
     pieces, refs = refs[: whole + 2 * split], refs[whole + 2 * split :]
-    keep_ref, send_ref, u_ref, dgate_ref, dup_ref, *refs = refs
-    n2_t_ref, dy_t_ref, down_ref, gu_w, d_w, n2_s, dy_s, sems, out_sem = refs
+    dn2_refs, refs = refs[:8], refs[8:]
+    u_ref, dgate_ref, dup_ref, n2_t_ref, dy_t_ref, down_ref, *refs = refs
+    gu_w, d_w, tiles, tile_sems, sems, out_sem = refs
     step = pl.program_id(0)
     steps = pl.num_programs(0)
+    one = tiles.shape[2]
 
     def copies():
         for i in range(whole + split):
             at = pl.ds(pl.multiple_of(chips_ref[i] * rows, rows), rows)
             for j in range(3):
-                if i < whole:
-                    here = pieces[i].at[j]
-                elif j < 2:
+                if i < whole or j < 2:
                     here = pieces[i].at[j]
                 else:
                     here = pieces[i + split]
@@ -397,24 +450,39 @@
                     there = d_w.at[at, :]
                 yield pltpu.make_async_copy(here, there, sems.at[i, j])
 
+    def tile_copies(j):
+        part, row = divmod(j, 4)
+        ref, at = ((0, 0), (1, 0), (1, one), (2, 0))[row]
+        for k, taken in enumerate((n2_refs, dy_refs)):
+            yield pltpu.make_async_copy(
+                taken[3 * part + ref].at[pl.ds(at, one), :],
+                tiles.at[j % 2, k],
+                tile_sems.at[j % 2, k],
+            )
+
     save = pltpu.make_async_copy(d_w, down_ref, out_sem)
 
     @pl.when(step == 0)
     def _():
         for copy in copies():
             copy.start()
+        for copy in tile_copies(0):
+            copy.start()
         for copy in copies():
             copy.wait()
         save.start()
 
-    for j in range(2):
-
-        @pl.when(step // 4 == j)
+    for j in range(8):
+
+        @pl.when(step == j)
         def _(j=j):
-            n2_s[...] = n2_refs[j][...]
-            dy_s[...] = dy_refs[j][...]
-
-    n2, dy = n2_s[...], dy_s[...]
+            if j < 7:
+                for copy in tile_copies(j + 1):
+                    copy.start()
+            for copy in tile_copies(j):
+                copy.wait()
+
+    n2, dy = tiles[step % 2, 0], tiles[step % 2, 1]
     n2_t_ref[...] = n2.T
     dy_t_ref[...] = dy.T
     gate_up = dot_ab(n2, gu_w[...])
@@ -428,14 +496,11 @@
     dup_ref[...] = dup
     dgate_ref[...] = dgate
     dn2 = dot_abt(jnp.concatenate([dgate, dup], axis=1), gu_w[...]).astype(BF)
-
-    @pl.when(step < steps // 2)
-    def _():
-        keep_ref[...] = dn2
-
-    @pl.when(step >= steps // 2)
-    def _():
-        send_ref[...] = dn2
+    for j in range(8):
+
+        @pl.when(step == j)
+        def _(j=j):
+            dn2_refs[j][...] = dn2
 
     @pl.when(step == steps - 1)
     def _():
@@ -444,32 +509,29 @@
 
 def feed_forward(chips, n2, dy, whole, split):
     rows = whole[0].shape[1]
-    one = n2[0].shape[0] // 4
+    one = n2[0].shape[0]
     length = 8 * one
     tile = lambda width: pl.BlockSpec((one, width), lambda i, c: (i, 0))
     turned = pl.BlockSpec((D, one), lambda i, c: (0, i))
-    taken = [
-        pl.BlockSpec((one, D), lambda i, c: (jnp.minimum(i, 3), 0)),
-        pl.BlockSpec((one, D), lambda i, c: (jnp.maximum(i - 4, 0), 0)),
-    ]
+    kept = pl.BlockSpec((one, D), lambda i, c: (0, 0))
     parts = len(whole) + len(split)
     return pl.pallas_call(
         functools.partial(feed_forward_kernel, len(whole), len(split), rows),
         grid_spec=pltpu.PrefetchScalarGridSpec(
             num_scalar_prefetch=1,
             grid=(8,),
-            in_specs=taken * 2 + [ANYWHERE] * (len(whole) + 2 * len(split)),
-            out_specs=taken + [tile(FF_OWN)] * 3 + [turned, turned, ANYWHERE],
+            in_specs=[ANYWHERE] * (12 + len(whole) + 2 * len(split)),
+            out_specs=[kept] * 8 + [tile(FF_OWN)] * 3 + [turned, turned, ANYWHERE],
             scratch_shapes=[
                 pltpu.VMEM((D, 2 * FF_OWN), BF),
                 pltpu.VMEM((D, FF_OWN), BF),
-                pltpu.VMEM((one, D), BF),
-                pltpu.VMEM((one, D), BF),
+                pltpu.VMEM((2, 2, one, D), BF),
+                pltpu.SemaphoreType.DMA((2, 2)),
                 pltpu.SemaphoreType.DMA((parts, 3)),
                 pltpu.SemaphoreType.DMA,
             ],
         ),
-        out_shape=[jax.ShapeDtypeStruct((length // 2, D), BF)] * 2
+        out_shape=[jax.ShapeDtypeStruct((one, D), BF)] * 8
         + [jax.ShapeDtypeStruct((length, FF_OWN), BF)] * 3
         + [jax.ShapeDtypeStruct((D, length), BF)] * 2
         + [jax.ShapeDtypeStruct((D, FF_OWN), BF)],
@@ -484,7 +546,7 @@
 
 
 def weight_grad_kernel(rows, place_ref, left_ref, right_ref, *refs):
-    out_refs, total = refs[:4], refs[4]
+    keep_ref, send_ref, total = refs
     width = right_ref.shape[1]
     for at in range(0, width, 256):
         to = min(at + 256, width)
@@ -494,16 +556,16 @@
     lo, yy = place_ref[1], place_ref[2]
     for k in range(2):
         row = jnp.where(lo == 0, k, 1 - k) * 2
-        out_refs[k][0] = total[row + yy].astype(BF)
-        out_refs[2 + k][0] = total[row + 1 - yy].astype(BF)
+        keep_ref[0, k] = total[row + yy].astype(BF)
+        send_ref[0, k] = total[row + 1 - yy].astype(BF)
 
 
 def weight_grad(place, left, right):
     count = lax.axis_size("hi")
     length, width = right.shape
     rows = left.shape[0] // (4 * count)
-    block = pl.BlockSpec((1, rows, width), lambda i, p: (i, 0, 0))
-    out = jax.ShapeDtypeStruct((count, rows, width), BF)
+    block = pl.BlockSpec((1, 2, rows, width), lambda i, p: (i, 0, 0, 0))
+    out = jax.ShapeDtypeStruct((count, 2, rows, width), BF)
     return pl.pallas_call(
         functools.partial(weight_grad_kernel, rows),
         grid_spec=pltpu.PrefetchScalarGridSpec(
@@ -513,10 +575,10 @@
                 pl.BlockSpec((4 * rows, length), lambda i, p: (lax.rem(i + p[0], count), 0)),
                 pl.BlockSpec((length, width), lambda i, p: (0, 0)),
             ],
-            out_specs=[block] * 4,
+            out_specs=[block] * 2,
             scratch_shapes=[pltpu.VMEM((4, rows, width), F32)],
         ),
-        out_shape=[out] * 4,
+        out_shape=[out] * 2,
         compiler_params=pltpu.CompilerParams(vmem_limit_bytes=VMEM_LIMIT),
         cost_estimate=cost(
             flops=2 * length * D * width, bytes_accessed=16 * 2**20, transcendentals=0
@@ -525,17 +587,13 @@
     )(place, left, right)
 
 
-def down_kernel(left_ref, right_ref, keep_ref, send_ref):
-    step = pl.program_id(0)
+def down_kernel(left_ref, right_ref, *out_refs):
     product = dot_abt(left_ref[...], right_ref[...]).astype(BF)
-
-    @pl.when(step < pl.num_programs(0) // 2)
-    def _():
-        keep_ref[...] = product
-
-    @pl.when(step >= pl.num_programs(0) // 2)
-    def _():
-        send_ref[...] = product
+    for j in range(8):
+
+        @pl.when(pl.program_id(0) == j)
+        def _(j=j):
+            out_refs[j][...] = product
 
 
 def down(left, right):
@@ -548,11 +606,8 @@
             pl.BlockSpec((one, width), lambda i: (i, 0)),
             pl.BlockSpec((D, width), lambda i: (0, 0)),
         ],
-        out_specs=[
-            pl.BlockSpec((one, D), lambda i: (jnp.minimum(i, 3), 0)),
-            pl.BlockSpec((one, D), lambda i: (jnp.maximum(i - 4, 0), 0)),
-        ],
-        out_shape=[jax.ShapeDtypeStruct((length // 2, D), BF)] * 2,
+        out_specs=[pl.BlockSpec((one, D), lambda i: (0, 0))] * 8,
+        out_shape=[jax.ShapeDtypeStruct((one, D), BF)] * 8,
         compiler_params=pltpu.CompilerParams(vmem_limit_bytes=VMEM_LIMIT),
         cost_estimate=cost(
             flops=2 * length * D * width, bytes_accessed=14 * 2**20, transcendentals=0
@@ -561,52 +616,60 @@
     )(left, right)
 
 
+def total_of(*parts):
+    return sum(part.astype(F32) for part in parts)
+
+
 class EightSum:
-    def __init__(self, keep, send):
-        self.keep = keep
-        self.one = keep.shape[0] // 4
-        self.half = self.one // 2
-        self.core = swap(send, "core")
-
-    def part(self, begin, rows):
-        at = slice(begin, begin + rows)
-        return self.keep[at].astype(F32) + self.core[at].astype(F32)
+    def __init__(self, parts):
+        self.keep = parts[:4]
+        self.core = [None] * 4
+        for k in (3, 1, 2, 0):
+            self.core[k] = swap(parts[4 + k], "core")
+        self.half = parts[0].shape[0] // 2
 
     def second(self, order):
         self.core = order.done(self.core)
-        one, half = self.one, self.half
-        both_lo = self.part(3 * one, half).astype(BF)
-        both_x = self.part(3 * one + half, half).astype(BF)
-        self.to_lo, self.to_x = swap(both_lo, "tensor"), swap(both_x, "lo")
+        half = self.half
+        both, by_x, by_lo = [total_of(self.keep[k], self.core[k]) for k in (3, 1, 2)]
+        self.to_lo = swap(both[:half].astype(BF), "tensor")
+        self.to_x = swap(both[half:].astype(BF), "lo")
+        self.x_first = swap(by_x[:half].astype(BF), "tensor")
+        self.lo_second = swap(by_lo[half:].astype(BF), "lo")
+        self.by_x, self.by_lo = by_x[half:], by_lo[:half]
 
     def third(self, order):
-        one, half = self.one, self.half
-        to_lo, to_x = order.done((self.to_lo, self.to_x))
-        by_x = [self.part(one, half), self.part(one + half, half) + to_x.astype(F32)]
-        by_lo = [self.part(2 * one, half) + to_lo.astype(F32), self.part(2 * one + half, half)]
-        self.by_x = swap(jnp.concatenate(by_x, axis=0).astype(BF), "tensor")
-        self.by_lo = swap(jnp.concatenate(by_lo, axis=0).astype(BF), "lo")
+        to_lo, to_x, self.x_first, self.lo_second = order.done(
+            (self.to_lo, self.to_x, self.x_first, self.lo_second)
+        )
+        self.x_second = swap(total_of(self.by_x, to_x).astype(BF), "tensor")
+        self.lo_first = swap(total_of(self.by_lo, to_lo).astype(BF), "lo")
 
     def total(self, order):
-        by_x, by_lo = order.done((self.by_x, self.by_lo))
-        return self.part(0, self.one) + by_x.astype(F32) + by_lo.astype(F32)
+        x_second, lo_first = order.done((self.x_second, self.lo_first))
+        return (
+            total_of(self.keep[0], self.core[0])
+            + jnp.concatenate([self.x_first, x_second], axis=0).astype(F32)
+            + jnp.concatenate([lo_first, self.lo_second], axis=0).astype(F32)
+        )
 
 
 class FourSum:
-    def __init__(self, own, by_x, core_own, core_by_x):
-        self.own, self.by_x = own, by_x
-        self.core_by_x, self.core_own = swap(core_by_x, "core"), swap(core_own, "core")
+    def __init__(self, own, first, second, core_own, core_first, core_second):
+        self.own, self.x = own, (first, second)
+        self.core_x = swap(core_first, "core"), swap(core_second, "core")
+        self.core_own = swap(core_own, "core")
 
     def second(self, order):
-        core_by_x = order.done(self.core_by_x)
-        by_x = (self.by_x.astype(F32) + core_by_x.astype(F32)).astype(BF)
-        self.x = swap(by_x, "tensor")
+        core_x = order.done(self.core_x)
+        by_x = [total_of(*pair).astype(BF) for pair in zip(self.x, core_x)]
+        self.x = [swap(part, "tensor") for part in by_x]
         order.mark = by_x
+
+    def total(self, order):
         self.core_own = order.done(self.core_own)
-
-    def total(self, order):
         x = order.done(self.x)
-        return self.own.astype(F32) + self.core_own.astype(F32) + x.astype(F32)
+        return total_of(self.own, self.core_own, jnp.concatenate(x, axis=0))
 
 
 class GradSum:
@@ -614,15 +677,25 @@
         self.keep = keep
         self.other = swap(send, "yy")
 
-    def across(self, order):
+    def across(self, order, by_gather):
         self.other = order.done(self.other)
-        self.far = [
-            turn((self.keep[k].astype(F32) + self.other[k].astype(F32)).astype(BF), "hi", k)
-            for k in range(1, lax.axis_size("hi"))
-        ]
-
-    def total(self, order):
-        self.far = order.done(self.far)
+        count = lax.axis_size("hi")
+        far = [total_of(self.keep[k], self.other[k]).astype(BF) for k in range(1, count)]
+        if by_gather:
+            self.every = [lax.all_gather(part, "hi") for part in far]
+        else:
+            self.every = None
+            self.far = [turn(part, "hi", k + 1) for k, part in enumerate(far)]
+        order.mark = far
+
+    def arrived(self, order):
+        if self.every is None:
+            self.far = order.done(self.far)
+        else:
+            every = order.done(self.every)
+            self.far = [others_of(part)[k] for k, part in enumerate(every)]
+
+    def total(self):
         total = self.keep[0].astype(F32) + self.other[0].astype(F32)
         for far in self.far:
             total = total + far.astype(F32)
@@ -701,7 +774,6 @@
     order.mark = n1
     att_shard = both_cores(attention_pack(core), order.done(att_core), 0)
     order.mark = att_shard
-    other_ids = order.done(other_ids)
     att_hi = [turn(att_shard, "hi", k) for k in steps]
     att_yy = swap(att_shard, "yy")
     att_lo = swap(att_shard, "lo")
@@ -715,60 +787,36 @@
     ff_theirs = lax.dynamic_slice_in_dim(ff_low, (1 - core) * FF_CORE, FF_CORE, 2)
     ff_core = swap(ff_theirs, "core")
     order.mark = ff_theirs
+
     ff_shard = both_cores(ff_mine, order.done(ff_core), 1)
     ff_own = lax.dynamic_slice_in_dim(ff_shard, lo * FF_OWN, FF_OWN, 2)
     ff_theirs = lax.dynamic_slice_in_dim(ff_shard, (1 - lo) * FF_OWN, FF_OWN, 2)
     order.mark = ff_theirs
-    ff_hi = [turn(ff_own, "hi", k) for k in steps]
-    ff_lo = swap(ff_theirs, "lo")
+    ff_hi = lax.all_gather(ff_own, "hi")
     att_lo = order.done(att_lo)
     att_lo_yy = swap(att_lo, "yy")
-
-    ids = both_cores(segments, other_ids, 0)
-    length = ids.shape[0]
-    places = jnp.arange(length, dtype=jnp.int32)
-    earlier = jnp.concatenate([ids[:1], ids[:-1]])
-    starts = lax.cummax(jnp.where((places == 0) | (ids != earlier), places, 0), axis=0)
-
-    def own_first(values):
-        parts = values.reshape(4, own_rows)
-        me = core * 2 + place_x
-        return jnp.concatenate(
-            [lax.dynamic_index_in_dim(parts, me ^ k, 0, keepdims=False) for k in range(4)]
-        )
-
-    starts = own_first(starts)
-    places = own_first(places)
-    positions = (places - starts).astype(F32)
-    frequency = 1.0 / ROPE_BASE ** (jnp.arange(0, HEAD_WIDTH, 2, dtype=F32) / HEAD_WIDTH)
-    angles = positions[:, None] * frequency[None, :]
-    cos_part, sin_part = jnp.cos(angles), jnp.sin(angles)
-    tables = (
-        jnp.concatenate([cos_part, cos_part], axis=1),
-        jnp.concatenate([-sin_part, sin_part], axis=1),
-        places[:, None],
-        places[None, :],
-        starts[None, :],
-    )
-    tables = order.done(tables)
-
     att_yy = order.done(att_yy)
     att_hi = order.done(att_hi)
     att_hi_lo = [swap(part, "lo") for part in att_hi]
     att_hi_yy = [swap(part, "yy") for part in att_hi]
-    n1_x = order.done(n1_x)
-    n1_near = jnp.concatenate([n1, n1_x], axis=0)
-    n1_far = swap(n1_near, "core")
-    order.mark = n1_near
-    cot_x = swap(order.after(cotangent), "tensor")
+    n1_core = swap(order.after(n1), "core")
     att_lo_yy = order.done(att_lo_yy)
-    ff_yy = swap(order.after(ff_own), "yy")
     att_hi_lo = order.done(att_hi_lo)
     att_hi_lo_yy = [swap(part, "yy") for part in att_hi_lo]
-    n1_far = order.done(n1_far)
+    ff_lo = swap(order.after(ff_theirs), "lo")
+    n1_core = order.done(n1_core)
+    n1_x = order.done(n1_x)
+    n1_core_x = swap(n1_x, "core")
+    other_ids = order.done(other_ids)
+    angles, key_place, row_place, row_start = documents(core, place_x, segments, other_ids)
+    sign = jnp.where(jnp.arange(HEAD_WIDTH) < HEAD_WIDTH // 2, -1.0, 1.0)
+    tables = order.after((jnp.cos(angles), jnp.sin(angles) * sign, key_place, row_place, row_start))
+    order.mark = tables[0]
     att_hi_yy = order.done(att_hi_yy)
-    cot_lo = swap(order.after(cotangent), "lo")
+    cot_x = swap(order.after(cotangent), "tensor")
+    n1_core_x = order.done(n1_core_x)
     att_hi_lo_yy = order.done(att_hi_lo_yy)
+    ff_yy = swap(order.after(ff_own), "yy")
 
     near_parts = [att_shard, att_lo]
     yy_parts = [att_yy, att_lo_yy]
@@ -776,83 +824,86 @@
         near_parts += [att_hi[k], att_hi_lo[k]]
         yy_parts += [att_hi_yy[k], att_hi_lo_yy[k]]
     att_parts = near_parts + yy_parts
-    n1_pair = order.after((n1_near, n1_far))
+    n1_parts = order.after((n1, n1_x, n1_core, n1_core_x))
     qkv, attn_rows, lse, *out_parts, att_weight = attention(
-        tree_order(-1), n1_pair, bias_local[None], tables, att_parts
+        tree_order(-1), n1_parts, bias_local[None], tables, att_parts
     )
     order.mark = lse
 
     out = FourSum(*out_parts)
     half = own_rows // 2
+    cot_x = order.done(cot_x)
+    ff_lo = order.done(ff_lo)
+    ff_lo_hi = [lax.all_gather(part, "hi") for part in (ff_lo[:2], ff_lo[2])]
     ff_yy = order.done(ff_yy)
-    ff_lo = order.done(ff_lo)
     ff_lo_yy = swap(ff_lo, "yy")
-    ff_hi = order.done(ff_hi)
-    ff_lo_hi_gu = [turn(order.after(ff_lo[:2]), "hi", k) for k in steps]
     out.second(order)
-    cot_x, cot_lo = order.done((cot_x, cot_lo))
-    cot_both = swap(cot_lo[:half], "tensor"), swap(cot_x[half:], "lo")
-    ff_lo_yy = order.done(ff_lo_yy)
-    ff_hi_yy = [swap(order.after(part), "yy") for part in ff_hi]
+    cot_lo = swap(order.after(cotangent), "lo")
     residual = rows_in + out.total(order)
     scale_two = rms_scale(residual)
     n2 = (residual * scale_two * gain_two).astype(BF)
-    n2_x, n2_lo = swap(n2, "tensor"), swap(n2, "lo")
+    n2_x_second, n2_lo_first = swap(n2[half:], "tensor"), swap(n2[:half], "lo")
+    n2_x_first, n2_lo_second = swap(n2[:half], "tensor"), swap(n2[half:], "lo")
     order.mark = n2
+    ff_hi = others_of(order.done(ff_hi))
+    order.mark = ff_hi
+    n2_x_second, n2_lo_first = order.done((n2_x_second, n2_lo_first))
+    n2_both = swap(n2_lo_first, "tensor"), swap(n2_x_second, "lo")
+    ff_lo_yy, cot_lo = order.done((ff_lo_yy, cot_lo))
+    ff_hi_yy = [swap(order.after(part), "yy") for part in ff_hi]
+    n2_x_first, n2_lo_second = order.done((n2_x_first, n2_lo_second))
+    n2_near = jnp.concatenate([n2_x_first, n2_x_second, n2_lo_first, n2_lo_second])
+    n2_core_near = swap(n2_near, "core")
+    order.mark = n2_near
+    n2_both = jnp.concatenate(order.done(n2_both))
+    n2_core_both, n2_core = swap(n2_both, "core"), swap(n2, "core")
+    order.mark = n2_both
+    cot_both = swap(order.after(cot_lo[:half]), "tensor"), swap(order.after(cot_x[half:]), "lo")
+    n2_core_near, n2_core_both, n2_core = order.done((n2_core_near, n2_core_both, n2_core))
     cot_both = order.done(cot_both)
-    cot_near = jnp.concatenate([cotangent, cot_x, cot_lo, *cot_both], axis=0)
-    order.mark = cot_near
-    ff_lo_hi_gu = order.done(ff_lo_hi_gu)
-    ff_lo_hi_d = [turn(order.after(ff_lo[2]), "hi", k) for k in steps]
-    n2_x, n2_lo = order.done((n2_x, n2_lo))
-    n2_both = swap(n2_lo[:half], "tensor"), swap(n2_x[half:], "lo")
+    cot_parts = [cotangent, jnp.concatenate([cot_x, cot_lo]), jnp.concatenate(cot_both)]
+    cot_parts += [swap(part, "core") for part in cot_parts]
+    order.mark = cot_parts[:3]
     ff_hi_yy = order.done(ff_hi_yy)
-    ff_lo_hi_yy_gu = [swap(order.after(part), "yy") for part in ff_lo_hi_gu]
-    cot_far = swap(order.after(cot_near), "core")
-    n2_both = order.done(n2_both)
-    n2_near = jnp.concatenate([n2, n2_x, n2_lo, *n2_both], axis=0)
-    n2_far = swap(n2_near, "core")
-    order.mark = n2_near
-    ff_lo_hi_d = order.done(ff_lo_hi_d)
+    ff_lo_hi_gu = others_of(order.done(ff_lo_hi[0]))
+    ff_lo_hi_yy_gu = [swap(part, "yy") for part in ff_lo_hi_gu]
+    order.mark = ff_lo_hi_gu
+    ff_lo_hi_d = others_of(order.done(ff_lo_hi[1]))
     ff_lo_hi_yy_d = [swap(part, "yy") for part in ff_lo_hi_d]
-    cot_far = order.done(cot_far)
-    n2_far = order.done(n2_far)
+    order.mark = ff_lo_hi_d
+    cot_parts = order.done(cot_parts)
     ff_lo_hi_yy_gu = order.done(ff_lo_hi_yy_gu)
     ff_lo_hi_yy_d = order.done(ff_lo_hi_yy_d)
+    n2_parts = [n2, n2_near, n2_both, n2_core, n2_core_near, n2_core_both]
 
     whole = [ff_own, ff_lo, ff_yy, ff_lo_yy, *ff_hi, *ff_hi_yy]
     split = [*zip(ff_lo_hi_gu, ff_lo_hi_d), *zip(ff_lo_hi_yy_gu, ff_lo_hi_yy_d)]
     ff_chips = [chip_at(0, l, y) for y in (0, 1) for l in (0, 1)]
     ff_chips += [chip_at(-k, l, y) for l in (0, 1) for y in (0, 1) for k in steps]
-    keep, send, hidden, gate_grad, up_grad, n2_t, cot_t, w_down = feed_forward(
-        jnp.stack(ff_chips).astype(jnp.int32),
-        order.after((n2_near, n2_far)),
-        (cot_near, cot_far),
-        whole,
-        split,
+    *dn2_parts, hidden, gate_grad, up_grad, n2_t, cot_t, w_down = feed_forward(
+        jnp.stack(ff_chips).astype(jnp.int32), order.after(n2_parts), cot_parts, whole, split
     )
     order.mark = w_down
 
     place = jnp.stack([hi, lo, yy]).astype(jnp.int32)
 
-    def grad_parts(left, right, send_now=True):
-        keep_own, keep_lo, send_own, send_lo = weight_grad(place, order.after(left), right)
-        order.mark = keep_own
-        first = GradSum(keep_lo, send_lo) if send_now else (keep_lo, send_lo)
-        return first, (keep_own, send_own)
+    def grad_of(left, right):
+        keep, send = weight_grad(place, order.after(left), right)
+        order.mark = keep
+        return GradSum(keep, send)
 
     ff_squares = 0.0
     rows_of = lambda value, which, axis: lax.dynamic_slice_in_dim(
         value, which * shard_rows, shard_rows, axis
     )
 
-    def this_side(lo_sum):
+    def summed_up(grad):
         nonlocal ff_squares
-        total = lo_sum.total(order)
+        total = order.after(grad.total())
         ff_squares = ff_squares + jnp.sum(total * total)
         low = total.astype(BF)
         order.mark = low
-        return low, swap(low, "lo")
+        return low[0], swap(low[1], "lo")
 
     def own_rows_of(low, other):
         other = order.done(other)
@@ -865,76 +916,62 @@
         order.mark = theirs
         return rows_of(cols, core, 0), swap(theirs, "core")
 
-    def own_sum(own):
-        nonlocal ff_squares
-        total = own.total(order)
-        ff_squares = ff_squares + jnp.sum(total * total)
-        order.mark = total.astype(BF)
-        return order.mark
-
-    dn2 = EightSum(keep, send)
-    d_lo, d_own = grad_parts(cot_t, hidden)
-    d_own = GradSum(*d_own)
+    dn2 = EightSum(dn2_parts)
+    d_sum = grad_of(cot_t, hidden)
     dn2.second(order)
-    g_lo, g_own = grad_parts(n2_t, gate_grad)
+    g_sum = grad_of(n2_t, gate_grad)
     dn2.third(order)
-    u_lo, u_own = grad_parts(n2_t, up_grad, False)
-    d_lo.across(order)
+    u_sum = grad_of(n2_t, up_grad)
+    d_sum.across(order, True)
     norm_two_in, gain_two_grad = norm_backward(residual, scale_two, gain_two, dn2.total(order))
     residual_grad = cotangent.astype(F32) + norm_two_in
     da = residual_grad.astype(BF)
-    da_x = swap(da, "tensor")
+    da_x = [swap(da[:half], "tensor"), swap(da[half:], "tensor")]
+    da_core = swap(da, "core")
     order.mark = da
-    keep, send = down(*order.after((hidden, w_down)))
-    order.mark = keep
+    branch_parts = down(*order.after((hidden, w_down)))
+    order.mark = branch_parts[0]
     da_x = order.done(da_x)
-    da_near = jnp.concatenate([da, da_x], axis=0)
-    da_far = swap(da_near, "core")
-    order.mark = da_near
-    d_own.across(order)
-    g_own = GradSum(g_own[0], order.after(g_own[1]))
-    g_lo.across(order)
-    u_lo = GradSum(u_lo[0], order.after(u_lo[1]))
-    d_way = this_side(d_lo)[1]
-    da_far = order.done(da_far)
-
-    projected_grad, bias_grad, *att_grads = attention_back(
-        sum_order(), order.after((da_near, da_far)), n1_pair, qkv, attn_rows, lse, att_weight, tables
+    da_core_x = [swap(part, "core") for part in da_x]
+    da_core, da_core_x = order.done((da_core, da_core_x))
+
+    _, bias_grad, *parts = attention_back(
+        sum_order(),
+        order.after((da, *da_x, da_core, *da_core_x)),
+        n1_parts,
+        qkv,
+        attn_rows,
+        lse,
+        att_weight,
+        tables,
     )
     order.mark = bias_grad
-    bias_grad = bias_grad[0]
-    att = ChipSum(*att_grads)
-    d_low = own_sum(d_own)
-    g_own.across(order)
-    g_way = this_side(g_lo)[1]
-    u_lo.across(order)
-    dn1_parts = [None] * 4
-    for k in (3, 2, 1, 0):
-        part = order.after(projected_grad)[k * own_rows : (k + 1) * own_rows]
-        dn1_parts[k] = dot_abt(part, att_weight[:, :QKV_COLS]).astype(BF)
-        order.mark = dn1_parts[k]
-    dn1 = FourSum(*dn1_parts)
+    g_sum.across(order, True)
+    dn1 = FourSum(*parts[:6])
+    att = ChipSum(*parts[6:])
     dn1.second(order)
+    d_sum.arrived(order)
+    u_sum.across(order, False)
     att.far_yy(order)
-    u_own = GradSum(u_own[0], order.after(u_own[1]))
+    norm_one_in, gain_one_grad = norm_backward(rows_in, scale_one, gain_one, dn1.total(order))
+    order.mark = gain_one_grad
+    att.far_hi(order)
+    d_low, d_way = summed_up(d_sum)
+    input_grad = residual_grad + norm_one_in
+    att.near_yy(order)
+    branch = EightSum(order.after(branch_parts))
+    g_sum.arrived(order)
+    g_low, g_way = summed_up(g_sum)
     d_rows = own_rows_of(d_low, d_way)
-    g_low = own_sum(g_own)
-    att.far_hi(order)
-    branch = EightSum(keep, order.after(send))
-    norm_one_in, gain_one_grad = norm_backward(rows_in, scale_one, gain_one, dn1.total(order))
-    input_grad = residual_grad + norm_one_in
-    order.mark = gain_one_grad
-    att.near_yy(order)
-    u_way = this_side(u_lo)[1]
     branch.second(order)
-    u_own.across(order)
-    g_rows = own_rows_of(g_low, g_way)
+    u_sum.arrived(order)
+    u_low, u_way = summed_up(u_sum)
     att_sum = att.total(order)
     att_low = att_sum.astype(BF)
     other_att = swap(rows_of(att_low, 1 - core, 0), "core")
     order.mark = att_low
+    g_rows = own_rows_of(g_low, g_way)
     branch.third(order)
-    u_low = own_sum(u_own)
     other_att = order.done(other_att)
 
     own_att = rows_of(att_low, core, 0)
@@ -946,6 +983,7 @@
     owned_squares = (
         jnp.sum(qkv_owned * qkv_owned) + jnp.sum(out_owned * out_owned) + ff_squares
     )
+    bias_grad = order.after(bias_grad)[0]
     bias_slots = lax.dynamic_update_slice_in_dim(
         jnp.zeros_like(bias_all), bias_grad[:Q_COLS], q_at, 0
     )

time: 652 us -> 646 us (level)
  waiting for transfers between devices: 271 us -> 226 us
  local copies, waits for them, and re-layouts: 28.1 us -> 50.9 us
  blocking collectives: 0 us -> 21.9 us
  other arithmetic: 102 us -> 86.4 us
  between operations: 9.94 us -> 21.1 us
  Pallas kernels: 155 us -> 163 us
    ppermute x66 -> x87, waiting for transfers between devices: 230 us -> 160 us  [swap(): return lax.ppermute(value, axis, [(0, 1), (1, 0)])]
    all_gather x0 -> x4, waiting for transfers between devices: none -> 51.6 us  [the longest x1 29.9 us: body(): ff_hi = lax.all_gather(ff_own, 'hi')]
    ppermute x11 -> x3, waiting for transfers between devices: 40.9 us -> 14.7 us  [turn(): lax.ppermute(value, axis, [(i, (i + steps) % count) for i in range(count)])]
    ppermute x11 -> x3, starting transfers between devices: 28.8 us -> 3.6 us  [turn(): lax.ppermute(value, axis, [(i, (i + steps) % count) for i in range(count)])]
    all_gather x0 -> x1, blocking collectives: none -> 21.9 us  [body(): ff_lo_hi = [lax.all_gather(part, 'hi') for part in (ff_lo[:2], ff_lo[2])]]
    ppermute x66 -> x87, starting transfers between devices: 44.6 us -> 64.6 us  [swap(): return lax.ppermute(value, axis, [(0, 1), (1, 0)])]
    reduce_sum x6 -> x3, other arithmetic: 14.6 us -> 3.16 us  [summed_up(): ff_squares = ff_squares + jnp.sum(total * total)]
    slice x8 -> x12, local copies, waits for them, and re-layouts: 2.02 us -> 13.2 us  [the longest x2 3.96 us: body(): ff_lo_hi = [lax.all_gather(part, 'hi') for part in (ff_lo[:2], ff_lo[2])]]
  transfers between devices with their start and end apart: 78 -> 95, of which waited for: 34 -> 35; matrix products, arithmetic and copies ran while one was open for 18% -> 18% of each run, Pallas kernels for 16% -> 17%
where the time goes in v2:
time: 646 us; the launch traced here: 640 us
  waiting for transfers between devices  226 us (35%)
  Pallas kernels  163 us (25%)
  other arithmetic  86.4 us (13%)
  starting transfers between devices  70.1 us (11%)
  local copies, waits for them, and re-layouts  50.9 us (8%)
  blocking collectives  21.9 us (3%)
  between operations  21.1 us (3%)
    ppermute x87, waiting for transfers between devices, swap(): return lax.ppermute(value, axis, [(0, 1), (1, 0)])  160 us
    ppermute x87, starting transfers between devices, swap(): return lax.ppermute(value, axis, [(0, 1), (1, 0)])  64.6 us
    pallas_call x1, Pallas kernels, feed_forward(): pl.pallas_call(functools.partial(feed_forward_kernel, len(whole), len(spl...  51.7 us
    pallas_call x3, Pallas kernels, weight_grad(): pl.pallas_call(functools.partial(weight_grad_kernel, rows), grid_spec=plt...  42.1 us
    all_gather x1, waiting for transfers between devices, body(): ff_hi = lax.all_gather(ff_own, 'hi')  29.9 us
    pallas_call x1, Pallas kernels, attention_back(): pl.pallas_call(functools.partial(attention_back_kernel, len(da), len(n1),...  26.7 us
    pallas_call x1, Pallas kernels, attention(): pl.pallas_call(functools.partial(attention_kernel, len(n1), parts, rows),...  23.2 us
    all_gather x1, blocking collectives, body(): ff_lo_hi = [lax.all_gather(part, 'hi') for part in (ff_lo[:2], ff_lo[2])]  21.9 us
  transfers between devices with their start and end apart: 95, of which 35 were waited for; matrix products, arithmetic and copies ran while one was open for 18% of the time, Pallas kernels for 17%

profile of v2, /device:TPU:0, one launch (start us, length us, event | category | flops | bytes accessed | tf_op | source)
XLA Modules:
  0.0 640.1 jit_solution(14741119251530737167)
XLA Ops:
  26.0 9.1 %collective-permute-done.4.refs_11_ = bf16[192,1024]{1,0:T(8,128)(2,1)S(1)} collective-permute-done((bf16[192,1024]{1,0:T(8,128)(2,1)S(1)}, bf16[192,1024]{1,0:T(8,128)(2,1)S(1)}, u32[]{:S(2)}, u32[]{:S(2)}) %collective-permute-start.4) | collective-permute-done | bytes 393248 | tf_op jit(solution)/shard_map/ppermute | solution.py:82
  42.5 10.5 %collective-permute-done.8.refs_15_ = bf16[192,1024]{1,0:T(8,128)(2,1)S(1)} collective-permute-done((bf16[192,1024]{1,0:T(8,128)(2,1)S(1)}, bf16[192,1024]{1,0:T(8,128)(2,1)S(1)}, u32[]{:S(2)}, u32[]{:S(2)}) %collective-permute-start.8) | collective-permute-done | bytes 393248 | tf_op jit(solution)/shard_map/ppermute | solution.py:82
  53.5 6.8 %collective-permute-done.refs_1_.refs_7_ = bf16[256,1536]{1,0:T(8,128)(2,1)} collective-permute-done((bf16[256,1536]{1,0:T(8,128)(2,1)S(1)}, bf16[256,1536]{1,0:T(8,128)(2,1)}, u32[]{:S(2)}, u32[]{:S(2)}) %collective-permute-start) | collective-permute-done | bytes 786464 | tf_op jit(solution)/shard_map/ppermute | solution.py:82
  73.1 7.5 %collective-permute-done.12.refs_17_ = bf16[192,1024]{1,0:T(8,128)(2,1)} collective-permute-done((bf16[192,1024]{1,0:T(8,128)(2,1)}, bf16[192,1024]{1,0:T(8,128)(2,1)}, u32[]{:S(2)}, u32[]{:S(2)}) %collective-permute-start.12) | collective-permute-done | bytes 393248 | tf_op jit(solution)/shard_map/ppermute | solution.py:82
  84.1 23.2 %attention.1 = (bf16[1024,640]{1,0:T(8,128)(2,1)}, bf16[1024,384]{1,0:T(8,128)(2,1)}, f32[8,1024]{1,0:T(8,128)}, bf16[256,1536]{1,0:T(8,128)(2,1)}, bf16[128,153...) custom-call(s32[8]{0:T(128)} %stack.100.chips_ref, ...), custom_call_target="tpu_custom_call" | custom-call | flops 1179648 | bytes 4096 | tf_op jit(solution)/shard_map/attention/pallas_call | solution.py:308
  116.3 8.1 %collective-permute-done.20 = bf16[128,1536]{1,0:T(8,128)(2,1)S(1)} collective-permute-done((bf16[128,1536]{1,0:T(8,128)(2,1)S(1)}, bf16[128,1536]{1,0:T(8,128)(2,1)S(1)}, u32[]{:S(2)}, u32[]{:S(2)}) %collective-permute-start.20) | collective-permute-done | bytes 393248 | tf_op jit(solution)/shard_map/ppermute | solution.py:82
  124.4 6.5 %collective-permute-done.19 = bf16[128,1536]{1,0:T(8,128)(2,1)S(1)} collective-permute-done((bf16[128,1536]{1,0:T(8,128)(2,1)S(1)}, bf16[128,1536]{1,0:T(8,128)(2,1)S(1)}, u32[]{:S(2)}, u32[]{:S(2)}) %collective-permute-start.19) | collective-permute-done | bytes 393248 | tf_op jit(solution)/shard_map/ppermute | solution.py:82
  135.0 10.0 %collective-permute-done.25 = bf16[128,1536]{1,0:T(8,128)(2,1)S(1)} collective-permute-done((bf16[128,1536]{1,0:T(8,128)(2,1)}, bf16[128,1536]{1,0:T(8,128)(2,1)S(1)}, u32[]{:S(2)}, u32[]{:S(2)}) %collective-permute-start.25) | collective-permute-done | bytes 393248 | tf_op jit(solution)/shard_map/ppermute | solution.py:82
  145.3 29.9 %all-gather.11.cloned.1.call-done = bf16[6,192,1152]{2,1,0:T(8,128)(2,1)} async-done(((bf16[3,192,1152]{2,1,0:T(8,128)(2,1)}), bf16[6,192,1152]{2,1,0:T(8,128)(2,1)}) %all-gather.11.cloned.1.call-update) | async-done | bytes 2654224 | tf_op jit(solution)/shard_map/all_gather | solution.py:795
  205.8 10.4 %collective-permute-done.34 = bf16[128,1536]{1,0:T(8,128)(2,1)S(1)} collective-permute-done((bf16[128,1536]{1,0:T(8,128)(2,1)S(1)}, bf16[128,1536]{1,0:T(8,128)(2,1)S(1)}, u32[]{:S(2)}, u32[]{:S(2)}) %collective-permute-start.34) | collective-permute-done | bytes 393248 | tf_op jit(solution)/shard_map/ppermute | solution.py:82
  221.9 14.8 %all-gather.13.cloned.1.call-done = bf16[4,192,1152]{2,1,0:T(8,128)(2,1)} async-done(((bf16[2,192,1152]{2,1,0:T(8,128)(2,1)}), bf16[4,192,1152]{2,1,0:T(8,128)(2,1)}) %all-gather.13.cloned.1.call-update) | async-done | bytes 1769488 | tf_op jit(solution)/shard_map/all_gather | solution.py:837
  239.5 21.9 %all_gather.25 = bf16[2,192,1152]{2,1,0:T(8,128)(2,1)S(1)} all-gather(bf16[1,192,1152]{2,1,0:T(8,128)(2,1)} %slice.204), channel_id=1, replica_groups=mesh['hi'=2,'lo'=2,'yy'=2,'core'=2,'tensor'=2] {'hi'}, dimensions={0}, use_global_device_ids=true | all-gather | bytes 1327104 | tf_op jit(solution)/shard_map/all_gather | solution.py:837
  263.2 11.5 %collective-permute-done.35.refs_21_ = bf16[192,1152]{1,0:T(8,128)(2,1)} collective-permute-done((bf16[192,1152]{1,0:T(8,128)(2,1)}, bf16[192,1152]{1,0:T(8,128)(2,1)}, u32[]{:S(2)}, u32[]{:S(2)}) %collective-permute-start.35) | collective-permute-done | bytes 442400 | tf_op jit(solution)/shard_map/ppermute | solution.py:82
  274.6 51.7 %feed_forward.1 = (bf16[256,1536]{1,0:T(8,128)(2,1)}, bf16[256,1536]{1,0:T(8,128)(2,1)}, bf16[256,1536]{1,0:T(8,128)(2,1)}, bf16[256,1536]{1,0:T(8,128)(2,1)}, b...) custom-call(s32[8]{0:T(128)} %stack.104.chips_ref, ...), custom_call_target="tpu_custom_call" | custom-call | flops 8847360 | bytes 15360 | tf_op jit(solution)/shard_map/feed_forward/pallas_call | solution.py:518
  328.0 13.9 %weight_grad.3 = (bf16[2,2,192,1152]{3,2,1,0:T(8,128)(2,1)}, bf16[2,2,192,1152]{3,2,1,0:T(8,128)(2,1)}) custom-call(s32[3]{0:T(128)} %pad_add_fusion.1.place_ref, bf16[1536,2048]{1,0:T(8,128)(2,1)} %get-tuple-element.308.left_ref, bf16[2048,1152]{1,0:T(8,128)(2,1)} %get-tuple-element.327.right_ref.left_ref), custom_call_target="tpu_custom_call" | custom-call | flops 1769472 | bytes 4096 | tf_op jit(solution)/shard_map/weight_grad/pallas_call | solution.py:569
  352.7 14.1 %weight_grad.4 = (bf16[2,2,192,1152]{3,2,1,0:T(8,128)(2,1)}, bf16[2,2,192,1152]{3,2,1,0:T(8,128)(2,1)}) custom-call(s32[3]{0:T(128)} %pad_add_fusion.1.place_ref, bf16[1536,2048]{1,0:T(8,128)(2,1)} %get-tuple-element.355.left_ref, bf16[2048,1152]{1,0:T(8,128)(2,1)} %get-tuple-element.319.right_ref), custom_call_target="tpu_custom_call" | custom-call | flops 1769472 | bytes 4096 | tf_op jit(solution)/shard_map/weight_grad/pallas_call | solution.py:569
  373.9 14.1 %weight_grad.5 = (bf16[2,2,192,1152]{3,2,1,0:T(8,128)(2,1)}, bf16[2,2,192,1152]{3,2,1,0:T(8,128)(2,1)}) custom-call(s32[3]{0:T(128)} %pad_add_fusion.1.place_ref, bf16[1536,2048]{1,0:T(8,128)(2,1)} %get-tuple-element.355.left_ref, bf16[2048,1152]{1,0:T(8,128)(2,1)} %get-tuple-element.356.right_ref), custom_call_target="tpu_custom_call" | custom-call | flops 1769472 | bytes 4096 | tf_op jit(solution)/shard_map/weight_grad/pallas_call | solution.py:569
  399.2 16.0 %down.1 = (bf16[256,1536]{1,0:T(8,128)(2,1)}, bf16[256,1536]{1,0:T(8,128)(2,1)}, bf16[256,1536]{1,0:T(8,128)(2,1)}, bf16[256,1536]{1,0:T(8,128)(2,1)}, bf16[256,...) custom-call(bf16[2048,1152]{1,0:T(8,128)(2,1)} %get-tuple-element.327.right, ...), custom_call_target="tpu_custom_call" | custom-call | flops 1769472 | bytes 3584 | tf_op jit(solution)/shard_map/down/pallas_call | solution.py:602
  418.1 26.7 %attention_back.1 = (bf16[1024,640]{1,0:T(8,128)(2,1)}, f32[1,640]{1,0:T(1,128)}, bf16[256,1536]{1,0:T(8,128)(2,1)}, bf16[128,1536]{1,0:T(8,128)(2,1)}, bf16[128...) custom-call(s32[8]{0:T(128)} %stack.113.chips_ref, ...), custom_call_target="tpu_custom_call" | custom-call | flops 2555904 | bytes 6144 | tf_op jit(solution)/shard_map/attention_back/pallas_call | solution.py:400
  454.4 13.7 %collective-permute-done.56 = bf16[2,2,192,1152]{3,2,1,0:T(8,128)(2,1)} collective-permute-done((bf16[2,2,192,1152]{3,2,1,0:T(8,128)(2,1)}, bf16[2,2,192,1152]{3,2,1,0:T(8,128)(2,1)}, u32[]{:S(2)}, u32[]{:S(2)}) %collective-permute-start.56) | collective-permute-done | bytes 1769504 | tf_op jit(solution)/shard_map/ppermute | solution.py:82
  488.4 30.4 %collective-permute-done.60 = bf16[2,192,1024]{2,1,0:T(8,128)(2,1)S(1)} collective-permute-done((bf16[2,192,1024]{2,1,0:T(8,128)(2,1)S(1)}, bf16[2,192,1024]{2,1,0:T(8,128)(2,1)S(1)}, u32[]{:S(2)}, u32[]{:S(2)}) %collective-permute-start.60) | collective-permute-done | bytes 786464 | tf_op jit(solution)/shard_map/ppermute | solution.py:82
  520.4 6.9 %all-gather.9.cloned.1.call-done = bf16[2,2,192,1152]{3,2,1,0:T(8,128)(2,1)} async-done(((bf16[1,2,192,1152]{3,2,1,0:T(8,128)(2,1)}), bf16[2,2,192,1152]{3,2,1,0:T(8,128)(2,1)}) %all-gather.9.cloned.1.call-update) | async-done | bytes 1769488 | tf_op jit(solution)/shard_map/all_gather | solution.py:685
  545.8 9.6 %collective-permute-done.77 = bf16[192,1024]{1,0:T(8,128)(2,1)S(1)} collective-permute-done((bf16[192,1024]{1,0:T(8,128)(2,1)S(1)}, bf16[192,1024]{1,0:T(8,128)(2,1)S(1)}, u32[]{:S(2)}, u32[]{:S(2)}) %collective-permute-start.77) | collective-permute-done | bytes 393248 | tf_op jit(solution)/shard_map/ppermute | solution.py:108
  601.3 6.3 collective-permute-done.80
  (478 shorter events, 245.4 us)
Async XLA Ops:
  7.2 167.9 %all-gather.11.cloned.1.call-start = ((), (), s32[]{:S(2)}) async-start(), calls=%async_computation.2 | async-start | bytes 3981312 | tf_op jit(solution)/shard_map/all_gather | solution.py:795
  64.0 44.1 %collective-permute-start.17 = (bf16[3,192,1152]{2,1,0:T(8,128)(2,1)}, bf16[3,192,1152]{2,1,0:T(8,128)(2,1)}, u32[]{:S(2)}, u32[]{:S(2)}) collective-permute-start(bf16[3,192,1152]{2,1,0:T(8,128)(2,1)} %get-tuple-element.253), channel_id=1, source_target_pairs={{0,8},{8,0},{1,9},{9,1},{2,10},{10,2},{3,11},{11,3},{4,12},{12,4},... | collective-permute-start | bytes 3981320 | tf_op jit(solution)/shard_map/ppermute | solution.py:82
  80.7 30.4 %collective-permute-start.16 = (bf16[3,192,1152]{2,1,0:T(8,128)(2,1)S(1)}, bf16[3,192,1152]{2,1,0:T(8,128)(2,1)}, u32[]{:S(2)}, u32[]{:S(2)}) collective-permute-start(bf16[3,192,1152]{2,1,0:T(8,128)(2,1)S(1)} %get-tuple-element.252.refs_12_), channel_id=1, source_target_pairs={{0,4},{4,0},{1,5},{5,1},{2,6},{6,2},{3,7},{7,3},{8,12},{12,8},{9,1... | collective-permute-start | bytes 3981320 | tf_op jit(solution)/shard_map/ppermute | solution.py:82
  108.0 128.7 %all-gather.13.cloned.1.call-start = ((), (), s32[]{:S(2)}) async-start(), calls=%async_computation.3 | async-start | bytes 2654208 | tf_op jit(solution)/shard_map/all_gather | solution.py:837
  115.6 63.6 %collective-permute-start.23 = (bf16[3,192,1152]{2,1,0:T(8,128)(2,1)}, bf16[3,192,1152]{2,1,0:T(8,128)(2,1)}, u32[]{:S(2)}, u32[]{:S(2)}) collective-permute-start(bf16[3,192,1152]{2,1,0:T(8,128)(2,1)} %collective-permute-done.17.refs_13_), channel_id=1, source_target_pairs={{0,4},{4,0},{1,5},{5,1},{2,6},{6,2},{3,7},{7,3},{8,12},{12,8},{9,1... | collective-permute-start | bytes 3981320 | tf_op jit(solution)/shard_map/ppermute | solution.py:82
  116.0 65.5 %collective-permute-start.24 = (bf16[256,1536]{1,0:T(8,128)(2,1)}, bf16[256,1536]{1,0:T(8,128)(2,1)}, u32[]{:S(2)}, u32[]{:S(2)}) collective-permute-start(bf16[256,1536]{1,0:T(8,128)(2,1)} %refs_6_), channel_id=1, source_target_pairs={{0,8},{8,0},{1,9},{9,1},{2,10},{10,2},{3,11},{11,3},{4,12},{12,4},... | collective-permute-start | bytes 2359304 | tf_op jit(solution)/shard_map/ppermute | solution.py:82
  133.5 44.2 %collective-permute-start.26 = (bf16[128,1536]{1,0:T(8,128)(2,1)}, bf16[128,1536]{1,0:T(8,128)(2,1)}, u32[]{:S(2)}, u32[]{:S(2)}) collective-permute-start(bf16[128,1536]{1,0:T(8,128)(2,1)} %get-tuple-element.467), channel_id=1, source_target_pairs={{0,8},{8,0},{1,9},{9,1},{2,10},{10,2},{3,11},{11,3},{4,12},{12,4},... | collective-permute-start | bytes 1179656 | tf_op jit(solution)/shard_map/ppermute | solution.py:82
  133.6 48.0 %collective-permute-start.21 = (bf16[128,1536]{1,0:T(8,128)(2,1)}, bf16[128,1536]{1,0:T(8,128)(2,1)}, u32[]{:S(2)}, u32[]{:S(2)}) collective-permute-start(bf16[128,1536]{1,0:T(8,128)(2,1)} %get-tuple-element.467), channel_id=1, source_target_pairs={{0,1},{1,0},{2,3},{3,2},{4,5},{5,4},{6,7},{7,6},{8,9},{9,8},{10,11... | collective-permute-start | bytes 1179656 | tf_op jit(solution)/shard_map/ppermute | solution.py:82
  145.1 36.5 %collective-permute-start.22 = (bf16[128,1536]{1,0:T(8,128)(2,1)}, bf16[128,1536]{1,0:T(8,128)(2,1)}, u32[]{:S(2)}, u32[]{:S(2)}) collective-permute-start(bf16[128,1536]{1,0:T(8,128)(2,1)} %get-tuple-element.466), channel_id=1, source_target_pairs={{0,8},{8,0},{1,9},{9,1},{2,10},{10,2},{3,11},{11,3},{4,12},{12,4},... | collective-permute-start | bytes 1179656 | tf_op jit(solution)/shard_map/ppermute | solution.py:82
  189.8 264.5 %all-gather.7.cloned.1.call-start = ((), (), s32[]{:S(2)}) async-start(), calls=%async_computation | async-start | bytes 2654208 | tf_op jit(solution)/shard_map/all_gather | solution.py:685
  190.5 31.4 %collective-permute-start.32 = (bf16[3,192,1152]{2,1,0:T(8,128)(2,1)}, bf16[3,192,1152]{2,1,0:T(8,128)(2,1)}, u32[]{:S(2)}, u32[]{:S(2)}) collective-permute-start(bf16[3,192,1152]{2,1,0:T(8,128)(2,1)} %dynamic-slice_bitcast_fusion.refs_16_), channel_id=1, source_target_pairs={{0,4},{4,0},{1,5},{5,1},{2,6},{6,2},{3,7},{7,3},{8,12},{12,8},{9,1... | collective-permute-start | bytes 3981320 | tf_op jit(solution)/shard_map/ppermute | solution.py:82
  205.2 57.9 %collective-permute-start.37 = (bf16[256,1536]{1,0:T(8,128)(2,1)}, bf16[256,1536]{1,0:T(8,128)(2,1)}, u32[]{:S(2)}, u32[]{:S(2)}) collective-permute-start(bf16[256,1536]{1,0:T(8,128)(2,1)} %refs_6_), channel_id=1, source_target_pairs={{0,2},{2,0},{1,3},{3,1},{4,6},{6,4},{5,7},{7,5},{8,10},{10,8},{9,1... | collective-permute-start | bytes 2359304 | tf_op jit(solution)/shard_map/ppermute | solution.py:82
  205.2 57.9 %collective-permute-start.38 = (bf16[512,1536]{1,0:T(8,128)(2,1)}, bf16[512,1536]{1,0:T(8,128)(2,1)}, u32[]{:S(2)}, u32[]{:S(2)}) collective-permute-start(bf16[512,1536]{1,0:T(8,128)(2,1)} %constant_dynamic-update-slice_fusion.6.refs_7_), channel_id=1, source_target_pairs={{0,2},{2,0},{1,3},{3,1},{4,6},{6,4},{5,7},{7,5},{8,10},{10,8},{9,1... | collective-permute-start | bytes 4718600 | tf_op jit(solution)/shard_map/ppermute | solution.py:82
  217.7 45.5 %collective-permute-start.39 = (bf16[256,1536]{1,0:T(8,128)(2,1)}, bf16[256,1536]{1,0:T(8,128)(2,1)}, u32[]{:S(2)}, u32[]{:S(2)}) collective-permute-start(bf16[256,1536]{1,0:T(8,128)(2,1)} %constant_dynamic-update-slice_fusion.8.refs_8_), channel_id=1, source_target_pairs={{0,2},{2,0},{1,3},{3,1},{4,6},{6,4},{5,7},{7,5},{8,10},{10,8},{9,1... | collective-permute-start | bytes 2359304 | tf_op jit(solution)/shard_map/ppermute | solution.py:82
  352.1 41.9 %collective-permute-start.57 = (bf16[2,2,192,1152]{3,2,1,0:T(8,128)(2,1)}, bf16[2,2,192,1152]{3,2,1,0:T(8,128)(2,1)}, u32[]{:S(2)}, u32[]{:S(2)}) collective-permute-start(bf16[2,2,192,1152]{3,2,1,0:T(8,128)(2,1)} %get-tuple-element.359), channel_id=1, source_target_pairs={{0,4},{4,0},{1,5},{5,1},{2,6},{6,2},{3,7},{7,3},{8,12},{12,8},{9,1... | collective-permute-start | bytes 5308424 | tf_op jit(solution)/shard_map/ppermute | solution.py:82
  373.3 72.5 %collective-permute-start.70 = (bf16[2,2,192,1152]{3,2,1,0:T(8,128)(2,1)}, bf16[2,2,192,1152]{3,2,1,0:T(8,128)(2,1)}, u32[]{:S(2)}, u32[]{:S(2)}) collective-permute-start(bf16[2,2,192,1152]{3,2,1,0:T(8,128)(2,1)} %get-tuple-element.384), channel_id=1, source_target_pairs={{0,4},{4,0},{1,5},{5,1},{2,6},{6,2},{3,7},{7,3},{8,12},{12,8},{9,1... | collective-permute-start | bytes 5308424 | tf_op jit(solution)/shard_map/ppermute | solution.py:82
  396.3 131.0 %all-gather.9.cloned.1.call-start = ((), (), s32[]{:S(2)}) async-start(), calls=%async_computation.1 | async-start | bytes 2654208 | tf_op jit(solution)/shard_map/all_gather | solution.py:685
  415.9 52.1 %collective-permute-start.56 = (bf16[2,2,192,1152]{3,2,1,0:T(8,128)(2,1)}, bf16[2,2,192,1152]{3,2,1,0:T(8,128)(2,1)}, u32[]{:S(2)}, u32[]{:S(2)}) collective-permute-start(bf16[2,2,192,1152]{3,2,1,0:T(8,128)(2,1)} %get-tuple-element.358), channel_id=1, source_target_pairs={{0,4},{4,0},{1,5},{5,1},{2,6},{6,2},{3,7},{7,3},{8,12},{12,8},{9,1... | collective-permute-start | bytes 5308424 | tf_op jit(solution)/shard_map/ppermute | solution.py:82
  445.4 27.6 %collective-permute-start.55 = (bf16[2,192,1024]{2,1,0:T(8,128)(2,1)}, bf16[2,192,1024]{2,1,0:T(8,128)(2,1)}, u32[]{:S(2)}, u32[]{:S(2)}) collective-permute-start(bf16[2,192,1024]{2,1,0:T(8,128)(2,1)} %get-tuple-element.354), channel_id=1, source_target_pairs={{0,8},{8,0},{1,9},{9,1},{2,10},{10,2},{3,11},{11,3},{4,12},{12,4},... | collective-permute-start | bytes 2359304 | tf_op jit(solution)/shard_map/ppermute | solution.py:82
  445.8 28.9 %collective-permute-start.62 = (bf16[256,1536]{1,0:T(8,128)(2,1)}, bf16[256,1536]{1,0:T(8,128)(2,1)S(1)}, u32[]{:S(2)}, u32[]{:S(2)}) collective-permute-start(bf16[256,1536]{1,0:T(8,128)(2,1)} %get-tuple-element.372), channel_id=1, source_target_pairs={{0,2},{2,0},{1,3},{3,1},{4,6},{6,4},{5,7},{7,5},{8,10},{10,8},{9,1... | collective-permute-start | bytes 2359304 | tf_op jit(solution)/shard_map/ppermute | solution.py:82
  470.6 72.4 %collective-permute-start.78 = (bf16[2,192,1152]{2,1,0:T(8,128)(2,1)}, bf16[2,192,1152]{2,1,0:T(8,128)(2,1)}, u32[]{:S(2)}, u32[]{:S(2)}) collective-permute-start(bf16[2,192,1152]{2,1,0:T(8,128)(2,1)} %fusion.17), channel_id=1, source_target_pairs={{0,16},{16,0},{1,17},{17,1},{2,18},{18,2},{3,19},{19,3},{4,20},{20... | collective-permute-start | bytes 2654216 | tf_op jit(solution)/shard_map/ppermute | solution.py:108
  474.8 44.0 %collective-permute-start.60 = (bf16[2,192,1024]{2,1,0:T(8,128)(2,1)S(1)}, bf16[2,192,1024]{2,1,0:T(8,128)(2,1)S(1)}, u32[]{:S(2)}, u32[]{:S(2)}) collective-permute-start(bf16[2,192,1024]{2,1,0:T(8,128)(2,1)S(1)} %copy-done.83), channel_id=1, source_target_pairs={{0,8},{8,0},{1,9},{9,1},{2,10},{10,2},{3,11},{11,3},{4,12},{12,4},... | collective-permute-start | bytes 2359304 | tf_op jit(solution)/shard_map/ppermute | solution.py:82
  487.8 43.2 %collective-permute-start.69 = (bf16[192,1152]{1,0:T(8,128)(2,1)}, bf16[192,1152]{1,0:T(8,128)(2,1)}, u32[]{:S(2)}, u32[]{:S(2)}) collective-permute-start(bf16[192,1152]{1,0:T(8,128)(2,1)} %get-tuple-element.459), channel_id=1, source_target_pairs={{0,8},{8,0},{1,9},{9,1},{2,10},{10,2},{3,11},{11,3},{4,12},{12,4},... | collective-permute-start | bytes 1327112 | tf_op jit(solution)/shard_map/ppermute | solution.py:82
  576.2 41.6 %collective-permute-start.90 = (bf16[96,2304]{1,0:T(8,128)(2,1)}, bf16[96,2304]{1,0:T(8,128)(2,1)}, u32[]{:S(2)}, u32[]{:S(2)}) collective-permute-start(bf16[96,2304]{1,0:T(8,128)(2,1)} %get-tuple-element.449), channel_id=1, source_target_pairs={{0,2},{2,0},{1,3},{3,1},{4,6},{6,4},{5,7},{7,5},{8,10},{10,8},{9,1... | collective-permute-start | bytes 1327112 | tf_op jit(solution)/shard_map/ppermute | solution.py:82
  (155 other events, 1748.9 us)
Sparse Core Ops, SparseCore 0:
  108.1 67.0 all-gather.10
  190.0 46.6 all-gather.12
  396.4 47.8 all-gather.6
  448.7 78.6 all-gather.8

commit v3 on v2

--- a/solution.py
+++ b/solution.py
@@ -588,17 +588,21 @@
 
 
 def down_kernel(left_ref, right_ref, *out_refs):
+    step = pl.program_id(0)
     product = dot_abt(left_ref[...], right_ref[...]).astype(BF)
-    for j in range(8):
-
-        @pl.when(pl.program_id(0) == j)
-        def _(j=j):
-            out_refs[j][...] = product
+    for k, ref in enumerate(out_refs):
+
+        @pl.when((step % 2 == k % 2) & (step // 4 == k // 2))
+        def _(ref=ref):
+            ref[...] = product
 
 
 def down(left, right):
     length, width = left.shape
     one = length // 8
+    parts = [
+        pl.BlockSpec((one, D), lambda i, j=j: (jnp.clip((i - j) // 2, 0, 1), 0)) for j in (0, 0, 4, 4)
+    ]
     return pl.pallas_call(
         down_kernel,
         grid=(8,),
@@ -606,8 +610,8 @@
             pl.BlockSpec((one, width), lambda i: (i, 0)),
             pl.BlockSpec((D, width), lambda i: (0, 0)),
         ],
-        out_specs=[pl.BlockSpec((one, D), lambda i: (0, 0))] * 8,
-        out_shape=[jax.ShapeDtypeStruct((one, D), BF)] * 8,
+        out_specs=parts,
+        out_shape=[jax.ShapeDtypeStruct((2 * one, D), BF)] * 4,
         compiler_params=pltpu.CompilerParams(vmem_limit_bytes=VMEM_LIMIT),
         cost_estimate=cost(
             flops=2 * length * D * width, bytes_accessed=14 * 2**20, transcendentals=0
@@ -654,6 +658,29 @@
         )
 
 
+class BranchSum:
+    def __init__(self, near, by_x, core_near, core_by_x):
+        self.near, self.by_x = near, by_x
+        self.core = swap(core_by_x, "core"), swap(core_near, "core")
+
+    def along_x(self, order):
+        by_x, near = order.done(self.core)
+        self.near = total_of(self.near, near)
+        self.x = swap(total_of(self.by_x, by_x).astype(BF), "tensor")
+
+    def along_lo(self, order):
+        total = self.near + order.done(self.x).astype(F32)
+        half = total.shape[0] // 2
+        self.own = total[:half]
+        self.lo = swap(total[half:].astype(BF), "lo")
+
+    def arrived(self, order):
+        self.lo = order.done(self.lo)
+
+    def total(self):
+        return self.own + self.lo.astype(F32)
+
+
 class FourSum:
     def __init__(self, own, first, second, core_own, core_first, core_second):
         self.own, self.x = own, (first, second)
@@ -686,7 +713,6 @@
         else:
             self.every = None
             self.far = [turn(part, "hi", k + 1) for k, part in enumerate(far)]
-        order.mark = far
 
     def arrived(self, order):
         if self.every is None:
@@ -792,7 +818,6 @@
     ff_own = lax.dynamic_slice_in_dim(ff_shard, lo * FF_OWN, FF_OWN, 2)
     ff_theirs = lax.dynamic_slice_in_dim(ff_shard, (1 - lo) * FF_OWN, FF_OWN, 2)
     order.mark = ff_theirs
-    ff_hi = lax.all_gather(ff_own, "hi")
     att_lo = order.done(att_lo)
     att_lo_yy = swap(att_lo, "yy")
     att_yy = order.done(att_yy)
@@ -804,15 +829,16 @@
     att_hi_lo = order.done(att_hi_lo)
     att_hi_lo_yy = [swap(part, "yy") for part in att_hi_lo]
     ff_lo = swap(order.after(ff_theirs), "lo")
+    ff_hi = lax.all_gather(order.after(ff_own), "hi")
     n1_core = order.done(n1_core)
-    n1_x = order.done(n1_x)
-    n1_core_x = swap(n1_x, "core")
     other_ids = order.done(other_ids)
     angles, key_place, row_place, row_start = documents(core, place_x, segments, other_ids)
     sign = jnp.where(jnp.arange(HEAD_WIDTH) < HEAD_WIDTH // 2, -1.0, 1.0)
     tables = order.after((jnp.cos(angles), jnp.sin(angles) * sign, key_place, row_place, row_start))
     order.mark = tables[0]
     att_hi_yy = order.done(att_hi_yy)
+    n1_x = order.done(n1_x)
+    n1_core_x = swap(n1_x, "core")
     cot_x = swap(order.after(cotangent), "tensor")
     n1_core_x = order.done(n1_core_x)
     att_hi_lo_yy = order.done(att_hi_lo_yy)
@@ -834,45 +860,43 @@
     half = own_rows // 2
     cot_x = order.done(cot_x)
     ff_lo = order.done(ff_lo)
-    ff_lo_hi = [lax.all_gather(part, "hi") for part in (ff_lo[:2], ff_lo[2])]
+    ff_lo_hi_gu = lax.all_gather(ff_lo[:2], "hi")
     ff_yy = order.done(ff_yy)
     ff_lo_yy = swap(ff_lo, "yy")
     out.second(order)
-    cot_lo = swap(order.after(cotangent), "lo")
+    ff_hi = others_of(order.done(ff_hi))
+    order.mark = ff_hi
     residual = rows_in + out.total(order)
     scale_two = rms_scale(residual)
     n2 = (residual * scale_two * gain_two).astype(BF)
     n2_x_second, n2_lo_first = swap(n2[half:], "tensor"), swap(n2[:half], "lo")
     n2_x_first, n2_lo_second = swap(n2[:half], "tensor"), swap(n2[half:], "lo")
     order.mark = n2
-    ff_hi = others_of(order.done(ff_hi))
-    order.mark = ff_hi
+    ff_lo_yy = order.done(ff_lo_yy)
+    ff_hi_yy = [swap(order.after(part), "yy") for part in ff_hi]
     n2_x_second, n2_lo_first = order.done((n2_x_second, n2_lo_first))
     n2_both = swap(n2_lo_first, "tensor"), swap(n2_x_second, "lo")
-    ff_lo_yy, cot_lo = order.done((ff_lo_yy, cot_lo))
-    ff_hi_yy = [swap(order.after(part), "yy") for part in ff_hi]
     n2_x_first, n2_lo_second = order.done((n2_x_first, n2_lo_second))
     n2_near = jnp.concatenate([n2_x_first, n2_x_second, n2_lo_first, n2_lo_second])
-    n2_core_near = swap(n2_near, "core")
-    order.mark = n2_near
+    n2_core_near, n2_core = swap(n2_near, "core"), swap(n2, "core")
+    ff_lo_hi_gu = others_of(order.done(ff_lo_hi_gu))
     n2_both = jnp.concatenate(order.done(n2_both))
-    n2_core_both, n2_core = swap(n2_both, "core"), swap(n2, "core")
-    order.mark = n2_both
-    cot_both = swap(order.after(cot_lo[:half]), "tensor"), swap(order.after(cot_x[half:]), "lo")
-    n2_core_near, n2_core_both, n2_core = order.done((n2_core_near, n2_core_both, n2_core))
+    n2_core_near, n2_core = order.done((n2_core_near, n2_core))
+    n2_core_both = swap(n2_both, "core")
+    cot_lo = swap(order.after(cotangent), "lo")
+    ff_lo_hi_yy_gu = [swap(order.after(part), "yy") for part in ff_lo_hi_gu]
+    ff_lo_hi_d = [turn(order.after(ff_lo[2]), "hi", k) for k in steps]
+    ff_hi_yy = order.done(ff_hi_yy)
+    cot_lo = order.done(cot_lo)
+    cot_both = swap(cot_lo[:half], "tensor"), swap(cot_x[half:], "lo")
+    ff_lo_hi_d = order.done(ff_lo_hi_d)
+    ff_lo_hi_yy_d = [swap(part, "yy") for part in ff_lo_hi_d]
+    n2_core_both = order.done(n2_core_both)
     cot_both = order.done(cot_both)
     cot_parts = [cotangent, jnp.concatenate([cot_x, cot_lo]), jnp.concatenate(cot_both)]
     cot_parts += [swap(part, "core") for part in cot_parts]
-    order.mark = cot_parts[:3]
-    ff_hi_yy = order.done(ff_hi_yy)
-    ff_lo_hi_gu = others_of(order.done(ff_lo_hi[0]))
-    ff_lo_hi_yy_gu = [swap(part, "yy") for part in ff_lo_hi_gu]
-    order.mark = ff_lo_hi_gu
-    ff_lo_hi_d = others_of(order.done(ff_lo_hi[1]))
-    ff_lo_hi_yy_d = [swap(part, "yy") for part in ff_lo_hi_d]
-    order.mark = ff_lo_hi_d
+    ff_lo_hi_yy_gu = order.done(ff_lo_hi_yy_gu)
     cot_parts = order.done(cot_parts)
-    ff_lo_hi_yy_gu = order.done(ff_lo_hi_yy_gu)
     ff_lo_hi_yy_d = order.done(ff_lo_hi_yy_d)
     n2_parts = [n2, n2_near, n2_both, n2_core, n2_core_near, n2_core_both]
 
@@ -931,6 +955,7 @@
     order.mark = da
     branch_parts = down(*order.after((hidden, w_down)))
     order.mark = branch_parts[0]
+    branch = BranchSum(*branch_parts)
     da_x = order.done(da_x)
     da_core_x = [swap(part, "core") for part in da_x]
     da_core, da_core_x = order.done((da_core, da_core_x))
@@ -946,33 +971,36 @@
         tables,
     )
     order.mark = bias_grad
+    d_sum.arrived(order)
     g_sum.across(order, True)
     dn1 = FourSum(*parts[:6])
     att = ChipSum(*parts[6:])
     dn1.second(order)
-    d_sum.arrived(order)
+    norm_one_in, gain_one_grad = norm_backward(rows_in, scale_one, gain_one, dn1.total(order))
     u_sum.across(order, False)
     att.far_yy(order)
-    norm_one_in, gain_one_grad = norm_backward(rows_in, scale_one, gain_one, dn1.total(order))
-    order.mark = gain_one_grad
+    bias_grad = order.after(bias_grad)[0]
+    bias_slots = lax.dynamic_update_slice_in_dim(
+        jnp.zeros_like(bias_all), bias_grad[:Q_COLS], q_at, 0
+    )
+    bias_slots = lax.dynamic_update_slice_in_dim(bias_slots, bias_grad[Q_COLS:], kv_at, 0)
     att.far_hi(order)
+    branch.along_x(order)
     d_low, d_way = summed_up(d_sum)
-    input_grad = residual_grad + norm_one_in
-    att.near_yy(order)
-    branch = EightSum(order.after(branch_parts))
     g_sum.arrived(order)
     g_low, g_way = summed_up(g_sum)
-    d_rows = own_rows_of(d_low, d_way)
-    branch.second(order)
+    att.near_yy(order)
+    input_grad = residual_grad + norm_one_in
+    branch.along_lo(order)
     u_sum.arrived(order)
-    u_low, u_way = summed_up(u_sum)
     att_sum = att.total(order)
     att_low = att_sum.astype(BF)
     other_att = swap(rows_of(att_low, 1 - core, 0), "core")
-    order.mark = att_low
+    u_low, u_way = summed_up(u_sum)
+    other_att = order.done(other_att)
+    d_rows = own_rows_of(d_low, d_way)
     g_rows = own_rows_of(g_low, g_way)
-    branch.third(order)
-    other_att = order.done(other_att)
+    branch.arrived(order)
 
     own_att = rows_of(att_low, core, 0)
     first_att = jnp.where(core == 0, own_att, other_att).astype(F32)
@@ -983,26 +1011,21 @@
     owned_squares = (
         jnp.sum(qkv_owned * qkv_owned) + jnp.sum(out_owned * out_owned) + ff_squares
     )
-    bias_grad = order.after(bias_grad)[0]
-    bias_slots = lax.dynamic_update_slice_in_dim(
-        jnp.zeros_like(bias_all), bias_grad[:Q_COLS], q_at, 0
-    )
-    bias_slots = lax.dynamic_update_slice_in_dim(bias_slots, bias_grad[Q_COLS:], kv_at, 0)
     summed = jnp.concatenate(
         [gain_one_grad, gain_two_grad, bias_slots, jnp.full((128,), owned_squares)]
     )
-    first = summed + order.done(swap(summed, "core"))
-    order.mark = first
-    u_rows = own_rows_of(u_low, u_way)
-    summed = first + order.done(swap(first, "tensor"))
+    summed = summed + order.done(swap(summed, "core"))
+    summed = summed + order.done(swap(summed, "tensor"))
     summed = summed + order.done(swap(summed, "yy"))
-    block_out = (residual + branch.total(order)).astype(BF)
     summed = summed + order.done(swap(summed, "lo"))
     step = 1
     while step < hi_count:
         moved = lax.ppermute(summed, "hi", [(i, i ^ step) for i in range(hi_count)])
         summed = summed + order.done(moved)
         step *= 2
+    order.mark = summed
+    u_rows = own_rows_of(u_low, u_way)
+    block_out = (residual + order.after(branch.total())).astype(BF)
 
     def owned(rows):
         mine, other = rows

time: 646 us -> 655 us (1.014)
  waiting for transfers between devices: 226 us -> 249 us
  blocking collectives: 21.9 us -> 0 us
  other arithmetic: 86.4 us -> 99.9 us
  starting transfers between devices: 70.1 us -> 62.1 us
    all_gather x2, waiting for transfers between devices: 6.88 us -> 55.1 us  [across(): self.every = [lax.all_gather(part, 'hi') for part in far]]
    all_gather x1 -> x0, blocking collectives: 21.9 us -> none  [body(): ff_lo_hi = [lax.all_gather(part, 'hi') for part in (ff_lo[:2], ff_lo[2])]]
    all_gather x2, waiting for transfers between devices: 44.7 us -> 27 us  [the longest x1 17.1 us: body(): ff_lo_hi_gu = lax.all_gather(ff_lo[:2], 'hi')]
    ppermute x3 -> x4, waiting for transfers between devices: 14.7 us -> 0.01 us  [turn(): lax.ppermute(value, axis, [(i, (i + steps) % count) for i in range(count)])]
    ppermute x87 -> x81, starting transfers between devices: 64.6 us -> 53.4 us  [swap(): return lax.ppermute(value, axis, [(0, 1), (1, 0)])]
    ppermute x87 -> x81, waiting for transfers between devices: 160 us -> 164 us  [swap(): return lax.ppermute(value, axis, [(0, 1), (1, 0)])]
    unnamed x174 -> x166, local copies, waits for them, and re-layouts: 14.1 us -> 15.3 us
  transfers between devices with their start and end apart: 95 -> 90, of which waited for: 35 -> 31; matrix products, arithmetic and copies ran while one was open for 18% -> 20% of each run, Pallas kernels for 17% -> 17%
where the time goes in v3:
time: 655 us; the launch traced here: 649 us
  waiting for transfers between devices  249 us (38%)
  Pallas kernels  163 us (25%)
  other arithmetic  99.9 us (15%)
  starting transfers between devices  62.1 us (9%)
  local copies, waits for them, and re-layouts  54.1 us (8%)
  between operations  20.9 us (3%)
    ppermute x81, waiting for transfers between devices, swap(): return lax.ppermute(value, axis, [(0, 1), (1, 0)])  164 us
    all_gather x2, waiting for transfers between devices, across(): self.every = [lax.all_gather(part, 'hi') for part in far]  55.1 us
    ppermute x81, starting transfers between devices, swap(): return lax.ppermute(value, axis, [(0, 1), (1, 0)])  53.4 us
    pallas_call x1, Pallas kernels, feed_forward(): pl.pallas_call(functools.partial(feed_forward_kernel, len(whole), len(spl...  51.6 us
    pallas_call x3, Pallas kernels, weight_grad(): pl.pallas_call(functools.partial(weight_grad_kernel, rows), grid_spec=plt...  42.2 us
    pallas_call x1, Pallas kernels, attention_back(): pl.pallas_call(functools.partial(attention_back_kernel, len(da), len(n1),...  26.9 us
    pallas_call x1, Pallas kernels, attention(): pl.pallas_call(functools.partial(attention_kernel, len(n1), parts, rows),...  23.3 us
    all_gather x1, waiting for transfers between devices, body(): ff_lo_hi_gu = lax.all_gather(ff_lo[:2], 'hi')  17.1 us
  transfers between devices with their start and end apart: 90, of which 31 were waited for; matrix products, arithmetic and copies ran while one was open for 20% of the time, Pallas kernels for 17%

profile of v3, /device:TPU:0, one launch (start us, length us, event | category | flops | bytes accessed | tf_op | source)
XLA Modules:
  0.0 648.9 jit_solution(16228048730861671577)
XLA Ops:
  27.9 12.4 %collective-permute-done.4.refs_11_ = bf16[192,1024]{1,0:T(8,128)(2,1)} collective-permute-done((bf16[192,1024]{1,0:T(8,128)(2,1)S(1)}, bf16[192,1024]{1,0:T(8,128)(2,1)}, u32[]{:S(2)}, u32[]{:S(2)}) %collective-permute-start.4) | collective-permute-done | bytes 393248 | tf_op jit(solution)/shard_map/ppermute | solution.py:82
  44.8 9.9 %collective-permute-done.10.refs_15_ = bf16[192,1024]{1,0:T(8,128)(2,1)S(1)} collective-permute-done((bf16[192,1024]{1,0:T(8,128)(2,1)}, bf16[192,1024]{1,0:T(8,128)(2,1)S(1)}, u32[]{:S(2)}, u32[]{:S(2)}) %collective-permute-start.10) | collective-permute-done | bytes 393248 | tf_op jit(solution)/shard_map/ppermute | solution.py:82
  66.8 9.2 %collective-permute-done.12.refs_17_ = bf16[192,1024]{1,0:T(8,128)(2,1)} collective-permute-done((bf16[192,1024]{1,0:T(8,128)(2,1)}, bf16[192,1024]{1,0:T(8,128)(2,1)}, u32[]{:S(2)}, u32[]{:S(2)}) %collective-permute-start.12) | collective-permute-done | bytes 393248 | tf_op jit(solution)/shard_map/ppermute | solution.py:82
  78.4 23.3 %attention.1 = (bf16[1024,640]{1,0:T(8,128)(2,1)}, bf16[1024,384]{1,0:T(8,128)(2,1)}, f32[8,1024]{1,0:T(8,128)}, bf16[256,1536]{1,0:T(8,128)(2,1)}, bf16[128,153...) custom-call(s32[8]{0:T(128)} %stack.100.chips_ref, ...), custom_call_target="tpu_custom_call" | custom-call | flops 1179648 | bytes 4096 | tf_op jit(solution)/shard_map/attention/pallas_call | solution.py:308
  102.3 16.2 %collective-permute-done.17.refs_13_ = bf16[3,192,1152]{2,1,0:T(8,128)(2,1)} collective-permute-done((bf16[3,192,1152]{2,1,0:T(8,128)(2,1)}, bf16[3,192,1152]{2,1,0:T(8,128)(2,1)}, u32[]{:S(2)}, u32[]{:S(2)}) %collective-permute-start.17) | collective-permute-done | bytes 1327136 | tf_op jit(solution)/shard_map/ppermute | solution.py:82
  123.2 9.9 %all-gather.11.cloned.1.call-done = bf16[6,192,1152]{2,1,0:T(8,128)(2,1)} async-done(((bf16[3,192,1152]{2,1,0:T(8,128)(2,1)}), bf16[6,192,1152]{2,1,0:T(8,128)(2,1)}) %all-gather.11.cloned.1.call-update) | async-done | bytes 2654224 | tf_op jit(solution)/shard_map/all_gather | solution.py:832
  155.4 5.8 collective-permute-done.21
  161.2 5.7 collective-permute-done.22
  180.1 17.1 %all-gather.13.cloned.1.call-done = bf16[4,192,1152]{2,1,0:T(8,128)(2,1)} async-done(((bf16[2,192,1152]{2,1,0:T(8,128)(2,1)}), bf16[4,192,1152]{2,1,0:T(8,128)(2,1)}) %all-gather.13.cloned.1.call-update) | async-done | bytes 1769488 | tf_op jit(solution)/shard_map/all_gather | solution.py:863
  207.0 27.8 %collective-permute-done.32 = bf16[256,1536]{1,0:T(8,128)(2,1)S(1)} collective-permute-done((bf16[256,1536]{1,0:T(8,128)(2,1)S(1)}, bf16[256,1536]{1,0:T(8,128)(2,1)S(1)}, u32[]{:S(2)}, u32[]{:S(2)}) %collective-permute-start.32) | collective-permute-done | bytes 786464 | tf_op jit(solution)/shard_map/ppermute | solution.py:82
  249.2 14.5 %collective-permute-done.40.refs_19_ = bf16[2,192,1152]{2,1,0:T(8,128)(2,1)} collective-permute-done((bf16[2,192,1152]{2,1,0:T(8,128)(2,1)}, bf16[2,192,1152]{2,1,0:T(8,128)(2,1)}, u32[]{:S(2)}, u32[]{:S(2)}) %collective-permute-start.40) | collective-permute-done | bytes 884768 | tf_op jit(solution)/shard_map/ppermute | solution.py:82
  263.7 8.5 %collective-permute-done.34.refs_21_ = bf16[192,1152]{1,0:T(8,128)(2,1)} collective-permute-done((bf16[192,1152]{1,0:T(8,128)(2,1)}, bf16[192,1152]{1,0:T(8,128)(2,1)}, u32[]{:S(2)}, u32[]{:S(2)}) %collective-permute-start.34) | collective-permute-done | bytes 442400 | tf_op jit(solution)/shard_map/ppermute | solution.py:82
  272.2 51.6 %feed_forward.1 = (bf16[256,1536]{1,0:T(8,128)(2,1)}, bf16[256,1536]{1,0:T(8,128)(2,1)}, bf16[256,1536]{1,0:T(8,128)(2,1)}, bf16[256,1536]{1,0:T(8,128)(2,1)}, b...) custom-call(s32[8]{0:T(128)} %stack.104.chips_ref, ...), custom_call_target="tpu_custom_call" | custom-call | flops 8847360 | bytes 15360 | tf_op jit(solution)/shard_map/feed_forward/pallas_call | solution.py:518
  325.6 14.1 %weight_grad.3 = (bf16[2,2,192,1152]{3,2,1,0:T(8,128)(2,1)}, bf16[2,2,192,1152]{3,2,1,0:T(8,128)(2,1)}) custom-call(s32[3]{0:T(128)} %pad_add_fusion.1.place_ref, bf16[1536,2048]{1,0:T(8,128)(2,1)} %get-tuple-element.293.left_ref, bf16[2048,1152]{1,0:T(8,128)(2,1)} %get-tuple-element.317.right_ref.left_ref), custom_call_target="tpu_custom_call" | custom-call | flops 1769472 | bytes 4096 | tf_op jit(solution)/shard_map/weight_grad/pallas_call | solution.py:569
  351.5 14.1 %weight_grad.4 = (bf16[2,2,192,1152]{3,2,1,0:T(8,128)(2,1)}, bf16[2,2,192,1152]{3,2,1,0:T(8,128)(2,1)}) custom-call(s32[3]{0:T(128)} %pad_add_fusion.1.place_ref, bf16[1536,2048]{1,0:T(8,128)(2,1)} %get-tuple-element.311.left_ref, bf16[2048,1152]{1,0:T(8,128)(2,1)} %get-tuple-element.304.right_ref), custom_call_target="tpu_custom_call" | custom-call | flops 1769472 | bytes 4096 | tf_op jit(solution)/shard_map/weight_grad/pallas_call | solution.py:569
  370.6 14.0 %weight_grad.5 = (bf16[2,2,192,1152]{3,2,1,0:T(8,128)(2,1)}, bf16[2,2,192,1152]{3,2,1,0:T(8,128)(2,1)}) custom-call(s32[3]{0:T(128)} %pad_add_fusion.1.place_ref, bf16[1536,2048]{1,0:T(8,128)(2,1)} %get-tuple-element.311.left_ref, bf16[2048,1152]{1,0:T(8,128)(2,1)} %get-tuple-element.312.right_ref), custom_call_target="tpu_custom_call" | custom-call | flops 1769472 | bytes 4096 | tf_op jit(solution)/shard_map/weight_grad/pallas_call | solution.py:569
  398.2 15.5 %down.1 = (bf16[512,1536]{1,0:T(8,128)(2,1)}, bf16[512,1536]{1,0:T(8,128)(2,1)}, bf16[512,1536]{1,0:T(8,128)(2,1)}, bf16[512,1536]{1,0:T(8,128)(2,1)}) custom-call(bf16[2048,1152]{1,0:T(8,128)(2,1)} %get-tuple-element.317.right_ref.left_ref, bf16[1536,1152]{1,0:T(8,128)(2,1)} %get-tuple-element.318.right_ref), custom_call_target="tpu_custom_call" | custom-call | flops 1769472 | bytes 3584 | tf_op jit(solution)/shard_map/down/pallas_call | solution.py:606
  416.9 26.9 %attention_back.1 = (bf16[1024,640]{1,0:T(8,128)(2,1)}, f32[1,640]{1,0:T(1,128)}, bf16[256,1536]{1,0:T(8,128)(2,1)}, bf16[128,1536]{1,0:T(8,128)(2,1)}, bf16[128...) custom-call(s32[8]{0:T(128)} %stack.113.chips_ref, ...), custom_call_target="tpu_custom_call" | custom-call | flops 2555904 | bytes 6144 | tf_op jit(solution)/shard_map/attention_back/pallas_call | solution.py:400
  455.4 7.3 %collective-permute-done.64 = bf16[128,1536]{1,0:T(8,128)(2,1)S(1)} collective-permute-done((bf16[128,1536]{1,0:T(8,128)(2,1)S(1)}, bf16[128,1536]{1,0:T(8,128)(2,1)S(1)}, u32[]{:S(2)}, u32[]{:S(2)}) %collective-permute-start.64) | collective-permute-done | bytes 393248 | tf_op jit(solution)/shard_map/ppermute | solution.py:82
  466.8 6.5 %collective-permute-done.65 = bf16[128,1536]{1,0:T(8,128)(2,1)} collective-permute-done((bf16[128,1536]{1,0:T(8,128)(2,1)}, bf16[128,1536]{1,0:T(8,128)(2,1)}, u32[]{:S(2)}, u32[]{:S(2)}) %collective-permute-start.65) | collective-permute-done | bytes 393248 | tf_op jit(solution)/shard_map/ppermute | solution.py:82
  501.6 55.1 %all-gather.9.cloned.1.call-done = bf16[2,2,192,1152]{3,2,1,0:T(8,128)(2,1)} async-done(((bf16[1,2,192,1152]{3,2,1,0:T(8,128)(2,1)}), bf16[2,2,192,1152]{3,2,1,0:T(8,128)(2,1)}) %all-gather.9.cloned.1.call-update) | async-done | bytes 1769488 | tf_op jit(solution)/shard_map/all_gather | solution.py:712
  588.4 5.7 collective-permute-done.70
  603.0 7.8 %collective-permute-done.81 = f32[5248]{0:T(1024)S(1)} collective-permute-done((f32[5248]{0:T(1024)S(1)}, f32[5248]{0:T(1024)S(1)}, u32[]{:S(2)}, u32[]{:S(2)}) %collective-permute-start.81) | collective-permute-done | bytes 21024 | tf_op jit(solution)/shard_map/ppermute | solution.py:82
  626.3 5.8 divide_subtract_fusion.1
  (453 shorter events, 243.3 us)
Async XLA Ops:
  7.2 125.9 %all-gather.11.cloned.1.call-start = ((), (), s32[]{:S(2)}) async-start(), calls=%async_computation.2 | async-start | bytes 3981312 | tf_op jit(solution)/shard_map/all_gather | solution.py:832
  65.0 132.1 %all-gather.13.cloned.1.call-start = ((), (), s32[]{:S(2)}) async-start(), calls=%async_computation.3 | async-start | bytes 2654208 | tf_op jit(solution)/shard_map/all_gather | solution.py:863
  65.3 53.3 %collective-permute-start.17 = (bf16[3,192,1152]{2,1,0:T(8,128)(2,1)}, bf16[3,192,1152]{2,1,0:T(8,128)(2,1)}, u32[]{:S(2)}, u32[]{:S(2)}) collective-permute-start(bf16[3,192,1152]{2,1,0:T(8,128)(2,1)} %get-tuple-element.238), channel_id=1, source_target_pairs={{0,8},{8,0},{1,9},{9,1},{2,10},{10,2},{3,11},{11,3},{4,12},{12,4},... | collective-permute-start | bytes 3981320 | tf_op jit(solution)/shard_map/ppermute | solution.py:82
  75.9 42.6 %collective-permute-start.16 = (bf16[3,192,1152]{2,1,0:T(8,128)(2,1)S(1)}, bf16[3,192,1152]{2,1,0:T(8,128)(2,1)}, u32[]{:S(2)}, u32[]{:S(2)}) collective-permute-start(bf16[3,192,1152]{2,1,0:T(8,128)(2,1)S(1)} %copy-done.3), channel_id=1, source_target_pairs={{0,4},{4,0},{1,5},{5,1},{2,6},{6,2},{3,7},{7,3},{8,12},{12,8},{9,1... | collective-permute-start | bytes 3981320 | tf_op jit(solution)/shard_map/ppermute | solution.py:82
  102.3 33.4 %collective-permute-start.13 = (bf16[256,1536]{1,0:T(8,128)(2,1)}, bf16[256,1536]{1,0:T(8,128)(2,1)}, u32[]{:S(2)}, u32[]{:S(2)}) collective-permute-start(bf16[256,1536]{1,0:T(8,128)(2,1)} %get-tuple-element.232), channel_id=1, source_target_pairs={{0,2},{2,0},{1,3},{3,1},{4,6},{6,4},{5,7},{7,5},{8,10},{10,8},{9,1... | collective-permute-start | bytes 2359304 | tf_op jit(solution)/shard_map/ppermute | solution.py:82
  122.9 27.7 %collective-permute-start.25 = (bf16[3,192,1152]{2,1,0:T(8,128)(2,1)}, bf16[3,192,1152]{2,1,0:T(8,128)(2,1)}, u32[]{:S(2)}, u32[]{:S(2)}) collective-permute-start(bf16[3,192,1152]{2,1,0:T(8,128)(2,1)} %collective-permute-done.17.refs_13_), channel_id=1, source_target_pairs={{0,4},{4,0},{1,5},{5,1},{2,6},{6,2},{3,7},{7,3},{8,12},{12,8},{9,1... | collective-permute-start | bytes 3981320 | tf_op jit(solution)/shard_map/ppermute | solution.py:82
  148.3 296.1 %all-gather.7.cloned.1.call-start = ((), (), s32[]{:S(2)}) async-start(), calls=%async_computation | async-start | bytes 2654208 | tf_op jit(solution)/shard_map/all_gather | solution.py:712
  173.0 27.6 %collective-permute-start.28 = (bf16[512,1536]{1,0:T(8,128)(2,1)}, bf16[512,1536]{1,0:T(8,128)(2,1)}, u32[]{:S(2)}, u32[]{:S(2)}) collective-permute-start(bf16[512,1536]{1,0:T(8,128)(2,1)} %constant_dynamic-update-slice_fusion.refs_1_), channel_id=1, source_target_pairs={{0,2},{2,0},{1,3},{3,1},{4,6},{6,4},{5,7},{7,5},{8,10},{10,8},{9,1... | collective-permute-start | bytes 4718600 | tf_op jit(solution)/shard_map/ppermute | solution.py:82
  175.9 31.1 %collective-permute-start.33 = (bf16[3,192,1152]{2,1,0:T(8,128)(2,1)}, bf16[3,192,1152]{2,1,0:T(8,128)(2,1)}, u32[]{:S(2)}, u32[]{:S(2)}) collective-permute-start(bf16[3,192,1152]{2,1,0:T(8,128)(2,1)} %dynamic-slice_bitcast_fusion.refs_16_), channel_id=1, source_target_pairs={{0,4},{4,0},{1,5},{5,1},{2,6},{6,2},{3,7},{7,3},{8,12},{12,8},{9,1... | collective-permute-start | bytes 3981320 | tf_op jit(solution)/shard_map/ppermute | solution.py:82
  197.1 44.6 %collective-permute-start.36 = (bf16[128,1536]{1,0:T(8,128)(2,1)}, bf16[128,1536]{1,0:T(8,128)(2,1)S(1)}, u32[]{:S(2)}, u32[]{:S(2)}) collective-permute-start(bf16[128,1536]{1,0:T(8,128)(2,1)} %slice.192), channel_id=1, source_target_pairs={{0,8},{8,0},{1,9},{9,1},{2,10},{10,2},{3,11},{11,3},{4,12},{12,4},... | collective-permute-start | bytes 1179656 | tf_op jit(solution)/shard_map/ppermute | solution.py:82
  200.5 34.3 %collective-permute-start.32 = (bf16[256,1536]{1,0:T(8,128)(2,1)S(1)}, bf16[256,1536]{1,0:T(8,128)(2,1)S(1)}, u32[]{:S(2)}, u32[]{:S(2)}) collective-permute-start(bf16[256,1536]{1,0:T(8,128)(2,1)S(1)} %copy-done.6), channel_id=1, source_target_pairs={{0,8},{8,0},{1,9},{9,1},{2,10},{10,2},{3,11},{11,3},{4,12},{12,4},... | collective-permute-start | bytes 2359304 | tf_op jit(solution)/shard_map/ppermute | solution.py:82
  202.6 37.4 %collective-permute-start.30 = (bf16[256,1536]{1,0:T(8,128)(2,1)S(1)}, bf16[256,1536]{1,0:T(8,128)(2,1)S(1)}, u32[]{:S(2)}, u32[]{:S(2)}) collective-permute-start(bf16[256,1536]{1,0:T(8,128)(2,1)S(1)} %constant_dynamic-update-slice_fusion.4.refs_2_), channel_id=1, source_target_pairs={{0,2},{2,0},{1,3},{3,1},{4,6},{6,4},{5,7},{7,5},{8,10},{10,8},{9,1... | collective-permute-start | bytes 2359304 | tf_op jit(solution)/shard_map/ppermute | solution.py:82
  204.1 35.4 %collective-permute-start.31 = (bf16[192,1152]{1,0:T(8,128)(2,1)S(1)}, bf16[192,1152]{1,0:T(8,128)(2,1)}, u32[]{:S(2)}, u32[]{:S(2)}) collective-permute-start(bf16[192,1152]{1,0:T(8,128)(2,1)S(1)} %slice_bitcast_fusion.7), channel_id=1, source_target_pairs={{0,16},{16,0},{1,17},{17,1},{2,18},{18,2},{3,19},{19,3},{4,20},{20... | collective-permute-start | bytes 1327112 | tf_op jit(solution)/shard_map/ppermute | solution.py:108
  339.6 45.0 %collective-permute-start.51 = (bf16[2,2,192,1152]{3,2,1,0:T(8,128)(2,1)}, bf16[2,2,192,1152]{3,2,1,0:T(8,128)(2,1)}, u32[]{:S(2)}, u32[]{:S(2)}) collective-permute-start(bf16[2,2,192,1152]{3,2,1,0:T(8,128)(2,1)} %get-tuple-element.309), channel_id=1, source_target_pairs={{0,4},{4,0},{1,5},{5,1},{2,6},{6,2},{3,7},{7,3},{8,12},{12,8},{9,1... | collective-permute-start | bytes 5308424 | tf_op jit(solution)/shard_map/ppermute | solution.py:82
  365.6 82.1 %collective-permute-start.63 = (bf16[2,2,192,1152]{3,2,1,0:T(8,128)(2,1)}, bf16[2,2,192,1152]{3,2,1,0:T(8,128)(2,1)}, u32[]{:S(2)}, u32[]{:S(2)}) collective-permute-start(bf16[2,2,192,1152]{3,2,1,0:T(8,128)(2,1)} %get-tuple-element.342), channel_id=1, source_target_pairs={{0,4},{4,0},{1,5},{5,1},{2,6},{6,2},{3,7},{7,3},{8,12},{12,8},{9,1... | collective-permute-start | bytes 5308424 | tf_op jit(solution)/shard_map/ppermute | solution.py:82
  391.4 165.3 %all-gather.9.cloned.1.call-start = ((), (), s32[]{:S(2)}) async-start(), calls=%async_computation.1 | async-start | bytes 2654208 | tf_op jit(solution)/shard_map/all_gather | solution.py:712
  415.4 57.9 %collective-permute-start.60 = (bf16[2,2,192,1152]{3,2,1,0:T(8,128)(2,1)}, bf16[2,2,192,1152]{3,2,1,0:T(8,128)(2,1)}, u32[]{:S(2)}, u32[]{:S(2)}) collective-permute-start(bf16[2,2,192,1152]{3,2,1,0:T(8,128)(2,1)} %get-tuple-element.338), channel_id=1, source_target_pairs={{0,4},{4,0},{1,5},{5,1},{2,6},{6,2},{3,7},{7,3},{8,12},{12,8},{9,1... | collective-permute-start | bytes 5308424 | tf_op jit(solution)/shard_map/ppermute | solution.py:82
  416.2 75.4 %collective-permute-start.52 = (bf16[512,1536]{1,0:T(8,128)(2,1)}, bf16[512,1536]{1,0:T(8,128)(2,1)}, u32[]{:S(2)}, u32[]{:S(2)}) collective-permute-start(bf16[512,1536]{1,0:T(8,128)(2,1)} %get-tuple-element.320), channel_id=1, source_target_pairs={{0,2},{2,0},{1,3},{3,1},{4,6},{6,4},{5,7},{7,5},{8,10},{10,8},{9,1... | collective-permute-start | bytes 4718600 | tf_op jit(solution)/shard_map/ppermute | solution.py:82
  455.4 36.2 %collective-permute-start.53 = (bf16[512,1536]{1,0:T(8,128)(2,1)}, bf16[512,1536]{1,0:T(8,128)(2,1)}, u32[]{:S(2)}, u32[]{:S(2)}) collective-permute-start(bf16[512,1536]{1,0:T(8,128)(2,1)} %get-tuple-element.321), channel_id=1, source_target_pairs={{0,2},{2,0},{1,3},{3,1},{4,6},{6,4},{5,7},{7,5},{8,10},{10,8},{9,1... | collective-permute-start | bytes 4718600 | tf_op jit(solution)/shard_map/ppermute | solution.py:82
  478.2 81.5 %collective-permute-start.69 = (bf16[2,192,1024]{2,1,0:T(8,128)(2,1)}, bf16[2,192,1024]{2,1,0:T(8,128)(2,1)}, u32[]{:S(2)}, u32[]{:S(2)}) collective-permute-start(bf16[2,192,1024]{2,1,0:T(8,128)(2,1)} %get-tuple-element.361), channel_id=1, source_target_pairs={{0,8},{8,0},{1,9},{9,1},{2,10},{10,2},{3,11},{11,3},{4,12},{12,4},... | collective-permute-start | bytes 2359304 | tf_op jit(solution)/shard_map/ppermute | solution.py:82
  480.9 88.2 %collective-permute-start.75 = (bf16[2,192,1152]{2,1,0:T(8,128)(2,1)}, bf16[2,192,1152]{2,1,0:T(8,128)(2,1)}, u32[]{:S(2)}, u32[]{:S(2)}) collective-permute-start(bf16[2,192,1152]{2,1,0:T(8,128)(2,1)} %fusion.17), channel_id=1, source_target_pairs={{0,16},{16,0},{1,17},{17,1},{2,18},{18,2},{3,19},{19,3},{4,20},{20... | collective-permute-start | bytes 2654216 | tf_op jit(solution)/shard_map/ppermute | solution.py:108
  494.7 69.2 %collective-permute-start.68 = (bf16[512,1536]{1,0:T(8,128)(2,1)}, bf16[512,1536]{1,0:T(8,128)(2,1)}, u32[]{:S(2)}, u32[]{:S(2)}) collective-permute-start(bf16[512,1536]{1,0:T(8,128)(2,1)} %add_convert_fusion), channel_id=1, source_target_pairs={{0,1},{1,0},{2,3},{3,2},{4,5},{5,4},{6,7},{7,6},{8,9},{9,8},{10,11... | collective-permute-start | bytes 4718600 | tf_op jit(solution)/shard_map/ppermute | solution.py:82
  498.1 82.2 %collective-permute-start.72 = (bf16[192,1152]{1,0:T(8,128)(2,1)}, bf16[192,1152]{1,0:T(8,128)(2,1)}, u32[]{:S(2)}, u32[]{:S(2)}) collective-permute-start(bf16[192,1152]{1,0:T(8,128)(2,1)} %get-tuple-element.429), channel_id=1, source_target_pairs={{0,8},{8,0},{1,9},{9,1},{2,10},{10,2},{3,11},{11,3},{4,12},{12,4},... | collective-permute-start | bytes 1327112 | tf_op jit(solution)/shard_map/ppermute | solution.py:82
  498.7 72.1 %collective-permute-start.74 = (bf16[192,1024]{1,0:T(8,128)(2,1)}, bf16[192,1024]{1,0:T(8,128)(2,1)}, u32[]{:S(2)}, u32[]{:S(2)}) collective-permute-start(bf16[192,1024]{1,0:T(8,128)(2,1)} %bitcast.34), channel_id=1, source_target_pairs={{0,16},{16,0},{1,17},{17,1},{2,18},{18,2},{3,19},{19,3},{4,20},{20... | collective-permute-start | bytes 1179656 | tf_op jit(solution)/shard_map/ppermute | solution.py:108
  (146 other events, 1699.7 us)
Sparse Core Ops, SparseCore 0:
  65.2 67.9 all-gather.10
  148.4 48.6 all-gather.12
  391.5 48.7 all-gather.6
  466.9 89.6 all-gather.8

commit v4 on v3

--- a/solution.py
+++ b/solution.py
@@ -426,68 +426,117 @@
     )(chips, *da, *n1, qkv, o, lse, weight, *tables)
 
 
-def feed_forward_kernel(whole, split, rows, chips_ref, *refs):
-    n2_refs, dy_refs, refs = refs[:6], refs[6:12], refs[12:]
-    pieces, refs = refs[: whole + 2 * split], refs[whole + 2 * split :]
-    dn2_refs, refs = refs[:8], refs[8:]
-    u_ref, dgate_ref, dup_ref, n2_t_ref, dy_t_ref, down_ref, *refs = refs
-    gu_w, d_w, tiles, tile_sems, sems, out_sem = refs
-    step = pl.program_id(0)
-    steps = pl.num_programs(0)
-    one = tiles.shape[2]
-
-    def copies():
-        for i in range(whole + split):
-            at = pl.ds(pl.multiple_of(chips_ref[i] * rows, rows), rows)
-            for j in range(3):
-                if i < whole or j < 2:
-                    here = pieces[i].at[j]
-                else:
-                    here = pieces[i + split]
-                if j < 2:
-                    there = gu_w.at[at, pl.ds(j * FF_OWN, FF_OWN)]
-                else:
-                    there = d_w.at[at, :]
-                yield pltpu.make_async_copy(here, there, sems.at[i, j])
-
-    def tile_copies(j):
-        part, row = divmod(j, 4)
-        ref, at = ((0, 0), (1, 0), (1, one), (2, 0))[row]
-        for k, taken in enumerate((n2_refs, dy_refs)):
-            yield pltpu.make_async_copy(
-                taken[3 * part + ref].at[pl.ds(at, one), :],
-                tiles.at[j % 2, k],
-                tile_sems.at[j % 2, k],
-            )
-
-    save = pltpu.make_async_copy(d_w, down_ref, out_sem)
-
-    @pl.when(step == 0)
-    def _():
-        for copy in copies():
-            copy.start()
-        for copy in tile_copies(0):
-            copy.start()
-        for copy in copies():
-            copy.wait()
-        save.start()
-
+def tile_copies(j, taken, tiles, sems, one):
+    part, row = divmod(j, 4)
+    ref, at = ((0, 0), (1, 0), (1, one), (2, 0))[row]
+    return pltpu.make_async_copy(
+        taken[3 * part + ref].at[pl.ds(at, one), :], tiles.at[j % 2], sems.at[j % 2]
+    )
+
+
+def take_tile(step, taken, tiles, sems, one):
     for j in range(8):
 
         @pl.when(step == j)
         def _(j=j):
             if j < 7:
-                for copy in tile_copies(j + 1):
-                    copy.start()
-            for copy in tile_copies(j):
-                copy.wait()
-
-    n2, dy = tiles[step % 2, 0], tiles[step % 2, 1]
+                tile_copies(j + 1, taken, tiles, sems, one).start()
+            tile_copies(j, taken, tiles, sems, one).wait()
+
+
+def weight_copies(pieces, chips_ref, rows, wide, there, sems):
+    for i, piece in enumerate(pieces):
+        at = pl.ds(pl.multiple_of(chips_ref[i] * rows, rows), rows)
+        for j in range(wide):
+            here = piece if piece.ndim == 2 else piece.at[j if wide > 1 else 2]
+            yield pltpu.make_async_copy(
+                here, there.at[at, pl.ds(j * FF_OWN, FF_OWN)], sems.at[i, j]
+            )
+
+
+def gate_up_kernel(count, rows, chips_ref, *refs):
+    n2_refs, pieces, refs = refs[:6], refs[6 : 6 + count], refs[6 + count :]
+    gate_up_ref, n2_t_ref, weights, tiles, tile_sems, sems = refs
+    step = pl.program_id(0)
+    one = tiles.shape[1]
+    copies = list(weight_copies(pieces, chips_ref, rows, 2, weights, sems))
+
+    @pl.when(step == 0)
+    def _():
+        for copy in copies:
+            copy.start()
+        tile_copies(0, n2_refs, tiles, tile_sems, one).start()
+        for copy in copies:
+            copy.wait()
+
+    take_tile(step, n2_refs, tiles, tile_sems, one)
+    n2 = tiles[step % 2]
     n2_t_ref[...] = n2.T
+    gate_up_ref[...] = dot_ab(n2, weights[...]).astype(BF)
+
+
+def gate_up(chips, n2, pieces):
+    rows = pieces[0].shape[1]
+    one = n2[0].shape[0]
+    length = 8 * one
+    return pl.pallas_call(
+        functools.partial(gate_up_kernel, len(pieces), rows),
+        grid_spec=pltpu.PrefetchScalarGridSpec(
+            num_scalar_prefetch=1,
+            grid=(8,),
+            in_specs=[ANYWHERE] * (6 + len(pieces)),
+            out_specs=[
+                pl.BlockSpec((one, 2 * FF_OWN), lambda i, c: (i, 0)),
+                pl.BlockSpec((D, one), lambda i, c: (0, i)),
+            ],
+            scratch_shapes=[
+                pltpu.VMEM((D, 2 * FF_OWN), BF),
+                pltpu.VMEM((2, one, D), BF),
+                pltpu.SemaphoreType.DMA((2,)),
+                pltpu.SemaphoreType.DMA((len(pieces), 2)),
+            ],
+        ),
+        out_shape=[
+            jax.ShapeDtypeStruct((length, 2 * FF_OWN), BF),
+            jax.ShapeDtypeStruct((D, length), BF),
+        ],
+        compiler_params=pltpu.CompilerParams(vmem_limit_bytes=VMEM_LIMIT),
+        cost_estimate=cost(
+            flops=4 * length * D * FF_OWN, bytes_accessed=30 * 2**20, transcendentals=0
+        ),
+        name="gate_up",
+    )(chips, *n2, *pieces)
+
+
+def feed_forward_kernel(count, rows, chips_ref, gate_up_ref, *refs):
+    dy_refs, refs = refs[:6], refs[6:]
+    gu_pieces, d_pieces, refs = refs[:count], refs[count : 2 * count], refs[2 * count :]
+    dn2_refs, refs = refs[:8], refs[8:]
+    u_ref, dgate_ref, dup_ref, dy_t_ref, down_ref, *refs = refs
+    gu_w, d_w, tiles, tile_sems, gu_sems, d_sems, out_sem = refs
+    step = pl.program_id(0)
+    one = tiles.shape[1]
+    gu_copies = list(weight_copies(gu_pieces, chips_ref, rows, 2, gu_w, gu_sems))
+    d_copies = list(weight_copies(d_pieces, chips_ref, rows, 1, d_w, d_sems))
+    save = pltpu.make_async_copy(d_w, down_ref, out_sem)
+
+    @pl.when(step == 0)
+    def _():
+        for copy in d_copies:
+            copy.start()
+        tile_copies(0, dy_refs, tiles, tile_sems, one).start()
+        for copy in gu_copies:
+            copy.start()
+        for copy in d_copies:
+            copy.wait()
+        save.start()
+
+    take_tile(step, dy_refs, tiles, tile_sems, one)
+    dy = tiles[step % 2]
     dy_t_ref[...] = dy.T
-    gate_up = dot_ab(n2, gu_w[...])
     du = dot_ab(dy, d_w[...])
-    gate, up = gate_up[:, :FF_OWN], gate_up[:, FF_OWN:]
+    gate = gate_up_ref[:, :FF_OWN].astype(F32)
+    up = gate_up_ref[:, FF_OWN:].astype(F32)
     sig = jax.nn.sigmoid(gate)
     silu = gate * sig
     u_ref[...] = (silu * up).astype(BF)
@@ -495,6 +544,12 @@
     dgate = (du * up * sig * (1.0 + gate * (1.0 - sig))).astype(BF)
     dup_ref[...] = dup
     dgate_ref[...] = dgate
+
+    @pl.when(step == 0)
+    def _():
+        for copy in gu_copies:
+            copy.wait()
+
     dn2 = dot_abt(jnp.concatenate([dgate, dup], axis=1), gu_w[...]).astype(BF)
     for j in range(8):
 
@@ -502,47 +557,48 @@
         def _(j=j):
             dn2_refs[j][...] = dn2
 
-    @pl.when(step == steps - 1)
+    @pl.when(step == pl.num_programs(0) - 1)
     def _():
         save.wait()
 
 
-def feed_forward(chips, n2, dy, whole, split):
-    rows = whole[0].shape[1]
-    one = n2[0].shape[0]
+def feed_forward(chips, gates, dy, gu_pieces, d_pieces):
+    count = len(d_pieces)
+    rows = d_pieces[0].shape[-2]
+    one = dy[0].shape[0]
     length = 8 * one
     tile = lambda width: pl.BlockSpec((one, width), lambda i, c: (i, 0))
-    turned = pl.BlockSpec((D, one), lambda i, c: (0, i))
     kept = pl.BlockSpec((one, D), lambda i, c: (0, 0))
-    parts = len(whole) + len(split)
     return pl.pallas_call(
-        functools.partial(feed_forward_kernel, len(whole), len(split), rows),
+        functools.partial(feed_forward_kernel, count, rows),
         grid_spec=pltpu.PrefetchScalarGridSpec(
             num_scalar_prefetch=1,
             grid=(8,),
-            in_specs=[ANYWHERE] * (12 + len(whole) + 2 * len(split)),
-            out_specs=[kept] * 8 + [tile(FF_OWN)] * 3 + [turned, turned, ANYWHERE],
+            in_specs=[tile(2 * FF_OWN)] + [ANYWHERE] * (6 + 2 * count),
+            out_specs=[kept] * 8
+            + [tile(FF_OWN)] * 3
+            + [pl.BlockSpec((D, one), lambda i, c: (0, i)), ANYWHERE],
             scratch_shapes=[
                 pltpu.VMEM((D, 2 * FF_OWN), BF),
                 pltpu.VMEM((D, FF_OWN), BF),
-                pltpu.VMEM((2, 2, one, D), BF),
-                pltpu.SemaphoreType.DMA((2, 2)),
-                pltpu.SemaphoreType.DMA((parts, 3)),
+                pltpu.VMEM((2, one, D), BF),
+                pltpu.SemaphoreType.DMA((2,)),
+                pltpu.SemaphoreType.DMA((count, 2)),
+                pltpu.SemaphoreType.DMA((count, 1)),
                 pltpu.SemaphoreType.DMA,
             ],
         ),
         out_shape=[jax.ShapeDtypeStruct((one, D), BF)] * 8
         + [jax.ShapeDtypeStruct((length, FF_OWN), BF)] * 3
-        + [jax.ShapeDtypeStruct((D, length), BF)] * 2
-        + [jax.ShapeDtypeStruct((D, FF_OWN), BF)],
+        + [jax.ShapeDtypeStruct((D, length), BF), jax.ShapeDtypeStruct((D, FF_OWN), BF)],
         compiler_params=pltpu.CompilerParams(vmem_limit_bytes=VMEM_LIMIT),
         cost_estimate=cost(
-            flops=2 * 5 * length * D * FF_OWN,
-            bytes_accessed=60 * 2**20,
+            flops=6 * length * D * FF_OWN,
+            bytes_accessed=50 * 2**20,
             transcendentals=length * FF_OWN,
         ),
         name="feed_forward",
-    )(chips, *n2, *dy, *whole, *[gu for gu, _ in split], *[d for _, d in split])
+    )(chips, gates, *dy, *gu_pieces, *d_pieces)
 
 
 def weight_grad_kernel(rows, place_ref, left_ref, right_ref, *refs):
@@ -691,7 +747,6 @@
         core_x = order.done(self.core_x)
         by_x = [total_of(*pair).astype(BF) for pair in zip(self.x, core_x)]
         self.x = [swap(part, "tensor") for part in by_x]
-        order.mark = by_x
 
     def total(self, order):
         self.core_own = order.done(self.core_own)
@@ -889,23 +944,30 @@
     ff_hi_yy = order.done(ff_hi_yy)
     cot_lo = order.done(cot_lo)
     cot_both = swap(cot_lo[:half], "tensor"), swap(cot_x[half:], "lo")
+    cot_near = jnp.concatenate([cot_x, cot_lo])
+    cot_core, cot_core_near = swap(order.after(cotangent), "core"), swap(cot_near, "core")
+    n2_core_both = order.done(n2_core_both)
     ff_lo_hi_d = order.done(ff_lo_hi_d)
     ff_lo_hi_yy_d = [swap(part, "yy") for part in ff_lo_hi_d]
-    n2_core_both = order.done(n2_core_both)
-    cot_both = order.done(cot_both)
-    cot_parts = [cotangent, jnp.concatenate([cot_x, cot_lo]), jnp.concatenate(cot_both)]
-    cot_parts += [swap(part, "core") for part in cot_parts]
     ff_lo_hi_yy_gu = order.done(ff_lo_hi_yy_gu)
-    cot_parts = order.done(cot_parts)
-    ff_lo_hi_yy_d = order.done(ff_lo_hi_yy_d)
     n2_parts = [n2, n2_near, n2_both, n2_core, n2_core_near, n2_core_both]
 
     whole = [ff_own, ff_lo, ff_yy, ff_lo_yy, *ff_hi, *ff_hi_yy]
-    split = [*zip(ff_lo_hi_gu, ff_lo_hi_d), *zip(ff_lo_hi_yy_gu, ff_lo_hi_yy_d)]
+    gu_pieces = [*whole, *ff_lo_hi_gu, *ff_lo_hi_yy_gu]
     ff_chips = [chip_at(0, l, y) for y in (0, 1) for l in (0, 1)]
     ff_chips += [chip_at(-k, l, y) for l in (0, 1) for y in (0, 1) for k in steps]
-    *dn2_parts, hidden, gate_grad, up_grad, n2_t, cot_t, w_down = feed_forward(
-        jnp.stack(ff_chips).astype(jnp.int32), order.after(n2_parts), cot_parts, whole, split
+    ff_chips = jnp.stack(ff_chips).astype(jnp.int32)
+    gates, n2_t = gate_up(ff_chips, order.after(n2_parts), gu_pieces)
+    order.mark = gates
+    cot_both = jnp.concatenate(order.done(cot_both))
+    cot_core_both = swap(cot_both, "core")
+    cot_core, cot_core_near = order.done((cot_core, cot_core_near))
+    ff_lo_hi_yy_d = order.done(ff_lo_hi_yy_d)
+    cot_core_both = order.done(cot_core_both)
+    cot_parts = [cotangent, cot_near, cot_both, cot_core, cot_core_near, cot_core_both]
+    d_pieces = [*whole, *ff_lo_hi_d, *ff_lo_hi_yy_d]
+    *dn2_parts, hidden, gate_grad, up_grad, cot_t, w_down = feed_forward(
+        ff_chips, gates, order.after(cot_parts), gu_pieces, d_pieces
     )
     order.mark = w_down
 
@@ -959,6 +1021,7 @@
     da_x = order.done(da_x)
     da_core_x = [swap(part, "core") for part in da_x]
     da_core, da_core_x = order.done((da_core, da_core_x))
+    g_sum.across(order, False)
 
     _, bias_grad, *parts = attention_back(
         sum_order(),
@@ -972,10 +1035,10 @@
     )
     order.mark = bias_grad
     d_sum.arrived(order)
-    g_sum.across(order, True)
     dn1 = FourSum(*parts[:6])
     att = ChipSum(*parts[6:])
     dn1.second(order)
+    g_sum.arrived(order)
     norm_one_in, gain_one_grad = norm_backward(rows_in, scale_one, gain_one, dn1.total(order))
     u_sum.across(order, False)
     att.far_yy(order)
@@ -987,7 +1050,6 @@
     att.far_hi(order)
     branch.along_x(order)
     d_low, d_way = summed_up(d_sum)
-    g_sum.arrived(order)
     g_low, g_way = summed_up(g_sum)
     att.near_yy(order)
     input_grad = residual_grad + norm_one_in

time: 655 us -> 640 us (0.977)
  waiting for transfers between devices: 249 us -> 235 us
  Pallas kernels: 163 us -> 173 us
  other arithmetic: 99.9 us -> 91.3 us
    all_gather x2 -> x1, waiting for transfers between devices: 55.1 us -> 0.01 us  [across(): self.every = [lax.all_gather(part, 'hi') for part in far]]
    ppermute x4 -> x5, waiting for transfers between devices: 0.01 us -> 44.1 us  [turn(): lax.ppermute(value, axis, [(i, (i + steps) % count) for i in range(count)])]
    pallas_call x1 -> x2, Pallas kernels: 51.6 us -> 61.5 us  [the longest x1 39.8 us: feed_forward(): pl.pallas_call(functools.partial(feed_forward_kernel, count, rows), grid_...]
    unnamed x166 -> x188, local copies, waits for them, and re-layouts: 15.3 us -> 18.6 us
  transfers between devices with their start and end apart: 90 -> 90, of which waited for: 31 -> 29; matrix products, arithmetic and copies ran while one was open for 20% -> 19% of each run, Pallas kernels for 17% -> 21%
where the time goes in v4:
time: 640 us; the launch traced here: 634 us
  waiting for transfers between devices  235 us (37%)
  Pallas kernels  173 us (27%)
  other arithmetic  91.3 us (14%)
  starting transfers between devices  57.4 us (9%)
  local copies, waits for them, and re-layouts  56 us (9%)
  between operations  21 us (3%)
    ppermute x81, waiting for transfers between devices, swap(): return lax.ppermute(value, axis, [(0, 1), (1, 0)])  160 us
    ppermute x81, starting transfers between devices, swap(): return lax.ppermute(value, axis, [(0, 1), (1, 0)])  49 us
    ppermute x5, waiting for transfers between devices, turn(): lax.ppermute(value, axis, [(i, (i + steps) % count) for i in range(count)])  44.1 us
    pallas_call x3, Pallas kernels, weight_grad(): pl.pallas_call(functools.partial(weight_grad_kernel, rows), grid_spec=plt...  42.3 us
    pallas_call x1, Pallas kernels, feed_forward(): pl.pallas_call(functools.partial(feed_forward_kernel, count, rows), grid_...  39.8 us
    pallas_call x1, Pallas kernels, attention_back(): pl.pallas_call(functools.partial(attention_back_kernel, len(da), len(n1),...  26.9 us
    pallas_call x1, Pallas kernels, attention(): pl.pallas_call(functools.partial(attention_kernel, len(n1), parts, rows),...  23.3 us
    pallas_call x1, Pallas kernels, gate_up(): pl.pallas_call(functools.partial(gate_up_kernel, len(pieces), rows), grid...  21.8 us
  transfers between devices with their start and end apart: 90, of which 29 were waited for; matrix products, arithmetic and copies ran while one was open for 19% of the time, Pallas kernels for 21%

profile of v4, /device:TPU:0, one launch (start us, length us, event | category | flops | bytes accessed | tf_op | source)
XLA Modules:
  0.0 633.7 jit_solution(10025505503050994490)
XLA Ops:
  27.6 12.7 %collective-permute-done.4.refs_11_ = bf16[192,1024]{1,0:T(8,128)(2,1)} collective-permute-done((bf16[192,1024]{1,0:T(8,128)(2,1)S(1)}, bf16[192,1024]{1,0:T(8,128)(2,1)}, u32[]{:S(2)}, u32[]{:S(2)}) %collective-permute-start.4) | collective-permute-done | bytes 393248 | tf_op jit(solution)/shard_map/ppermute | solution.py:82
  44.9 9.9 %collective-permute-done.10.refs_15_ = bf16[192,1024]{1,0:T(8,128)(2,1)S(1)} collective-permute-done((bf16[192,1024]{1,0:T(8,128)(2,1)}, bf16[192,1024]{1,0:T(8,128)(2,1)S(1)}, u32[]{:S(2)}, u32[]{:S(2)}) %collective-permute-start.10) | collective-permute-done | bytes 393248 | tf_op jit(solution)/shard_map/ppermute | solution.py:82
  67.7 8.4 %collective-permute-done.12.refs_17_ = bf16[192,1024]{1,0:T(8,128)(2,1)} collective-permute-done((bf16[192,1024]{1,0:T(8,128)(2,1)}, bf16[192,1024]{1,0:T(8,128)(2,1)}, u32[]{:S(2)}, u32[]{:S(2)}) %collective-permute-start.12) | collective-permute-done | bytes 393248 | tf_op jit(solution)/shard_map/ppermute | solution.py:82
  78.5 23.3 %attention.1 = (bf16[1024,640]{1,0:T(8,128)(2,1)}, bf16[1024,384]{1,0:T(8,128)(2,1)}, f32[8,1024]{1,0:T(8,128)}, bf16[256,1536]{1,0:T(8,128)(2,1)}, bf16[128,153...) custom-call(s32[8]{0:T(128)} %stack.100.chips_ref, ...), custom_call_target="tpu_custom_call" | custom-call | flops 1179648 | bytes 4096 | tf_op jit(solution)/shard_map/attention/pallas_call | solution.py:308
  102.4 16.3 %collective-permute-done.17.refs_7_.refs_15_ = bf16[3,192,1152]{2,1,0:T(8,128)(2,1)} collective-permute-done((bf16[3,192,1152]{2,1,0:T(8,128)(2,1)}, bf16[3,192,1152]{2,1,0:T(8,128)(2,1)}, u32[]{:S(2)}, u32[]{:S(2)}) %collective-permute-start.17) | collective-permute-done | bytes 1327136 | tf_op jit(solution)/shard_map/ppermute | solution.py:82
  123.7 9.6 %all-gather.8.cloned.1.call-done = bf16[6,192,1152]{2,1,0:T(8,128)(2,1)} async-done(((bf16[3,192,1152]{2,1,0:T(8,128)(2,1)}), bf16[6,192,1152]{2,1,0:T(8,128)(2,1)}) %all-gather.8.cloned.1.call-update) | async-done | bytes 2654224 | tf_op jit(solution)/shard_map/all_gather | solution.py:887
  178.7 19.1 %all-gather.10.cloned.1.call-done = bf16[4,192,1152]{2,1,0:T(8,128)(2,1)} async-done(((bf16[2,192,1152]{2,1,0:T(8,128)(2,1)}), bf16[4,192,1152]{2,1,0:T(8,128)(2,1)}) %all-gather.10.cloned.1.call-update) | async-done | bytes 1769488 | tf_op jit(solution)/shard_map/all_gather | solution.py:918
  207.8 27.4 %collective-permute-done.31 = bf16[256,1536]{1,0:T(8,128)(2,1)S(1)} collective-permute-done((bf16[256,1536]{1,0:T(8,128)(2,1)}, bf16[256,1536]{1,0:T(8,128)(2,1)S(1)}, u32[]{:S(2)}, u32[]{:S(2)}) %collective-permute-start.31) | collective-permute-done | bytes 786464 | tf_op jit(solution)/shard_map/ppermute | solution.py:82
  240.9 21.8 %gate_up.1 = (bf16[2048,2304]{1,0:T(8,128)(2,1)}, bf16[1536,2048]{1,0:T(8,128)(2,1)}) custom-call(s32[8]{0:T(128)} %stack.104.chips_ref, bf16[256,1536]{1,0:T(8,128)(2,1)} %multiply_convert_fusion.refs_0_, bf16[512,1536]{1,0:T(8,128)(2,1)} %constant_dynamic-update-slice_fusion.refs_1_, bf16[256,1536]{1,0:T(8,128)(2,1)} %copy-done.27, ...), custom_call_target="tpu_custom_call" | custom-call | flops 3538944 | bytes 7680 | tf_op jit(solution)/shard_map/gate_up/pallas_call | solution.py:482
  265.9 11.8 %collective-permute-done.40.refs_21_ = bf16[192,1152]{1,0:T(8,128)(2,1)} collective-permute-done((bf16[192,1152]{1,0:T(8,128)(2,1)}, bf16[192,1152]{1,0:T(8,128)(2,1)}, u32[]{:S(2)}, u32[]{:S(2)}) %collective-permute-start.40) | collective-permute-done | bytes 442400 | tf_op jit(solution)/shard_map/ppermute | solution.py:82
  277.7 39.8 %feed_forward.1 = (bf16[256,1536]{1,0:T(8,128)(2,1)}, bf16[256,1536]{1,0:T(8,128)(2,1)}, bf16[256,1536]{1,0:T(8,128)(2,1)}, bf16[256,1536]{1,0:T(8,128)(2,1)}, b...) custom-call(s32[8]{0:T(128)} %stack.104.chips_ref, ...), custom_call_target="tpu_custom_call" | custom-call | flops 5308416 | bytes 12800 | tf_op jit(solution)/shard_map/feed_forward/pallas_call | solution.py:572
  319.2 14.1 %weight_grad.3 = (bf16[2,2,192,1152]{3,2,1,0:T(8,128)(2,1)}, bf16[2,2,192,1152]{3,2,1,0:T(8,128)(2,1)}) custom-call(s32[3]{0:T(128)} %pad_add_fusion.1.place_ref, bf16[1536,2048]{1,0:T(8,128)(2,1)} %get-tuple-element.303.left_ref, bf16[2048,1152]{1,0:T(8,128)(2,1)} %get-tuple-element.327.right_ref.left_ref), custom_call_target="tpu_custom_call" | custom-call | flops 1769472 | bytes 4096 | tf_op jit(solution)/shard_map/weight_grad/pallas_call | solution.py:625
  344.6 14.1 %weight_grad.4 = (bf16[2,2,192,1152]{3,2,1,0:T(8,128)(2,1)}, bf16[2,2,192,1152]{3,2,1,0:T(8,128)(2,1)}) custom-call(s32[3]{0:T(128)} %pad_add_fusion.1.place_ref, bf16[1536,2048]{1,0:T(8,128)(2,1)} %get-tuple-element.321.left_ref, bf16[2048,1152]{1,0:T(8,128)(2,1)} %get-tuple-element.314.right_ref), custom_call_target="tpu_custom_call" | custom-call | flops 1769472 | bytes 4096 | tf_op jit(solution)/shard_map/weight_grad/pallas_call | solution.py:625
  363.6 14.1 %weight_grad.5 = (bf16[2,2,192,1152]{3,2,1,0:T(8,128)(2,1)}, bf16[2,2,192,1152]{3,2,1,0:T(8,128)(2,1)}) custom-call(s32[3]{0:T(128)} %pad_add_fusion.1.place_ref, bf16[1536,2048]{1,0:T(8,128)(2,1)} %get-tuple-element.321.left_ref, bf16[2048,1152]{1,0:T(8,128)(2,1)} %get-tuple-element.322.right_ref), custom_call_target="tpu_custom_call" | custom-call | flops 1769472 | bytes 4096 | tf_op jit(solution)/shard_map/weight_grad/pallas_call | solution.py:625
  390.1 15.5 %down.1 = (bf16[512,1536]{1,0:T(8,128)(2,1)}, bf16[512,1536]{1,0:T(8,128)(2,1)}, bf16[512,1536]{1,0:T(8,128)(2,1)}, bf16[512,1536]{1,0:T(8,128)(2,1)}) custom-call(bf16[2048,1152]{1,0:T(8,128)(2,1)} %get-tuple-element.327.right_ref.left_ref, bf16[1536,1152]{1,0:T(8,128)(2,1)} %get-tuple-element.328.right_ref), custom_call_target="tpu_custom_call" | custom-call | flops 1769472 | bytes 3584 | tf_op jit(solution)/shard_map/down/pallas_call | solution.py:662
  412.9 26.9 %attention_back.1 = (bf16[1024,640]{1,0:T(8,128)(2,1)}, f32[1,640]{1,0:T(1,128)}, bf16[256,1536]{1,0:T(8,128)(2,1)}, bf16[128,1536]{1,0:T(8,128)(2,1)}, bf16[128...) custom-call(s32[8]{0:T(128)} %stack.113.chips_ref, ...), custom_call_target="tpu_custom_call" | custom-call | flops 2555904 | bytes 6144 | tf_op jit(solution)/shard_map/attention_back/pallas_call | solution.py:400
  447.8 35.7 %collective-permute-done.67 = bf16[2,192,1152]{2,1,0:T(8,128)(2,1)} collective-permute-done((bf16[2,192,1152]{2,1,0:T(8,128)(2,1)}, bf16[2,192,1152]{2,1,0:T(8,128)(2,1)}, u32[]{:S(2)}, u32[]{:S(2)}) %collective-permute-start.67) | collective-permute-done | bytes 884768 | tf_op jit(solution)/shard_map/ppermute | solution.py:108
  487.4 7.7 %collective-permute-done.65 = bf16[128,1536]{1,0:T(8,128)(2,1)S(1)} collective-permute-done((bf16[128,1536]{1,0:T(8,128)(2,1)S(1)}, bf16[128,1536]{1,0:T(8,128)(2,1)S(1)}, u32[]{:S(2)}, u32[]{:S(2)}) %collective-permute-start.65) | collective-permute-done | bytes 393248 | tf_op jit(solution)/shard_map/ppermute | solution.py:82
  524.5 10.1 %collective-permute-done.70 = bf16[2,192,1024]{2,1,0:T(8,128)(2,1)} collective-permute-done((bf16[2,192,1024]{2,1,0:T(8,128)(2,1)}, bf16[2,192,1024]{2,1,0:T(8,128)(2,1)}, u32[]{:S(2)}, u32[]{:S(2)}) %collective-permute-start.70) | collective-permute-done | bytes 786464 | tf_op jit(solution)/shard_map/ppermute | solution.py:82
  536.2 14.6 %collective-permute-done.69 = bf16[512,1536]{1,0:T(8,128)(2,1)} collective-permute-done((bf16[512,1536]{1,0:T(8,128)(2,1)}, bf16[512,1536]{1,0:T(8,128)(2,1)}, u32[]{:S(2)}, u32[]{:S(2)}) %collective-permute-start.69) | collective-permute-done | bytes 1572896 | tf_op jit(solution)/shard_map/ppermute | solution.py:82
  555.7 8.4 %collective-permute-done.75 = bf16[192,1024]{1,0:T(8,128)(2,1)S(1)} collective-permute-done((bf16[192,1024]{1,0:T(8,128)(2,1)S(1)}, bf16[192,1024]{1,0:T(8,128)(2,1)S(1)}, u32[]{:S(2)}, u32[]{:S(2)}) %collective-permute-start.75) | collective-permute-done | bytes 393248 | tf_op jit(solution)/shard_map/ppermute | solution.py:108
  591.1 5.5 collective-permute-done.82
  611.1 5.8 divide_subtract_fusion.1
  620.6 5.3 divide_subtract_fusion
  (475 shorter events, 234.8 us)
Async XLA Ops:
  7.2 126.1 %all-gather.8.cloned.1.call-start = ((), (), s32[]{:S(2)}) async-start(), calls=%async_computation.1 | async-start | bytes 3981312 | tf_op jit(solution)/shard_map/all_gather | solution.py:887
  65.2 132.6 %all-gather.10.cloned.1.call-start = ((), (), s32[]{:S(2)}) async-start(), calls=%async_computation.2 | async-start | bytes 2654208 | tf_op jit(solution)/shard_map/all_gather | solution.py:918
  65.5 53.3 %collective-permute-start.17 = (bf16[3,192,1152]{2,1,0:T(8,128)(2,1)}, bf16[3,192,1152]{2,1,0:T(8,128)(2,1)}, u32[]{:S(2)}, u32[]{:S(2)}) collective-permute-start(bf16[3,192,1152]{2,1,0:T(8,128)(2,1)} %get-tuple-element.242), channel_id=1, source_target_pairs={{0,8},{8,0},{1,9},{9,1},{2,10},{10,2},{3,11},{11,3},{4,12},{12,4},... | collective-permute-start | bytes 3981320 | tf_op jit(solution)/shard_map/ppermute | solution.py:82
  76.1 42.6 %collective-permute-start.16 = (bf16[3,192,1152]{2,1,0:T(8,128)(2,1)S(1)}, bf16[3,192,1152]{2,1,0:T(8,128)(2,1)S(1)}, u32[]{:S(2)}, u32[]{:S(2)}) collective-permute-start(bf16[3,192,1152]{2,1,0:T(8,128)(2,1)S(1)} %copy-done), channel_id=1, source_target_pairs={{0,4},{4,0},{1,5},{5,1},{2,6},{6,2},{3,7},{7,3},{8,12},{12,8},{9,1... | collective-permute-start | bytes 3981320 | tf_op jit(solution)/shard_map/ppermute | solution.py:82
  102.3 32.4 %collective-permute-start.13 = (bf16[256,1536]{1,0:T(8,128)(2,1)}, bf16[256,1536]{1,0:T(8,128)(2,1)}, u32[]{:S(2)}, u32[]{:S(2)}) collective-permute-start(bf16[256,1536]{1,0:T(8,128)(2,1)} %get-tuple-element.237), channel_id=1, source_target_pairs={{0,2},{2,0},{1,3},{3,1},{4,6},{6,4},{5,7},{7,5},{8,10},{10,8},{9,1... | collective-permute-start | bytes 2359304 | tf_op jit(solution)/shard_map/ppermute | solution.py:82
  149.0 293.8 %all-gather.6.cloned.1.call-start = ((), (), s32[]{:S(2)}) async-start(), calls=%async_computation | async-start | bytes 2654208 | tf_op jit(solution)/shard_map/all_gather | solution.py:767
  174.7 33.1 %collective-permute-start.32 = (bf16[3,192,1152]{2,1,0:T(8,128)(2,1)S(1)}, bf16[3,192,1152]{2,1,0:T(8,128)(2,1)}, u32[]{:S(2)}, u32[]{:S(2)}) collective-permute-start(bf16[3,192,1152]{2,1,0:T(8,128)(2,1)S(1)} %dynamic-slice_bitcast_fusion.refs_10_.refs_18_), channel_id=1, source_target_pairs={{0,4},{4,0},{1,5},{5,1},{2,6},{6,2},{3,7},{7,3},{8,12},{12,8},{9,1... | collective-permute-start | bytes 3981320 | tf_op jit(solution)/shard_map/ppermute | solution.py:82
  197.8 64.8 %collective-permute-start.36 = (bf16[128,1536]{1,0:T(8,128)(2,1)}, bf16[128,1536]{1,0:T(8,128)(2,1)}, u32[]{:S(2)}, u32[]{:S(2)}) collective-permute-start(bf16[128,1536]{1,0:T(8,128)(2,1)} %slice.192), channel_id=1, source_target_pairs={{0,8},{8,0},{1,9},{9,1},{2,10},{10,2},{3,11},{11,3},{4,12},{12,4},... | collective-permute-start | bytes 1179656 | tf_op jit(solution)/shard_map/ppermute | solution.py:82
  200.9 34.3 %collective-permute-start.31 = (bf16[256,1536]{1,0:T(8,128)(2,1)}, bf16[256,1536]{1,0:T(8,128)(2,1)S(1)}, u32[]{:S(2)}, u32[]{:S(2)}) collective-permute-start(bf16[256,1536]{1,0:T(8,128)(2,1)} %refs_0_), channel_id=1, source_target_pairs={{0,8},{8,0},{1,9},{9,1},{2,10},{10,2},{3,11},{11,3},{4,12},{12,4},... | collective-permute-start | bytes 2359304 | tf_op jit(solution)/shard_map/ppermute | solution.py:82
  202.0 36.8 %collective-permute-start.30 = (bf16[256,1536]{1,0:T(8,128)(2,1)S(1)}, bf16[256,1536]{1,0:T(8,128)(2,1)S(1)}, u32[]{:S(2)}, u32[]{:S(2)}) collective-permute-start(bf16[256,1536]{1,0:T(8,128)(2,1)S(1)} %constant_dynamic-update-slice_fusion.4.refs_2_), channel_id=1, source_target_pairs={{0,2},{2,0},{1,3},{3,1},{4,6},{6,4},{5,7},{7,5},{8,10},{10,8},{9,1... | collective-permute-start | bytes 2359304 | tf_op jit(solution)/shard_map/ppermute | solution.py:82
  204.5 36.4 %collective-permute-start.33 = (bf16[2,192,1152]{2,1,0:T(8,128)(2,1)}, bf16[2,192,1152]{2,1,0:T(8,128)(2,1)}, u32[]{:S(2)}, u32[]{:S(2)}) collective-permute-start(bf16[2,192,1152]{2,1,0:T(8,128)(2,1)} %dynamic-slice_bitcast_fusion.1.refs_12_), channel_id=1, source_target_pairs={{0,4},{4,0},{1,5},{5,1},{2,6},{6,2},{3,7},{7,3},{8,12},{12,8},{9,1... | collective-permute-start | bytes 2654216 | tf_op jit(solution)/shard_map/ppermute | solution.py:82
  207.8 32.6 %collective-permute-start.34 = (bf16[192,1152]{1,0:T(8,128)(2,1)}, bf16[192,1152]{1,0:T(8,128)(2,1)}, u32[]{:S(2)}, u32[]{:S(2)}) collective-permute-start(bf16[192,1152]{1,0:T(8,128)(2,1)} %slice_bitcast_fusion.7), channel_id=1, source_target_pairs={{0,16},{16,0},{1,17},{17,1},{2,18},{18,2},{3,19},{19,3},{4,20},{20... | collective-permute-start | bytes 1327112 | tf_op jit(solution)/shard_map/ppermute | solution.py:108
  333.2 44.5 %collective-permute-start.51 = (bf16[2,2,192,1152]{3,2,1,0:T(8,128)(2,1)}, bf16[2,2,192,1152]{3,2,1,0:T(8,128)(2,1)}, u32[]{:S(2)}, u32[]{:S(2)}) collective-permute-start(bf16[2,2,192,1152]{3,2,1,0:T(8,128)(2,1)} %get-tuple-element.319), channel_id=1, source_target_pairs={{0,4},{4,0},{1,5},{5,1},{2,6},{6,2},{3,7},{7,3},{8,12},{12,8},{9,1... | collective-permute-start | bytes 5308424 | tf_op jit(solution)/shard_map/ppermute | solution.py:82
  358.7 54.2 %collective-permute-start.59 = (bf16[2,2,192,1152]{3,2,1,0:T(8,128)(2,1)}, bf16[2,2,192,1152]{3,2,1,0:T(8,128)(2,1)}, u32[]{:S(2)}, u32[]{:S(2)}) collective-permute-start(bf16[2,2,192,1152]{3,2,1,0:T(8,128)(2,1)} %get-tuple-element.337), channel_id=1, source_target_pairs={{0,4},{4,0},{1,5},{5,1},{2,6},{6,2},{3,7},{7,3},{8,12},{12,8},{9,1... | collective-permute-start | bytes 5308424 | tf_op jit(solution)/shard_map/ppermute | solution.py:82
  407.2 87.9 %collective-permute-start.61 = (bf16[2,2,192,1152]{3,2,1,0:T(8,128)(2,1)}, bf16[2,2,192,1152]{3,2,1,0:T(8,128)(2,1)}, u32[]{:S(2)}, u32[]{:S(2)}) collective-permute-start(bf16[2,2,192,1152]{3,2,1,0:T(8,128)(2,1)} %get-tuple-element.350), channel_id=1, source_target_pairs={{0,4},{4,0},{1,5},{5,1},{2,6},{6,2},{3,7},{7,3},{8,12},{12,8},{9,1... | collective-permute-start | bytes 5308424 | tf_op jit(solution)/shard_map/ppermute | solution.py:82
  442.8 40.7 %collective-permute-start.67 = (bf16[2,192,1152]{2,1,0:T(8,128)(2,1)}, bf16[2,192,1152]{2,1,0:T(8,128)(2,1)}, u32[]{:S(2)}, u32[]{:S(2)}) collective-permute-start(bf16[2,192,1152]{2,1,0:T(8,128)(2,1)} %fusion.17), channel_id=1, source_target_pairs={{0,16},{16,0},{1,17},{17,1},{2,18},{18,2},{3,19},{19,3},{4,20},{20... | collective-permute-start | bytes 2654216 | tf_op jit(solution)/shard_map/ppermute | solution.py:108
  442.9 52.2 %collective-permute-start.60 = (bf16[2,192,1024]{2,1,0:T(8,128)(2,1)}, bf16[2,192,1024]{2,1,0:T(8,128)(2,1)S(1)}, u32[]{:S(2)}, u32[]{:S(2)}) collective-permute-start(bf16[2,192,1024]{2,1,0:T(8,128)(2,1)} %get-tuple-element.349), channel_id=1, source_target_pairs={{0,8},{8,0},{1,9},{9,1},{2,10},{10,2},{3,11},{11,3},{4,12},{12,4},... | collective-permute-start | bytes 2359304 | tf_op jit(solution)/shard_map/ppermute | solution.py:82
  446.4 37.2 %collective-permute-start.64 = (bf16[128,1536]{1,0:T(8,128)(2,1)S(1)}, bf16[128,1536]{1,0:T(8,128)(2,1)S(1)}, u32[]{:S(2)}, u32[]{:S(2)}) collective-permute-start(bf16[128,1536]{1,0:T(8,128)(2,1)S(1)} %add_convert_fusion.7), channel_id=1, source_target_pairs={{0,1},{1,0},{2,3},{3,2},{4,5},{5,4},{6,7},{7,6},{8,9},{9,8},{10,11... | collective-permute-start | bytes 1179656 | tf_op jit(solution)/shard_map/ppermute | solution.py:82
  447.7 64.4 %collective-permute-start.52 = (bf16[512,1536]{1,0:T(8,128)(2,1)}, bf16[512,1536]{1,0:T(8,128)(2,1)}, u32[]{:S(2)}, u32[]{:S(2)}) collective-permute-start(bf16[512,1536]{1,0:T(8,128)(2,1)} %get-tuple-element.330), channel_id=1, source_target_pairs={{0,2},{2,0},{1,3},{3,1},{4,6},{6,4},{5,7},{7,5},{8,10},{10,8},{9,1... | collective-permute-start | bytes 4718600 | tf_op jit(solution)/shard_map/ppermute | solution.py:82
  499.5 35.1 %collective-permute-start.70 = (bf16[2,192,1024]{2,1,0:T(8,128)(2,1)}, bf16[2,192,1024]{2,1,0:T(8,128)(2,1)}, u32[]{:S(2)}, u32[]{:S(2)}) collective-permute-start(bf16[2,192,1024]{2,1,0:T(8,128)(2,1)} %get-tuple-element.372), channel_id=1, source_target_pairs={{0,8},{8,0},{1,9},{9,1},{2,10},{10,2},{3,11},{11,3},{4,12},{12,4},... | collective-permute-start | bytes 2359304 | tf_op jit(solution)/shard_map/ppermute | solution.py:82
  501.8 53.6 %collective-permute-start.76 = (bf16[2,192,1152]{2,1,0:T(8,128)(2,1)}, bf16[2,192,1152]{2,1,0:T(8,128)(2,1)}, u32[]{:S(2)}, u32[]{:S(2)}) collective-permute-start(bf16[2,192,1152]{2,1,0:T(8,128)(2,1)} %fusion.18), channel_id=1, source_target_pairs={{0,16},{16,0},{1,17},{17,1},{2,18},{18,2},{3,19},{19,3},{4,20},{20... | collective-permute-start | bytes 2654216 | tf_op jit(solution)/shard_map/ppermute | solution.py:108
  515.3 35.4 %collective-permute-start.69 = (bf16[512,1536]{1,0:T(8,128)(2,1)}, bf16[512,1536]{1,0:T(8,128)(2,1)}, u32[]{:S(2)}, u32[]{:S(2)}) collective-permute-start(bf16[512,1536]{1,0:T(8,128)(2,1)} %add_convert_fusion), channel_id=1, source_target_pairs={{0,1},{1,0},{2,3},{3,2},{4,5},{5,4},{6,7},{7,6},{8,9},{9,8},{10,11... | collective-permute-start | bytes 4718600 | tf_op jit(solution)/shard_map/ppermute | solution.py:82
  520.1 55.5 %collective-permute-start.72 = (bf16[192,1152]{1,0:T(8,128)(2,1)}, bf16[192,1152]{1,0:T(8,128)(2,1)}, u32[]{:S(2)}, u32[]{:S(2)}) collective-permute-start(bf16[192,1152]{1,0:T(8,128)(2,1)} %get-tuple-element.437), channel_id=1, source_target_pairs={{0,8},{8,0},{1,9},{9,1},{2,10},{10,2},{3,11},{11,3},{4,12},{12,4},... | collective-permute-start | bytes 1327112 | tf_op jit(solution)/shard_map/ppermute | solution.py:82
  521.1 48.5 %collective-permute-start.73 = (bf16[192,1152]{1,0:T(8,128)(2,1)}, bf16[192,1152]{1,0:T(8,128)(2,1)}, u32[]{:S(2)}, u32[]{:S(2)}) collective-permute-start(bf16[192,1152]{1,0:T(8,128)(2,1)} %get-tuple-element.439), channel_id=1, source_target_pairs={{0,8},{8,0},{1,9},{9,1},{2,10},{10,2},{3,11},{11,3},{4,12},{12,4},... | collective-permute-start | bytes 1327112 | tf_op jit(solution)/shard_map/ppermute | solution.py:82
  (157 other events, 2417.5 us)
Sparse Core Ops, SparseCore 0:
  65.3 67.9 all-gather.7
  149.2 48.6 all-gather.9
  383.3 48.9 all-gather.5

commit v5 on v4

--- a/solution.py
+++ b/solution.py
@@ -942,13 +942,9 @@
     ff_lo_hi_yy_gu = [swap(order.after(part), "yy") for part in ff_lo_hi_gu]
     ff_lo_hi_d = [turn(order.after(ff_lo[2]), "hi", k) for k in steps]
     ff_hi_yy = order.done(ff_hi_yy)
-    cot_lo = order.done(cot_lo)
-    cot_both = swap(cot_lo[:half], "tensor"), swap(cot_x[half:], "lo")
-    cot_near = jnp.concatenate([cot_x, cot_lo])
-    cot_core, cot_core_near = swap(order.after(cotangent), "core"), swap(cot_near, "core")
+    cot_both_lo = swap(cot_x[half:], "lo")
+    cot_core = swap(order.after(cotangent), "core")
     n2_core_both = order.done(n2_core_both)
-    ff_lo_hi_d = order.done(ff_lo_hi_d)
-    ff_lo_hi_yy_d = [swap(part, "yy") for part in ff_lo_hi_d]
     ff_lo_hi_yy_gu = order.done(ff_lo_hi_yy_gu)
     n2_parts = [n2, n2_near, n2_both, n2_core, n2_core_near, n2_core_both]
 
@@ -959,9 +955,16 @@
     ff_chips = jnp.stack(ff_chips).astype(jnp.int32)
     gates, n2_t = gate_up(ff_chips, order.after(n2_parts), gu_pieces)
     order.mark = gates
-    cot_both = jnp.concatenate(order.done(cot_both))
+    cot_lo = order.done(cot_lo)
+    cot_both_x = swap(cot_lo[:half], "tensor")
+    cot_near = jnp.concatenate([cot_x, cot_lo])
+    cot_core_near = swap(cot_near, "core")
+    ff_lo_hi_d = order.done(ff_lo_hi_d)
+    ff_lo_hi_yy_d = [swap(part, "yy") for part in ff_lo_hi_d]
+    cot_core, cot_both_lo = order.done((cot_core, cot_both_lo))
+    cot_both = jnp.concatenate([order.done(cot_both_x), cot_both_lo])
     cot_core_both = swap(cot_both, "core")
-    cot_core, cot_core_near = order.done((cot_core, cot_core_near))
+    cot_core_near = order.done(cot_core_near)
     ff_lo_hi_yy_d = order.done(ff_lo_hi_yy_d)
     cot_core_both = order.done(cot_core_both)
     cot_parts = [cotangent, cot_near, cot_both, cot_core, cot_core_near, cot_core_both]
@@ -1038,8 +1041,9 @@
     dn1 = FourSum(*parts[:6])
     att = ChipSum(*parts[6:])
     dn1.second(order)
+    norm_one_in, gain_one_grad = norm_backward(rows_in, scale_one, gain_one, dn1.total(order))
     g_sum.arrived(order)
-    norm_one_in, gain_one_grad = norm_backward(rows_in, scale_one, gain_one, dn1.total(order))
+    branch.along_x(order)
     u_sum.across(order, False)
     att.far_yy(order)
     bias_grad = order.after(bias_grad)[0]
@@ -1048,7 +1052,6 @@
     )
     bias_slots = lax.dynamic_update_slice_in_dim(bias_slots, bias_grad[Q_COLS:], kv_at, 0)
     att.far_hi(order)
-    branch.along_x(order)
     d_low, d_way = summed_up(d_sum)
     g_low, g_way = summed_up(g_sum)
     att.near_yy(order)

time: 640 us -> 643 us (level)
    ppermute x81, waiting for transfers between devices: 160 us -> 145 us  [swap(): return lax.ppermute(value, axis, [(0, 1), (1, 0)])]
    unnamed x188 -> x166, local copies, waits for them, and re-layouts: 18.6 us -> 17.6 us
  transfers between devices with their start and end apart: 90 -> 90, of which waited for: 29 -> 36; matrix products, arithmetic and copies ran while one was open for 19% -> 20% of each run, Pallas kernels for 21% -> 21%
where the time goes in v5:
time: 643 us; the launch traced here: 636 us
  waiting for transfers between devices  230 us (36%)
  Pallas kernels  173 us (27%)
  other arithmetic  93.7 us (15%)
  starting transfers between devices  62.5 us (10%)
  local copies, waits for them, and re-layouts  56.4 us (9%)
  between operations  20.9 us (3%)
    ppermute x81, waiting for transfers between devices, swap(): return lax.ppermute(value, axis, [(0, 1), (1, 0)])  145 us
    ppermute x81, starting transfers between devices, swap(): return lax.ppermute(value, axis, [(0, 1), (1, 0)])  55.2 us
    ppermute x5, waiting for transfers between devices, turn(): lax.ppermute(value, axis, [(i, (i + steps) % count) for i in range(count)])  50.5 us
    pallas_call x3, Pallas kernels, weight_grad(): pl.pallas_call(functools.partial(weight_grad_kernel, rows), grid_spec=plt...  42.3 us
    pallas_call x1, Pallas kernels, feed_forward(): pl.pallas_call(functools.partial(feed_forward_kernel, count, rows), grid_...  39.8 us
    pallas_call x1, Pallas kernels, attention_back(): pl.pallas_call(functools.partial(attention_back_kernel, len(da), len(n1),...  26.9 us
    pallas_call x1, Pallas kernels, attention(): pl.pallas_call(functools.partial(attention_kernel, len(n1), parts, rows),...  23.2 us
    all_gather x1, waiting for transfers between devices, body(): ff_lo_hi_gu = lax.all_gather(ff_lo[:2], 'hi')  23.2 us
  transfers between devices with their start and end apart: 90, of which 36 were waited for; matrix products, arithmetic and copies ran while one was open for 20% of the time, Pallas kernels for 21%

profile of v5, /device:TPU:0, one launch (start us, length us, event | category | flops | bytes accessed | tf_op | source)
XLA Modules:
  0.0 636.4 jit_solution(13497428498177186137)
XLA Ops:
  27.6 12.7 %collective-permute-done.4.refs_11_ = bf16[192,1024]{1,0:T(8,128)(2,1)} collective-permute-done((bf16[192,1024]{1,0:T(8,128)(2,1)S(1)}, bf16[192,1024]{1,0:T(8,128)(2,1)}, u32[]{:S(2)}, u32[]{:S(2)}) %collective-permute-start.4) | collective-permute-done | bytes 393248 | tf_op jit(solution)/shard_map/ppermute | solution.py:82
  44.9 9.9 %collective-permute-done.10.refs_15_ = bf16[192,1024]{1,0:T(8,128)(2,1)S(1)} collective-permute-done((bf16[192,1024]{1,0:T(8,128)(2,1)}, bf16[192,1024]{1,0:T(8,128)(2,1)S(1)}, u32[]{:S(2)}, u32[]{:S(2)}) %collective-permute-start.10) | collective-permute-done | bytes 393248 | tf_op jit(solution)/shard_map/ppermute | solution.py:82
  67.7 8.4 %collective-permute-done.12.refs_17_ = bf16[192,1024]{1,0:T(8,128)(2,1)} collective-permute-done((bf16[192,1024]{1,0:T(8,128)(2,1)}, bf16[192,1024]{1,0:T(8,128)(2,1)}, u32[]{:S(2)}, u32[]{:S(2)}) %collective-permute-start.12) | collective-permute-done | bytes 393248 | tf_op jit(solution)/shard_map/ppermute | solution.py:82
  78.4 23.2 %attention.1 = (bf16[1024,640]{1,0:T(8,128)(2,1)}, bf16[1024,384]{1,0:T(8,128)(2,1)}, f32[8,1024]{1,0:T(8,128)}, bf16[256,1536]{1,0:T(8,128)(2,1)}, bf16[128,153...) custom-call(s32[8]{0:T(128)} %stack.100.chips_ref, ...), custom_call_target="tpu_custom_call" | custom-call | flops 1179648 | bytes 4096 | tf_op jit(solution)/shard_map/attention/pallas_call | solution.py:308
  102.3 16.3 %collective-permute-done.17.refs_7_.refs_15_ = bf16[3,192,1152]{2,1,0:T(8,128)(2,1)} collective-permute-done((bf16[3,192,1152]{2,1,0:T(8,128)(2,1)}, bf16[3,192,1152]{2,1,0:T(8,128)(2,1)}, u32[]{:S(2)}, u32[]{:S(2)}) %collective-permute-start.17) | collective-permute-done | bytes 1327136 | tf_op jit(solution)/shard_map/ppermute | solution.py:82
  123.7 9.6 %all-gather.8.cloned.1.call-done = bf16[6,192,1152]{2,1,0:T(8,128)(2,1)} async-done(((bf16[3,192,1152]{2,1,0:T(8,128)(2,1)}), bf16[6,192,1152]{2,1,0:T(8,128)(2,1)}) %all-gather.8.cloned.1.call-update) | async-done | bytes 2654224 | tf_op jit(solution)/shard_map/all_gather | solution.py:887
  174.7 23.2 %all-gather.10.cloned.1.call-done = bf16[4,192,1152]{2,1,0:T(8,128)(2,1)} async-done(((bf16[2,192,1152]{2,1,0:T(8,128)(2,1)}), bf16[4,192,1152]{2,1,0:T(8,128)(2,1)}) %all-gather.10.cloned.1.call-update) | async-done | bytes 1769488 | tf_op jit(solution)/shard_map/all_gather | solution.py:918
  213.7 10.5 %collective-permute-done.32.refs_13_ = bf16[2,192,1152]{2,1,0:T(8,128)(2,1)} collective-permute-done((bf16[2,192,1152]{2,1,0:T(8,128)(2,1)}, bf16[2,192,1152]{2,1,0:T(8,128)(2,1)}, u32[]{:S(2)}, u32[]{:S(2)}) %collective-permute-start.32) | collective-permute-done | bytes 884768 | tf_op jit(solution)/shard_map/ppermute | solution.py:82
  224.2 21.8 %gate_up.1 = (bf16[2048,2304]{1,0:T(8,128)(2,1)}, bf16[1536,2048]{1,0:T(8,128)(2,1)}) custom-call(s32[8]{0:T(128)} %stack.104.chips_ref, bf16[256,1536]{1,0:T(8,128)(2,1)} %multiply_convert_fusion.refs_0_, bf16[512,1536]{1,0:T(8,128)(2,1)} %constant_dynamic-update-slice_fusion.refs_1_, bf16[256,1536]{1,0:T(8,128)(2,1)} %constant_dynamic-update-slice_fusion.4.refs_2_, ...), custom_call_target="tpu_custom_call" | custom-call | flops 3538944 | bytes 7680 | tf_op jit(solution)/shard_map/gate_up/pallas_call | solution.py:482
  251.9 5.8 collective-permute-done.34
  260.9 10.8 %collective-permute-done.40.refs_21_ = bf16[192,1152]{1,0:T(8,128)(2,1)S(1)} collective-permute-done((bf16[192,1152]{1,0:T(8,128)(2,1)}, bf16[192,1152]{1,0:T(8,128)(2,1)S(1)}, u32[]{:S(2)}, u32[]{:S(2)}) %collective-permute-start.40) | collective-permute-done | bytes 442400 | tf_op jit(solution)/shard_map/ppermute | solution.py:82
  272.5 39.8 %feed_forward.1 = (bf16[256,1536]{1,0:T(8,128)(2,1)}, bf16[256,1536]{1,0:T(8,128)(2,1)}, bf16[256,1536]{1,0:T(8,128)(2,1)}, bf16[256,1536]{1,0:T(8,128)(2,1)}, b...) custom-call(s32[8]{0:T(128)} %stack.104.chips_ref, ...), custom_call_target="tpu_custom_call" | custom-call | flops 5308416 | bytes 12800 | tf_op jit(solution)/shard_map/feed_forward/pallas_call | solution.py:572
  314.0 14.1 %weight_grad.3 = (bf16[2,2,192,1152]{3,2,1,0:T(8,128)(2,1)}, bf16[2,2,192,1152]{3,2,1,0:T(8,128)(2,1)}) custom-call(s32[3]{0:T(128)} %pad_add_fusion.1.place_ref, bf16[1536,2048]{1,0:T(8,128)(2,1)} %get-tuple-element.303.left_ref, bf16[2048,1152]{1,0:T(8,128)(2,1)} %get-tuple-element.327.right_ref.left_ref), custom_call_target="tpu_custom_call" | custom-call | flops 1769472 | bytes 4096 | tf_op jit(solution)/shard_map/weight_grad/pallas_call | solution.py:625
  339.2 14.1 %weight_grad.4 = (bf16[2,2,192,1152]{3,2,1,0:T(8,128)(2,1)}, bf16[2,2,192,1152]{3,2,1,0:T(8,128)(2,1)}) custom-call(s32[3]{0:T(128)} %pad_add_fusion.1.place_ref, bf16[1536,2048]{1,0:T(8,128)(2,1)} %get-tuple-element.321.left_ref, bf16[2048,1152]{1,0:T(8,128)(2,1)} %get-tuple-element.314.right_ref), custom_call_target="tpu_custom_call" | custom-call | flops 1769472 | bytes 4096 | tf_op jit(solution)/shard_map/weight_grad/pallas_call | solution.py:625
  359.9 14.1 %weight_grad.5 = (bf16[2,2,192,1152]{3,2,1,0:T(8,128)(2,1)}, bf16[2,2,192,1152]{3,2,1,0:T(8,128)(2,1)}) custom-call(s32[3]{0:T(128)} %pad_add_fusion.1.place_ref, bf16[1536,2048]{1,0:T(8,128)(2,1)} %get-tuple-element.321.left_ref, bf16[2048,1152]{1,0:T(8,128)(2,1)} %get-tuple-element.322.right_ref), custom_call_target="tpu_custom_call" | custom-call | flops 1769472 | bytes 4096 | tf_op jit(solution)/shard_map/weight_grad/pallas_call | solution.py:625
  385.9 15.4 %down.1 = (bf16[512,1536]{1,0:T(8,128)(2,1)}, bf16[512,1536]{1,0:T(8,128)(2,1)}, bf16[512,1536]{1,0:T(8,128)(2,1)}, bf16[512,1536]{1,0:T(8,128)(2,1)}) custom-call(bf16[2048,1152]{1,0:T(8,128)(2,1)} %get-tuple-element.327.right_ref.left_ref, bf16[1536,1152]{1,0:T(8,128)(2,1)} %get-tuple-element.328.right_ref), custom_call_target="tpu_custom_call" | custom-call | flops 1769472 | bytes 3584 | tf_op jit(solution)/shard_map/down/pallas_call | solution.py:662
  406.9 26.9 %attention_back.1 = (bf16[1024,640]{1,0:T(8,128)(2,1)}, f32[1,640]{1,0:T(1,128)}, bf16[256,1536]{1,0:T(8,128)(2,1)}, bf16[128,1536]{1,0:T(8,128)(2,1)}, bf16[128...) custom-call(s32[8]{0:T(128)} %stack.113.chips_ref, ...), custom_call_target="tpu_custom_call" | custom-call | flops 2555904 | bytes 6144 | tf_op jit(solution)/shard_map/attention_back/pallas_call | solution.py:400
  449.8 7.6 %collective-permute-done.64 = bf16[128,1536]{1,0:T(8,128)(2,1)} collective-permute-done((bf16[128,1536]{1,0:T(8,128)(2,1)}, bf16[128,1536]{1,0:T(8,128)(2,1)}, u32[]{:S(2)}, u32[]{:S(2)}) %collective-permute-start.64) | collective-permute-done | bytes 393248 | tf_op jit(solution)/shard_map/ppermute | solution.py:82
  461.2 28.8 %collective-permute-done.60 = bf16[2,192,1152]{2,1,0:T(8,128)(2,1)S(1)} collective-permute-done((bf16[2,192,1152]{2,1,0:T(8,128)(2,1)}, bf16[2,192,1152]{2,1,0:T(8,128)(2,1)S(1)}, u32[]{:S(2)}, u32[]{:S(2)}) %collective-permute-start.60) | collective-permute-done | bytes 884768 | tf_op jit(solution)/shard_map/ppermute | solution.py:108
  520.0 15.4 %collective-permute-done.69 = bf16[2,192,1024]{2,1,0:T(8,128)(2,1)} collective-permute-done((bf16[2,192,1024]{2,1,0:T(8,128)(2,1)}, bf16[2,192,1024]{2,1,0:T(8,128)(2,1)}, u32[]{:S(2)}, u32[]{:S(2)}) %collective-permute-start.69) | collective-permute-done | bytes 786464 | tf_op jit(solution)/shard_map/ppermute | solution.py:82
  546.2 20.2 %collective-permute-done.75 = bf16[192,1024]{1,0:T(8,128)(2,1)S(1)} collective-permute-done((bf16[192,1024]{1,0:T(8,128)(2,1)S(1)}, bf16[192,1024]{1,0:T(8,128)(2,1)S(1)}, u32[]{:S(2)}, u32[]{:S(2)}) %collective-permute-start.75) | collective-permute-done | bytes 393248 | tf_op jit(solution)/shard_map/ppermute | solution.py:108
  592.1 5.9 collective-permute-done.82
  613.8 5.8 divide_subtract_fusion.1
  623.3 5.3 divide_subtract_fusion
  (453 shorter events, 249.7 us)
Async XLA Ops:
  7.2 126.1 %all-gather.8.cloned.1.call-start = ((), (), s32[]{:S(2)}) async-start(), calls=%async_computation.1 | async-start | bytes 3981312 | tf_op jit(solution)/shard_map/all_gather | solution.py:887
  65.2 132.7 %all-gather.10.cloned.1.call-start = ((), (), s32[]{:S(2)}) async-start(), calls=%async_computation.2 | async-start | bytes 2654208 | tf_op jit(solution)/shard_map/all_gather | solution.py:918
  65.4 53.3 %collective-permute-start.17 = (bf16[3,192,1152]{2,1,0:T(8,128)(2,1)}, bf16[3,192,1152]{2,1,0:T(8,128)(2,1)}, u32[]{:S(2)}, u32[]{:S(2)}) collective-permute-start(bf16[3,192,1152]{2,1,0:T(8,128)(2,1)} %get-tuple-element.242), channel_id=1, source_target_pairs={{0,8},{8,0},{1,9},{9,1},{2,10},{10,2},{3,11},{11,3},{4,12},{12,4},... | collective-permute-start | bytes 3981320 | tf_op jit(solution)/shard_map/ppermute | solution.py:82
  76.1 42.6 %collective-permute-start.16 = (bf16[3,192,1152]{2,1,0:T(8,128)(2,1)S(1)}, bf16[3,192,1152]{2,1,0:T(8,128)(2,1)S(1)}, u32[]{:S(2)}, u32[]{:S(2)}) collective-permute-start(bf16[3,192,1152]{2,1,0:T(8,128)(2,1)S(1)} %copy-done), channel_id=1, source_target_pairs={{0,4},{4,0},{1,5},{5,1},{2,6},{6,2},{3,7},{7,3},{8,12},{12,8},{9,1... | collective-permute-start | bytes 3981320 | tf_op jit(solution)/shard_map/ppermute | solution.py:82
  102.3 32.5 %collective-permute-start.13 = (bf16[256,1536]{1,0:T(8,128)(2,1)}, bf16[256,1536]{1,0:T(8,128)(2,1)}, u32[]{:S(2)}, u32[]{:S(2)}) collective-permute-start(bf16[256,1536]{1,0:T(8,128)(2,1)} %get-tuple-element.237), channel_id=1, source_target_pairs={{0,2},{2,0},{1,3},{3,1},{4,6},{6,4},{5,7},{7,5},{8,10},{10,8},{9,1... | collective-permute-start | bytes 2359304 | tf_op jit(solution)/shard_map/ppermute | solution.py:82
  149.0 286.6 %all-gather.6.cloned.1.call-start = ((), (), s32[]{:S(2)}) async-start(), calls=%async_computation | async-start | bytes 2654208 | tf_op jit(solution)/shard_map/all_gather | solution.py:767
  171.7 40.2 %collective-permute-start.31 = (bf16[3,192,1152]{2,1,0:T(8,128)(2,1)S(1)}, bf16[3,192,1152]{2,1,0:T(8,128)(2,1)}, u32[]{:S(2)}, u32[]{:S(2)}) collective-permute-start(bf16[3,192,1152]{2,1,0:T(8,128)(2,1)S(1)} %dynamic-slice_bitcast_fusion.refs_10_.refs_18_), channel_id=1, source_target_pairs={{0,4},{4,0},{1,5},{5,1},{2,6},{6,2},{3,7},{7,3},{8,12},{12,8},{9,1... | collective-permute-start | bytes 3981320 | tf_op jit(solution)/shard_map/ppermute | solution.py:82
  205.4 40.6 %collective-permute-start.33 = (bf16[256,1536]{1,0:T(8,128)(2,1)}, bf16[256,1536]{1,0:T(8,128)(2,1)}, u32[]{:S(2)}, u32[]{:S(2)}) collective-permute-start(bf16[256,1536]{1,0:T(8,128)(2,1)} %refs_0_), channel_id=1, source_target_pairs={{0,8},{8,0},{1,9},{9,1},{2,10},{10,2},{3,11},{11,3},{4,12},{12,4},... | collective-permute-start | bytes 2359304 | tf_op jit(solution)/shard_map/ppermute | solution.py:82
  207.7 43.2 %collective-permute-start.36 = (bf16[128,1536]{1,0:T(8,128)(2,1)}, bf16[128,1536]{1,0:T(8,128)(2,1)}, u32[]{:S(2)}, u32[]{:S(2)}) collective-permute-start(bf16[128,1536]{1,0:T(8,128)(2,1)} %slice.191), channel_id=1, source_target_pairs={{0,8},{8,0},{1,9},{9,1},{2,10},{10,2},{3,11},{11,3},{4,12},{12,4},... | collective-permute-start | bytes 1179656 | tf_op jit(solution)/shard_map/ppermute | solution.py:82
  211.8 39.1 %collective-permute-start.35 = (bf16[256,1536]{1,0:T(8,128)(2,1)}, bf16[256,1536]{1,0:T(8,128)(2,1)S(1)}, u32[]{:S(2)}, u32[]{:S(2)}) collective-permute-start(bf16[256,1536]{1,0:T(8,128)(2,1)} %refs_0_), channel_id=1, source_target_pairs={{0,2},{2,0},{1,3},{3,1},{4,6},{6,4},{5,7},{7,5},{8,10},{10,8},{9,1... | collective-permute-start | bytes 2359304 | tf_op jit(solution)/shard_map/ppermute | solution.py:82
  213.7 37.2 %collective-permute-start.37 = (bf16[192,1152]{1,0:T(8,128)(2,1)}, bf16[192,1152]{1,0:T(8,128)(2,1)}, u32[]{:S(2)}, u32[]{:S(2)}) collective-permute-start(bf16[192,1152]{1,0:T(8,128)(2,1)} %slice_bitcast_fusion.7), channel_id=1, source_target_pairs={{0,16},{16,0},{1,17},{17,1},{2,18},{18,2},{3,19},{19,3},{4,20},{20... | collective-permute-start | bytes 1327112 | tf_op jit(solution)/shard_map/ppermute | solution.py:108
  328.0 46.0 %collective-permute-start.51 = (bf16[2,2,192,1152]{3,2,1,0:T(8,128)(2,1)}, bf16[2,2,192,1152]{3,2,1,0:T(8,128)(2,1)}, u32[]{:S(2)}, u32[]{:S(2)}) collective-permute-start(bf16[2,2,192,1152]{3,2,1,0:T(8,128)(2,1)} %get-tuple-element.319), channel_id=1, source_target_pairs={{0,4},{4,0},{1,5},{5,1},{2,6},{6,2},{3,7},{7,3},{8,12},{12,8},{9,1... | collective-permute-start | bytes 5308424 | tf_op jit(solution)/shard_map/ppermute | solution.py:82
  353.3 53.6 %collective-permute-start.54 = (bf16[2,2,192,1152]{3,2,1,0:T(8,128)(2,1)}, bf16[2,2,192,1152]{3,2,1,0:T(8,128)(2,1)}, u32[]{:S(2)}, u32[]{:S(2)}) collective-permute-start(bf16[2,2,192,1152]{3,2,1,0:T(8,128)(2,1)} %get-tuple-element.332), channel_id=1, source_target_pairs={{0,4},{4,0},{1,5},{5,1},{2,6},{6,2},{3,7},{7,3},{8,12},{12,8},{9,1... | collective-permute-start | bytes 5308424 | tf_op jit(solution)/shard_map/ppermute | solution.py:82
  434.3 55.7 %collective-permute-start.68 = (bf16[2,2,192,1152]{3,2,1,0:T(8,128)(2,1)}, bf16[2,2,192,1152]{3,2,1,0:T(8,128)(2,1)}, u32[]{:S(2)}, u32[]{:S(2)}) collective-permute-start(bf16[2,2,192,1152]{3,2,1,0:T(8,128)(2,1)} %get-tuple-element.368), channel_id=1, source_target_pairs={{0,4},{4,0},{1,5},{5,1},{2,6},{6,2},{3,7},{7,3},{8,12},{12,8},{9,1... | collective-permute-start | bytes 5308424 | tf_op jit(solution)/shard_map/ppermute | solution.py:82
  435.1 54.9 %collective-permute-start.52 = (bf16[512,1536]{1,0:T(8,128)(2,1)}, bf16[512,1536]{1,0:T(8,128)(2,1)}, u32[]{:S(2)}, u32[]{:S(2)}) collective-permute-start(bf16[512,1536]{1,0:T(8,128)(2,1)} %get-tuple-element.330), channel_id=1, source_target_pairs={{0,2},{2,0},{1,3},{3,1},{4,6},{6,4},{5,7},{7,5},{8,10},{10,8},{9,1... | collective-permute-start | bytes 4718600 | tf_op jit(solution)/shard_map/ppermute | solution.py:82
  435.1 54.9 %collective-permute-start.53 = (bf16[512,1536]{1,0:T(8,128)(2,1)}, bf16[512,1536]{1,0:T(8,128)(2,1)}, u32[]{:S(2)}, u32[]{:S(2)}) collective-permute-start(bf16[512,1536]{1,0:T(8,128)(2,1)} %get-tuple-element.331), channel_id=1, source_target_pairs={{0,2},{2,0},{1,3},{3,1},{4,6},{6,4},{5,7},{7,5},{8,10},{10,8},{9,1... | collective-permute-start | bytes 4718600 | tf_op jit(solution)/shard_map/ppermute | solution.py:82
  449.8 40.2 %collective-permute-start.60 = (bf16[2,192,1152]{2,1,0:T(8,128)(2,1)}, bf16[2,192,1152]{2,1,0:T(8,128)(2,1)S(1)}, u32[]{:S(2)}, u32[]{:S(2)}) collective-permute-start(bf16[2,192,1152]{2,1,0:T(8,128)(2,1)} %fusion.17), channel_id=1, source_target_pairs={{0,16},{16,0},{1,17},{17,1},{2,18},{18,2},{3,19},{19,3},{4,20},{20... | collective-permute-start | bytes 2654216 | tf_op jit(solution)/shard_map/ppermute | solution.py:108
  457.4 37.8 %collective-permute-start.67 = (bf16[2,192,1024]{2,1,0:T(8,128)(2,1)}, bf16[2,192,1024]{2,1,0:T(8,128)(2,1)S(1)}, u32[]{:S(2)}, u32[]{:S(2)}) collective-permute-start(bf16[2,192,1024]{2,1,0:T(8,128)(2,1)} %get-tuple-element.367), channel_id=1, source_target_pairs={{0,8},{8,0},{1,9},{9,1},{2,10},{10,2},{3,11},{11,3},{4,12},{12,4},... | collective-permute-start | bytes 2359304 | tf_op jit(solution)/shard_map/ppermute | solution.py:82
  500.1 38.5 %collective-permute-start.66 = (bf16[512,1536]{1,0:T(8,128)(2,1)}, bf16[512,1536]{1,0:T(8,128)(2,1)}, u32[]{:S(2)}, u32[]{:S(2)}) collective-permute-start(bf16[512,1536]{1,0:T(8,128)(2,1)} %add_convert_fusion), channel_id=1, source_target_pairs={{0,1},{1,0},{2,3},{3,2},{4,5},{5,4},{6,7},{7,6},{8,9},{9,8},{10,11... | collective-permute-start | bytes 4718600 | tf_op jit(solution)/shard_map/ppermute | solution.py:82
  501.8 33.6 %collective-permute-start.69 = (bf16[2,192,1024]{2,1,0:T(8,128)(2,1)}, bf16[2,192,1024]{2,1,0:T(8,128)(2,1)}, u32[]{:S(2)}, u32[]{:S(2)}) collective-permute-start(bf16[2,192,1024]{2,1,0:T(8,128)(2,1)} %get-tuple-element.371), channel_id=1, source_target_pairs={{0,8},{8,0},{1,9},{9,1},{2,10},{10,2},{3,11},{11,3},{4,12},{12,4},... | collective-permute-start | bytes 2359304 | tf_op jit(solution)/shard_map/ppermute | solution.py:82
  501.8 42.9 %collective-permute-start.76 = (bf16[2,192,1152]{2,1,0:T(8,128)(2,1)}, bf16[2,192,1152]{2,1,0:T(8,128)(2,1)}, u32[]{:S(2)}, u32[]{:S(2)}) collective-permute-start(bf16[2,192,1152]{2,1,0:T(8,128)(2,1)} %fusion.18), channel_id=1, source_target_pairs={{0,16},{16,0},{1,17},{17,1},{2,18},{18,2},{3,19},{19,3},{4,20},{20... | collective-permute-start | bytes 2654216 | tf_op jit(solution)/shard_map/ppermute | solution.py:108
  515.6 61.7 %collective-permute-start.72 = (bf16[192,1152]{1,0:T(8,128)(2,1)}, bf16[192,1152]{1,0:T(8,128)(2,1)}, u32[]{:S(2)}, u32[]{:S(2)}) collective-permute-start(bf16[192,1152]{1,0:T(8,128)(2,1)} %get-tuple-element.437), channel_id=1, source_target_pairs={{0,8},{8,0},{1,9},{9,1},{2,10},{10,2},{3,11},{11,3},{4,12},{12,4},... | collective-permute-start | bytes 1327112 | tf_op jit(solution)/shard_map/ppermute | solution.py:82
  518.3 53.0 %collective-permute-start.73 = (bf16[192,1152]{1,0:T(8,128)(2,1)}, bf16[192,1152]{1,0:T(8,128)(2,1)}, u32[]{:S(2)}, u32[]{:S(2)}) collective-permute-start(bf16[192,1152]{1,0:T(8,128)(2,1)} %get-tuple-element.439), channel_id=1, source_target_pairs={{0,8},{8,0},{1,9},{9,1},{2,10},{10,2},{3,11},{11,3},{4,12},{12,4},... | collective-permute-start | bytes 1327112 | tf_op jit(solution)/shard_map/ppermute | solution.py:82
  544.6 38.2 %collective-permute-start.71 = (bf16[256,1536]{1,0:T(8,128)(2,1)}, bf16[256,1536]{1,0:T(8,128)(2,1)}, u32[]{:S(2)}, u32[]{:S(2)}) collective-permute-start(bf16[256,1536]{1,0:T(8,128)(2,1)} %slice.323), channel_id=1, source_target_pairs={{0,8},{8,0},{1,9},{9,1},{2,10},{10,2},{3,11},{11,3},{4,12},{12,4},... | collective-permute-start | bytes 2359304 | tf_op jit(solution)/shard_map/ppermute | solution.py:82
  (146 other events, 1677.2 us)
Sparse Core Ops, SparseCore 0:
  65.3 67.9 all-gather.7
  149.1 48.6 all-gather.9
  379.7 47.2 all-gather.5

commit v6 on v5

--- a/solution.py
+++ b/solution.py
@@ -1041,9 +1041,8 @@
     dn1 = FourSum(*parts[:6])
     att = ChipSum(*parts[6:])
     dn1.second(order)
+    g_sum.arrived(order)
     norm_one_in, gain_one_grad = norm_backward(rows_in, scale_one, gain_one, dn1.total(order))
-    g_sum.arrived(order)
-    branch.along_x(order)
     u_sum.across(order, False)
     att.far_yy(order)
     bias_grad = order.after(bias_grad)[0]
@@ -1052,6 +1051,7 @@
     )
     bias_slots = lax.dynamic_update_slice_in_dim(bias_slots, bias_grad[Q_COLS:], kv_at, 0)
     att.far_hi(order)
+    branch.along_x(order)
     d_low, d_way = summed_up(d_sum)
     g_low, g_way = summed_up(g_sum)
     att.near_yy(order)

time: 643 us -> 636 us (0.989)
    unnamed x166 -> x190, local copies, waits for them, and re-layouts: 17.6 us -> 19.7 us
  transfers between devices with their start and end apart: 90 -> 90, of which waited for: 36 -> 31; matrix products, arithmetic and copies ran while one was open for 20% -> 20% of each run, Pallas kernels for 21% -> 21%
where the time goes in v6:
time: 636 us; the launch traced here: 631 us
  waiting for transfers between devices  225 us (35%)
  Pallas kernels  173 us (27%)
  other arithmetic  92.4 us (15%)
  starting transfers between devices  60.9 us (10%)
  local copies, waits for them, and re-layouts  58.1 us (9%)
  between operations  21 us (3%)
    ppermute x81, waiting for transfers between devices, swap(): return lax.ppermute(value, axis, [(0, 1), (1, 0)])  145 us
    ppermute x81, starting transfers between devices, swap(): return lax.ppermute(value, axis, [(0, 1), (1, 0)])  54.1 us
    ppermute x5, waiting for transfers between devices, turn(): lax.ppermute(value, axis, [(i, (i + steps) % count) for i in range(count)])  44.6 us
    pallas_call x3, Pallas kernels, weight_grad(): pl.pallas_call(functools.partial(weight_grad_kernel, rows), grid_spec=plt...  42.3 us
    pallas_call x1, Pallas kernels, feed_forward(): pl.pallas_call(functools.partial(feed_forward_kernel, count, rows), grid_...  39.8 us
    pallas_call x1, Pallas kernels, attention_back(): pl.pallas_call(functools.partial(attention_back_kernel, len(da), len(n1),...  26.9 us
    pallas_call x1, Pallas kernels, attention(): pl.pallas_call(functools.partial(attention_kernel, len(n1), parts, rows),...  23.3 us
    all_gather x1, waiting for transfers between devices, body(): ff_lo_hi_gu = lax.all_gather(ff_lo[:2], 'hi')  23.2 us
  transfers between devices with their start and end apart: 90, of which 31 were waited for; matrix products, arithmetic and copies ran while one was open for 20% of the time, Pallas kernels for 21%

profile of v6, /device:TPU:0, one launch (start us, length us, event | category | flops | bytes accessed | tf_op | source)
XLA Modules:
  0.0 630.5 jit_solution(6988699647385556137)
XLA Ops:
  27.6 12.7 %collective-permute-done.4.refs_11_ = bf16[192,1024]{1,0:T(8,128)(2,1)} collective-permute-done((bf16[192,1024]{1,0:T(8,128)(2,1)S(1)}, bf16[192,1024]{1,0:T(8,128)(2,1)}, u32[]{:S(2)}, u32[]{:S(2)}) %collective-permute-start.4) | collective-permute-done | bytes 393248 | tf_op jit(solution)/shard_map/ppermute | solution.py:82
  44.9 9.9 %collective-permute-done.10.refs_15_ = bf16[192,1024]{1,0:T(8,128)(2,1)S(1)} collective-permute-done((bf16[192,1024]{1,0:T(8,128)(2,1)}, bf16[192,1024]{1,0:T(8,128)(2,1)S(1)}, u32[]{:S(2)}, u32[]{:S(2)}) %collective-permute-start.10) | collective-permute-done | bytes 393248 | tf_op jit(solution)/shard_map/ppermute | solution.py:82
  67.7 8.4 %collective-permute-done.12.refs_17_ = bf16[192,1024]{1,0:T(8,128)(2,1)} collective-permute-done((bf16[192,1024]{1,0:T(8,128)(2,1)}, bf16[192,1024]{1,0:T(8,128)(2,1)}, u32[]{:S(2)}, u32[]{:S(2)}) %collective-permute-start.12) | collective-permute-done | bytes 393248 | tf_op jit(solution)/shard_map/ppermute | solution.py:82
  78.5 23.3 %attention.1 = (bf16[1024,640]{1,0:T(8,128)(2,1)}, bf16[1024,384]{1,0:T(8,128)(2,1)}, f32[8,1024]{1,0:T(8,128)}, bf16[256,1536]{1,0:T(8,128)(2,1)}, bf16[128,153...) custom-call(s32[8]{0:T(128)} %stack.100.chips_ref, ...), custom_call_target="tpu_custom_call" | custom-call | flops 1179648 | bytes 4096 | tf_op jit(solution)/shard_map/attention/pallas_call | solution.py:308
  102.4 16.3 %collective-permute-done.17.refs_7_.refs_15_ = bf16[3,192,1152]{2,1,0:T(8,128)(2,1)} collective-permute-done((bf16[3,192,1152]{2,1,0:T(8,128)(2,1)}, bf16[3,192,1152]{2,1,0:T(8,128)(2,1)}, u32[]{:S(2)}, u32[]{:S(2)}) %collective-permute-start.17) | collective-permute-done | bytes 1327136 | tf_op jit(solution)/shard_map/ppermute | solution.py:82
  123.7 9.6 %all-gather.8.cloned.1.call-done = bf16[6,192,1152]{2,1,0:T(8,128)(2,1)} async-done(((bf16[3,192,1152]{2,1,0:T(8,128)(2,1)}), bf16[6,192,1152]{2,1,0:T(8,128)(2,1)}) %all-gather.8.cloned.1.call-update) | async-done | bytes 2654224 | tf_op jit(solution)/shard_map/all_gather | solution.py:887
  174.7 23.2 %all-gather.10.cloned.1.call-done = bf16[4,192,1152]{2,1,0:T(8,128)(2,1)} async-done(((bf16[2,192,1152]{2,1,0:T(8,128)(2,1)}), bf16[4,192,1152]{2,1,0:T(8,128)(2,1)}) %all-gather.10.cloned.1.call-update) | async-done | bytes 1769488 | tf_op jit(solution)/shard_map/all_gather | solution.py:918
  213.7 10.5 %collective-permute-done.32.refs_13_ = bf16[2,192,1152]{2,1,0:T(8,128)(2,1)} collective-permute-done((bf16[2,192,1152]{2,1,0:T(8,128)(2,1)}, bf16[2,192,1152]{2,1,0:T(8,128)(2,1)}, u32[]{:S(2)}, u32[]{:S(2)}) %collective-permute-start.32) | collective-permute-done | bytes 884768 | tf_op jit(solution)/shard_map/ppermute | solution.py:82
  224.2 21.8 %gate_up.1 = (bf16[2048,2304]{1,0:T(8,128)(2,1)}, bf16[1536,2048]{1,0:T(8,128)(2,1)}) custom-call(s32[8]{0:T(128)} %stack.104.chips_ref, bf16[256,1536]{1,0:T(8,128)(2,1)} %multiply_convert_fusion.refs_0_, bf16[512,1536]{1,0:T(8,128)(2,1)} %constant_dynamic-update-slice_fusion.refs_1_, bf16[256,1536]{1,0:T(8,128)(2,1)} %constant_dynamic-update-slice_fusion.4.refs_2_, ...), custom_call_target="tpu_custom_call" | custom-call | flops 3538944 | bytes 7680 | tf_op jit(solution)/shard_map/gate_up/pallas_call | solution.py:482
  252.0 5.8 collective-permute-done.34
  260.9 10.8 %collective-permute-done.40.refs_21_ = bf16[192,1152]{1,0:T(8,128)(2,1)S(1)} collective-permute-done((bf16[192,1152]{1,0:T(8,128)(2,1)}, bf16[192,1152]{1,0:T(8,128)(2,1)S(1)}, u32[]{:S(2)}, u32[]{:S(2)}) %collective-permute-start.40) | collective-permute-done | bytes 442400 | tf_op jit(solution)/shard_map/ppermute | solution.py:82
  272.5 39.8 %feed_forward.1 = (bf16[256,1536]{1,0:T(8,128)(2,1)}, bf16[256,1536]{1,0:T(8,128)(2,1)}, bf16[256,1536]{1,0:T(8,128)(2,1)}, bf16[256,1536]{1,0:T(8,128)(2,1)}, b...) custom-call(s32[8]{0:T(128)} %stack.104.chips_ref, ...), custom_call_target="tpu_custom_call" | custom-call | flops 5308416 | bytes 12800 | tf_op jit(solution)/shard_map/feed_forward/pallas_call | solution.py:572
  314.0 14.1 %weight_grad.3 = (bf16[2,2,192,1152]{3,2,1,0:T(8,128)(2,1)}, bf16[2,2,192,1152]{3,2,1,0:T(8,128)(2,1)}) custom-call(s32[3]{0:T(128)} %pad_add_fusion.1.place_ref, bf16[1536,2048]{1,0:T(8,128)(2,1)} %get-tuple-element.303.left_ref, bf16[2048,1152]{1,0:T(8,128)(2,1)} %get-tuple-element.327.right_ref.left_ref), custom_call_target="tpu_custom_call" | custom-call | flops 1769472 | bytes 4096 | tf_op jit(solution)/shard_map/weight_grad/pallas_call | solution.py:625
  339.1 14.1 %weight_grad.4 = (bf16[2,2,192,1152]{3,2,1,0:T(8,128)(2,1)}, bf16[2,2,192,1152]{3,2,1,0:T(8,128)(2,1)}) custom-call(s32[3]{0:T(128)} %pad_add_fusion.1.place_ref, bf16[1536,2048]{1,0:T(8,128)(2,1)} %get-tuple-element.321.left_ref, bf16[2048,1152]{1,0:T(8,128)(2,1)} %get-tuple-element.314.right_ref), custom_call_target="tpu_custom_call" | custom-call | flops 1769472 | bytes 4096 | tf_op jit(solution)/shard_map/weight_grad/pallas_call | solution.py:625
  360.0 14.1 %weight_grad.5 = (bf16[2,2,192,1152]{3,2,1,0:T(8,128)(2,1)}, bf16[2,2,192,1152]{3,2,1,0:T(8,128)(2,1)}) custom-call(s32[3]{0:T(128)} %pad_add_fusion.1.place_ref, bf16[1536,2048]{1,0:T(8,128)(2,1)} %get-tuple-element.321.left_ref, bf16[2048,1152]{1,0:T(8,128)(2,1)} %get-tuple-element.322.right_ref), custom_call_target="tpu_custom_call" | custom-call | flops 1769472 | bytes 4096 | tf_op jit(solution)/shard_map/weight_grad/pallas_call | solution.py:625
  386.6 15.3 %down.1 = (bf16[512,1536]{1,0:T(8,128)(2,1)}, bf16[512,1536]{1,0:T(8,128)(2,1)}, bf16[512,1536]{1,0:T(8,128)(2,1)}, bf16[512,1536]{1,0:T(8,128)(2,1)}) custom-call(bf16[2048,1152]{1,0:T(8,128)(2,1)} %get-tuple-element.327.right_ref.left_ref, bf16[1536,1152]{1,0:T(8,128)(2,1)} %get-tuple-element.328.right_ref), custom_call_target="tpu_custom_call" | custom-call | flops 1769472 | bytes 3584 | tf_op jit(solution)/shard_map/down/pallas_call | solution.py:662
  407.3 26.9 %attention_back.1 = (bf16[1024,640]{1,0:T(8,128)(2,1)}, f32[1,640]{1,0:T(1,128)}, bf16[256,1536]{1,0:T(8,128)(2,1)}, bf16[128,1536]{1,0:T(8,128)(2,1)}, bf16[128...) custom-call(s32[8]{0:T(128)} %stack.113.chips_ref, ...), custom_call_target="tpu_custom_call" | custom-call | flops 2555904 | bytes 6144 | tf_op jit(solution)/shard_map/attention_back/pallas_call | solution.py:400
  443.1 36.0 %collective-permute-done.67 = bf16[2,192,1152]{2,1,0:T(8,128)(2,1)} collective-permute-done((bf16[2,192,1152]{2,1,0:T(8,128)(2,1)}, bf16[2,192,1152]{2,1,0:T(8,128)(2,1)}, u32[]{:S(2)}, u32[]{:S(2)}) %collective-permute-start.67) | collective-permute-done | bytes 884768 | tf_op jit(solution)/shard_map/ppermute | solution.py:108
  482.7 8.0 %collective-permute-done.65 = bf16[128,1536]{1,0:T(8,128)(2,1)S(1)} collective-permute-done((bf16[128,1536]{1,0:T(8,128)(2,1)S(1)}, bf16[128,1536]{1,0:T(8,128)(2,1)S(1)}, u32[]{:S(2)}, u32[]{:S(2)}) %collective-permute-start.65) | collective-permute-done | bytes 393248 | tf_op jit(solution)/shard_map/ppermute | solution.py:82
  520.0 8.8 %collective-permute-done.70 = bf16[2,192,1024]{2,1,0:T(8,128)(2,1)} collective-permute-done((bf16[2,192,1024]{2,1,0:T(8,128)(2,1)}, bf16[2,192,1024]{2,1,0:T(8,128)(2,1)}, u32[]{:S(2)}, u32[]{:S(2)}) %collective-permute-start.70) | collective-permute-done | bytes 786464 | tf_op jit(solution)/shard_map/ppermute | solution.py:82
  530.3 14.6 %collective-permute-done.69 = bf16[512,1536]{1,0:T(8,128)(2,1)} collective-permute-done((bf16[512,1536]{1,0:T(8,128)(2,1)}, bf16[512,1536]{1,0:T(8,128)(2,1)}, u32[]{:S(2)}, u32[]{:S(2)}) %collective-permute-start.69) | collective-permute-done | bytes 1572896 | tf_op jit(solution)/shard_map/ppermute | solution.py:82
  550.1 8.6 %collective-permute-done.75 = bf16[192,1024]{1,0:T(8,128)(2,1)S(1)} collective-permute-done((bf16[192,1024]{1,0:T(8,128)(2,1)S(1)}, bf16[192,1024]{1,0:T(8,128)(2,1)S(1)}, u32[]{:S(2)}, u32[]{:S(2)}) %collective-permute-start.75) | collective-permute-done | bytes 393248 | tf_op jit(solution)/shard_map/ppermute | solution.py:108
  585.7 6.4 %collective-permute-done.82 = f32[5248]{0:T(1024)S(1)} collective-permute-done((f32[5248]{0:T(1024)S(1)}, f32[5248]{0:T(1024)S(1)}, u32[]{:S(2)}, u32[]{:S(2)}) %collective-permute-start.82) | collective-permute-done | bytes 21024 | tf_op jit(solution)/shard_map/ppermute | solution.py:82
  607.9 5.8 divide_subtract_fusion.1
  (477 shorter events, 244.8 us)
Async XLA Ops:
  7.2 126.1 %all-gather.8.cloned.1.call-start = ((), (), s32[]{:S(2)}) async-start(), calls=%async_computation.1 | async-start | bytes 3981312 | tf_op jit(solution)/shard_map/all_gather | solution.py:887
  65.2 132.6 %all-gather.10.cloned.1.call-start = ((), (), s32[]{:S(2)}) async-start(), calls=%async_computation.2 | async-start | bytes 2654208 | tf_op jit(solution)/shard_map/all_gather | solution.py:918
  65.5 53.3 %collective-permute-start.17 = (bf16[3,192,1152]{2,1,0:T(8,128)(2,1)}, bf16[3,192,1152]{2,1,0:T(8,128)(2,1)}, u32[]{:S(2)}, u32[]{:S(2)}) collective-permute-start(bf16[3,192,1152]{2,1,0:T(8,128)(2,1)} %get-tuple-element.242), channel_id=1, source_target_pairs={{0,8},{8,0},{1,9},{9,1},{2,10},{10,2},{3,11},{11,3},{4,12},{12,4},... | collective-permute-start | bytes 3981320 | tf_op jit(solution)/shard_map/ppermute | solution.py:82
  76.1 42.6 %collective-permute-start.16 = (bf16[3,192,1152]{2,1,0:T(8,128)(2,1)S(1)}, bf16[3,192,1152]{2,1,0:T(8,128)(2,1)S(1)}, u32[]{:S(2)}, u32[]{:S(2)}) collective-permute-start(bf16[3,192,1152]{2,1,0:T(8,128)(2,1)S(1)} %copy-done), channel_id=1, source_target_pairs={{0,4},{4,0},{1,5},{5,1},{2,6},{6,2},{3,7},{7,3},{8,12},{12,8},{9,1... | collective-permute-start | bytes 3981320 | tf_op jit(solution)/shard_map/ppermute | solution.py:82
  102.3 32.4 %collective-permute-start.13 = (bf16[256,1536]{1,0:T(8,128)(2,1)}, bf16[256,1536]{1,0:T(8,128)(2,1)}, u32[]{:S(2)}, u32[]{:S(2)}) collective-permute-start(bf16[256,1536]{1,0:T(8,128)(2,1)} %get-tuple-element.237), channel_id=1, source_target_pairs={{0,2},{2,0},{1,3},{3,1},{4,6},{6,4},{5,7},{7,5},{8,10},{10,8},{9,1... | collective-permute-start | bytes 2359304 | tf_op jit(solution)/shard_map/ppermute | solution.py:82
  149.0 288.2 %all-gather.6.cloned.1.call-start = ((), (), s32[]{:S(2)}) async-start(), calls=%async_computation | async-start | bytes 2654208 | tf_op jit(solution)/shard_map/all_gather | solution.py:767
  171.7 30.8 %collective-permute-start.28 = (bf16[512,1536]{1,0:T(8,128)(2,1)}, bf16[512,1536]{1,0:T(8,128)(2,1)}, u32[]{:S(2)}, u32[]{:S(2)}) collective-permute-start(bf16[512,1536]{1,0:T(8,128)(2,1)} %constant_dynamic-update-slice_fusion.refs_1_), channel_id=1, source_target_pairs={{0,2},{2,0},{1,3},{3,1},{4,6},{6,4},{5,7},{7,5},{8,10},{10,8},{9,1... | collective-permute-start | bytes 4718600 | tf_op jit(solution)/shard_map/ppermute | solution.py:82
  171.7 40.1 %collective-permute-start.31 = (bf16[3,192,1152]{2,1,0:T(8,128)(2,1)S(1)}, bf16[3,192,1152]{2,1,0:T(8,128)(2,1)}, u32[]{:S(2)}, u32[]{:S(2)}) collective-permute-start(bf16[3,192,1152]{2,1,0:T(8,128)(2,1)S(1)} %dynamic-slice_bitcast_fusion.refs_10_.refs_18_), channel_id=1, source_target_pairs={{0,4},{4,0},{1,5},{5,1},{2,6},{6,2},{3,7},{7,3},{8,12},{12,8},{9,1... | collective-permute-start | bytes 3981320 | tf_op jit(solution)/shard_map/ppermute | solution.py:82
  205.4 40.7 %collective-permute-start.33 = (bf16[256,1536]{1,0:T(8,128)(2,1)}, bf16[256,1536]{1,0:T(8,128)(2,1)}, u32[]{:S(2)}, u32[]{:S(2)}) collective-permute-start(bf16[256,1536]{1,0:T(8,128)(2,1)} %refs_0_), channel_id=1, source_target_pairs={{0,8},{8,0},{1,9},{9,1},{2,10},{10,2},{3,11},{11,3},{4,12},{12,4},... | collective-permute-start | bytes 2359304 | tf_op jit(solution)/shard_map/ppermute | solution.py:82
  207.7 43.2 %collective-permute-start.36 = (bf16[128,1536]{1,0:T(8,128)(2,1)}, bf16[128,1536]{1,0:T(8,128)(2,1)}, u32[]{:S(2)}, u32[]{:S(2)}) collective-permute-start(bf16[128,1536]{1,0:T(8,128)(2,1)} %slice.191), channel_id=1, source_target_pairs={{0,8},{8,0},{1,9},{9,1},{2,10},{10,2},{3,11},{11,3},{4,12},{12,4},... | collective-permute-start | bytes 1179656 | tf_op jit(solution)/shard_map/ppermute | solution.py:82
  211.8 39.1 %collective-permute-start.35 = (bf16[256,1536]{1,0:T(8,128)(2,1)}, bf16[256,1536]{1,0:T(8,128)(2,1)S(1)}, u32[]{:S(2)}, u32[]{:S(2)}) collective-permute-start(bf16[256,1536]{1,0:T(8,128)(2,1)} %refs_0_), channel_id=1, source_target_pairs={{0,2},{2,0},{1,3},{3,1},{4,6},{6,4},{5,7},{7,5},{8,10},{10,8},{9,1... | collective-permute-start | bytes 2359304 | tf_op jit(solution)/shard_map/ppermute | solution.py:82
  213.7 37.3 %collective-permute-start.37 = (bf16[192,1152]{1,0:T(8,128)(2,1)}, bf16[192,1152]{1,0:T(8,128)(2,1)}, u32[]{:S(2)}, u32[]{:S(2)}) collective-permute-start(bf16[192,1152]{1,0:T(8,128)(2,1)} %slice_bitcast_fusion.7), channel_id=1, source_target_pairs={{0,16},{16,0},{1,17},{17,1},{2,18},{18,2},{3,19},{19,3},{4,20},{20... | collective-permute-start | bytes 1327112 | tf_op jit(solution)/shard_map/ppermute | solution.py:108
  328.1 46.0 %collective-permute-start.51 = (bf16[2,2,192,1152]{3,2,1,0:T(8,128)(2,1)}, bf16[2,2,192,1152]{3,2,1,0:T(8,128)(2,1)}, u32[]{:S(2)}, u32[]{:S(2)}) collective-permute-start(bf16[2,2,192,1152]{3,2,1,0:T(8,128)(2,1)} %get-tuple-element.319), channel_id=1, source_target_pairs={{0,4},{4,0},{1,5},{5,1},{2,6},{6,2},{3,7},{7,3},{8,12},{12,8},{9,1... | collective-permute-start | bytes 5308424 | tf_op jit(solution)/shard_map/ppermute | solution.py:82
  353.3 54.0 %collective-permute-start.59 = (bf16[2,2,192,1152]{3,2,1,0:T(8,128)(2,1)}, bf16[2,2,192,1152]{3,2,1,0:T(8,128)(2,1)}, u32[]{:S(2)}, u32[]{:S(2)}) collective-permute-start(bf16[2,2,192,1152]{3,2,1,0:T(8,128)(2,1)} %get-tuple-element.337), channel_id=1, source_target_pairs={{0,4},{4,0},{1,5},{5,1},{2,6},{6,2},{3,7},{7,3},{8,12},{12,8},{9,1... | collective-permute-start | bytes 5308424 | tf_op jit(solution)/shard_map/ppermute | solution.py:82
  403.3 87.3 %collective-permute-start.61 = (bf16[2,2,192,1152]{3,2,1,0:T(8,128)(2,1)}, bf16[2,2,192,1152]{3,2,1,0:T(8,128)(2,1)}, u32[]{:S(2)}, u32[]{:S(2)}) collective-permute-start(bf16[2,2,192,1152]{3,2,1,0:T(8,128)(2,1)} %get-tuple-element.350), channel_id=1, source_target_pairs={{0,4},{4,0},{1,5},{5,1},{2,6},{6,2},{3,7},{7,3},{8,12},{12,8},{9,1... | collective-permute-start | bytes 5308424 | tf_op jit(solution)/shard_map/ppermute | solution.py:82
  437.2 41.9 %collective-permute-start.67 = (bf16[2,192,1152]{2,1,0:T(8,128)(2,1)}, bf16[2,192,1152]{2,1,0:T(8,128)(2,1)}, u32[]{:S(2)}, u32[]{:S(2)}) collective-permute-start(bf16[2,192,1152]{2,1,0:T(8,128)(2,1)} %fusion.17), channel_id=1, source_target_pairs={{0,16},{16,0},{1,17},{17,1},{2,18},{18,2},{3,19},{19,3},{4,20},{20... | collective-permute-start | bytes 2654216 | tf_op jit(solution)/shard_map/ppermute | solution.py:108
  437.2 53.5 %collective-permute-start.60 = (bf16[2,192,1024]{2,1,0:T(8,128)(2,1)}, bf16[2,192,1024]{2,1,0:T(8,128)(2,1)S(1)}, u32[]{:S(2)}, u32[]{:S(2)}) collective-permute-start(bf16[2,192,1024]{2,1,0:T(8,128)(2,1)} %get-tuple-element.349), channel_id=1, source_target_pairs={{0,8},{8,0},{1,9},{9,1},{2,10},{10,2},{3,11},{11,3},{4,12},{12,4},... | collective-permute-start | bytes 2359304 | tf_op jit(solution)/shard_map/ppermute | solution.py:82
  439.9 39.3 %collective-permute-start.64 = (bf16[128,1536]{1,0:T(8,128)(2,1)S(1)}, bf16[128,1536]{1,0:T(8,128)(2,1)S(1)}, u32[]{:S(2)}, u32[]{:S(2)}) collective-permute-start(bf16[128,1536]{1,0:T(8,128)(2,1)S(1)} %add_convert_fusion.7), channel_id=1, source_target_pairs={{0,1},{1,0},{2,3},{3,2},{4,5},{5,4},{6,7},{7,6},{8,9},{9,8},{10,11... | collective-permute-start | bytes 1179656 | tf_op jit(solution)/shard_map/ppermute | solution.py:82
  443.1 63.1 %collective-permute-start.52 = (bf16[512,1536]{1,0:T(8,128)(2,1)}, bf16[512,1536]{1,0:T(8,128)(2,1)}, u32[]{:S(2)}, u32[]{:S(2)}) collective-permute-start(bf16[512,1536]{1,0:T(8,128)(2,1)} %get-tuple-element.330), channel_id=1, source_target_pairs={{0,2},{2,0},{1,3},{3,1},{4,6},{6,4},{5,7},{7,5},{8,10},{10,8},{9,1... | collective-permute-start | bytes 4718600 | tf_op jit(solution)/shard_map/ppermute | solution.py:82
  494.1 34.6 %collective-permute-start.70 = (bf16[2,192,1024]{2,1,0:T(8,128)(2,1)}, bf16[2,192,1024]{2,1,0:T(8,128)(2,1)}, u32[]{:S(2)}, u32[]{:S(2)}) collective-permute-start(bf16[2,192,1024]{2,1,0:T(8,128)(2,1)} %get-tuple-element.372), channel_id=1, source_target_pairs={{0,8},{8,0},{1,9},{9,1},{2,10},{10,2},{3,11},{11,3},{4,12},{12,4},... | collective-permute-start | bytes 2359304 | tf_op jit(solution)/shard_map/ppermute | solution.py:82
  496.4 52.7 %collective-permute-start.76 = (bf16[2,192,1152]{2,1,0:T(8,128)(2,1)}, bf16[2,192,1152]{2,1,0:T(8,128)(2,1)}, u32[]{:S(2)}, u32[]{:S(2)}) collective-permute-start(bf16[2,192,1152]{2,1,0:T(8,128)(2,1)} %fusion.18), channel_id=1, source_target_pairs={{0,16},{16,0},{1,17},{17,1},{2,18},{18,2},{3,19},{19,3},{4,20},{20... | collective-permute-start | bytes 2654216 | tf_op jit(solution)/shard_map/ppermute | solution.py:108
  509.3 35.6 %collective-permute-start.69 = (bf16[512,1536]{1,0:T(8,128)(2,1)}, bf16[512,1536]{1,0:T(8,128)(2,1)}, u32[]{:S(2)}, u32[]{:S(2)}) collective-permute-start(bf16[512,1536]{1,0:T(8,128)(2,1)} %add_convert_fusion), channel_id=1, source_target_pairs={{0,1},{1,0},{2,3},{3,2},{4,5},{5,4},{6,7},{7,6},{8,9},{9,8},{10,11... | collective-permute-start | bytes 4718600 | tf_op jit(solution)/shard_map/ppermute | solution.py:82
  515.7 54.0 %collective-permute-start.72 = (bf16[192,1152]{1,0:T(8,128)(2,1)}, bf16[192,1152]{1,0:T(8,128)(2,1)}, u32[]{:S(2)}, u32[]{:S(2)}) collective-permute-start(bf16[192,1152]{1,0:T(8,128)(2,1)} %get-tuple-element.437), channel_id=1, source_target_pairs={{0,8},{8,0},{1,9},{9,1},{2,10},{10,2},{3,11},{11,3},{4,12},{12,4},... | collective-permute-start | bytes 1327112 | tf_op jit(solution)/shard_map/ppermute | solution.py:82
  516.7 47.0 %collective-permute-start.73 = (bf16[192,1152]{1,0:T(8,128)(2,1)}, bf16[192,1152]{1,0:T(8,128)(2,1)}, u32[]{:S(2)}, u32[]{:S(2)}) collective-permute-start(bf16[192,1152]{1,0:T(8,128)(2,1)} %get-tuple-element.439), channel_id=1, source_target_pairs={{0,8},{8,0},{1,9},{9,1},{2,10},{10,2},{3,11},{11,3},{4,12},{12,4},... | collective-permute-start | bytes 1327112 | tf_op jit(solution)/shard_map/ppermute | solution.py:82
  (158 other events, 2358.9 us)
Sparse Core Ops, SparseCore 0:
  65.3 67.9 all-gather.7
  149.2 48.6 all-gather.9
  379.7 47.2 all-gather.5
